TPU v7x, 32 devices: a whole 2x2x4 slice. The times are simulated.
32 devices in a mesh: tensor: 2 (over x), dp: 16 (over z, y, core).
Axes of the slice: x: 2, y: 2, z: 4, core: 2. Of those that a mesh axis runs over, the one named last changes fastest.
Arguments:
- inputs: bfloat16 [4096, 8192], P('dp', 'tensor'), may hold values from -6 to 6
- frozen_value_weight: bfloat16 [8192, 1024], P(None, 'tensor'), may hold values from -0.0625 to 0.0625
- adapter_down_matrix: bfloat16 [16, 8192, 16], P('dp', 'tensor'), may hold values from -0.0625 to 0.0625
- adapter_up_matrix: bfloat16 [16, 16, 1024], P('dp', None, 'tensor'), may hold values from -1.5 to 1.5
- value_cotangent: bfloat16 [4096, 1024], P('dp', 'tensor'), may hold values from -6 to 6
- tenant_of_block: int32 [32], P('dp'), may hold values from 0 to 15
- quotas: int32 [16], replicated, may hold values from 128 to 1023
Outputs:
- adapted_values: bfloat16 [4096, 1024], P('dp', 'tensor')
- gradient_inputs: bfloat16 [4096, 8192], P('dp', 'tensor')
- down_grad: float32 [16, 8192, 16], P('dp', 'tensor')
- gradient_up_matrix: float32 [16, 16, 1024], P('dp', None, 'tensor')
All inputs are finite; a program needn't handle non-finite values.
Results may differ from a plain program's by a relative error of at most 0.015.
Values may be sent and summed in bfloat16 or wider, within the bound.
No kernel may reach another device: no remote copies, remote signals or barrier semaphores. Data moves between devices by JAX's collectives and lax.ppermute only.
A program may use at most 64 MiB of HBM per device.

v0:
```python
import jax
import jax.numpy as jnp
from jax import lax
from jax.sharding import PartitionSpec as P

ADAPTER_RANK = 16
BLOCK = 128


adapter_scale = 2.0


def on_device(
    inputs,
    frozen_value_weight,
    adapter_down_matrix,
    adapter_up_matrix,
    value_cotangent,
    tenant_of_block,
    quotas,
):
    token_rows, local_features = inputs.shape
    local_values = frozen_value_weight.shape[1]
    nblocks = tenant_of_block.shape[0]
    owned_adapters = adapter_down_matrix.shape[0]
    adapter_count = owned_adapters * lax.axis_size("dp")
    frozen_output = jnp.dot(
        lax.all_gather(inputs, "tensor", axis=1, tiled=True),
        frozen_value_weight,
        preferred_element_type=jnp.float32,
    )
    partial_value = lax.dot_general(
        value_cotangent,
        frozen_value_weight,
        (((1,), (1,)), ((), ())),
        preferred_element_type=jnp.float32,
    )
    summed_gradient = lax.psum_scatter(
        partial_value.astype(jnp.bfloat16), "tensor", scatter_dimension=1, tiled=True
    ).astype(jnp.float32)
    tenant_all = lax.all_gather(tenant_of_block, "dp", axis=0, tiled=True)
    down_all, up_all = (
        lax.all_gather(adapter_down_matrix, "dp", axis=0, tiled=True),
        lax.all_gather(adapter_up_matrix, "dp", axis=0, tiled=True),
    )
    down_blocks = down_all[tenant_of_block]
    up_blocks = up_all[tenant_of_block]
    input_blocks = inputs.reshape(nblocks, BLOCK, local_features)
    value_grad_blocks = value_cotangent.reshape(nblocks, BLOCK, local_values)
    low_part = jnp.einsum(
        "bnd,bdr->bnr", input_blocks, down_blocks, preferred_element_type=jnp.float32
    )
    gradient_portion = adapter_scale * jnp.einsum(
        "bnk,brk->bnr", value_grad_blocks, up_blocks, preferred_element_type=jnp.float32
    )
    low_sum, grad_sum = (
        lax.psum(low_part.astype(jnp.bfloat16), "tensor").astype(jnp.float32),
        lax.psum(gradient_portion.astype(jnp.bfloat16), "tensor").astype(jnp.float32),
    )
    reduced_features = low_sum.astype(jnp.bfloat16)
    gradient_lowrank = grad_sum.astype(jnp.bfloat16)
    raised_output = jnp.einsum(
        "bnr,brk->bnk", reduced_features, up_blocks, preferred_element_type=jnp.float32
    )
    adapted_values = (
        frozen_output + adapter_scale * raised_output.reshape(token_rows, local_values)
    ).astype(jnp.bfloat16)
    adapter_input = jnp.einsum(
        "bnr,bdr->bnd", gradient_lowrank, down_blocks, preferred_element_type=jnp.float32
    )
    gradient_inputs = (summed_gradient + adapter_input.reshape(token_rows, local_features)).astype(
        jnp.bfloat16
    )
    adapter_ids = jnp.arange(adapter_count, dtype=jnp.int32)
    counts = (
        jnp.sum((tenant_all[:, None] == adapter_ids[None, :]).astype(jnp.float32), axis=0) * BLOCK
    )
    scale = quotas.astype(jnp.float32) / jnp.maximum(counts, 1.0)
    local_hot = (tenant_of_block[:, None] == adapter_ids[None, :]).astype(jnp.float32)
    block_weight = jnp.dot(local_hot, scale, precision=lax.Precision.HIGHEST)
    grad_a = (
        jnp.einsum(
            "bnd,bnr->bdr", input_blocks, gradient_lowrank, preferred_element_type=jnp.float32
        )
        * block_weight[:, None, None]
    )
    up_gradient_local = (
        adapter_scale
        * jnp.einsum(
            "bnr,bnk->brk", reduced_features, value_grad_blocks, preferred_element_type=jnp.float32
        )
        * block_weight[:, None, None]
    )
    dense_a = jnp.einsum("ba,bdr->adr", local_hot, grad_a, precision=lax.Precision.HIGHEST)
    dense_b = jnp.einsum(
        "mw,mqf->wqf", local_hot, up_gradient_local, precision=lax.Precision.HIGHEST
    )
    recv_a, recv_b = (
        lax.all_to_all(
            dense_a.astype(jnp.bfloat16), "dp", split_axis=0, concat_axis=0, tiled=True
        ).astype(dense_a.dtype),
        lax.all_to_all(
            dense_b.astype(jnp.bfloat16), "dp", split_axis=0, concat_axis=0, tiled=True
        ).astype(dense_b.dtype),
    )
    sources = lax.axis_size("dp")
    down_grad = jnp.sum(
        recv_a.reshape(sources, owned_adapters, local_features, ADAPTER_RANK), axis=0
    )
    gradient_up_matrix = jnp.sum(
        recv_b.reshape(sources, owned_adapters, ADAPTER_RANK, local_values), axis=0
    )
    return (adapted_values, gradient_inputs, down_grad, gradient_up_matrix)


def solution(mesh):
    placed = (
        P("dp", "tensor"),
        P(None, "tensor"),
        P("dp", "tensor", None),
        P("dp", None, "tensor"),
        P("dp", "tensor"),
        P("dp"),
        P(),
    )
    return jax.shard_map(
        on_device,
        mesh=mesh,
        in_specs=placed,
        out_specs=(
            P("dp", "tensor"),
            P("dp", "tensor"),
            P("dp", "tensor", None),
            P("dp", None, "tensor"),
        ),
        check_vma=False,
    )
```

profile of v0, /device:TPU:0, one launch (start us, length us, event | category | flops | bytes accessed | tf_op | source)
XLA Modules:
  0.0 179.6 jit_solution(13898288771830569278)
XLA Ops:
  7.2 0.0 copy-start
  7.2 0.0 all-gather.5.cloned.1.call-start
  7.2 0.7 all-gather.5.cloned.1.call-update
  7.9 0.0 all-gather.3.cloned.1.call-start
  8.0 0.7 all-gather.3.cloned.1.call-update
  8.7 0.0 reduce-scatter.2.cloned.1.call-start
  8.7 0.0 copy-done
  8.7 7.7 %convolution_convert_fusion = bf16[256,8192]{1,0:T(8,128)(2,1)} fusion(bf16[256,512]{1,0:T(8,128)(2,1)S(1)} %copy-done, bf16[8192,512]{1,0:T(8,128)(2,1)} %param.8), kind=kOutput, calls=%fused_computation.2 | convolution fusion | flops 2149580800 | bytes 12845056 | tf_op jit(solution)/shard_map/dot_general | solution.py:32
  16.4 0.0 copy-start.3
  16.5 0.0 copy-start.2
  16.5 0.0 copy-start.5
  16.5 0.0 copy-start.1
  16.5 0.0 reduce-scatter.2.cloned.1.call-update
  16.5 0.6 copy-done.3
  17.1 0.1 copy-done.2
  17.2 24.1 %all_gather.14 = bf16[16,16,512]{2,1,0:T(8,128)(2,1)S(1)} all-gather(bf16[1,16,512]{2,1,0:T(8,128)(2,1)S(1)} %copy-done.2), channel_id=1, replica_groups=mesh['tensor'=2,'dp'=16] {'dp'}, dimensions={0}, use_global_device_ids=true | all-gather | bytes 278528 | tf_op jit(solution)/shard_map/all_gather | solution.py:44
  41.3 0.5 gather_fusion.1
  41.8 0.0 copy-done.5
  41.9 0.6 dynamic-slice
  43.1 0.2 dynamic-update-slice
  43.3 7.0 %all-reduce = s32[32]{0:T(128)S(1)} all-reduce(s32[32]{0:T(128)S(1)} %dynamic-update-slice), channel_id=1, replica_groups=mesh['tensor'=2,'dp'=16] {'dp'}, use_global_device_ids=true, to_apply=%add | all-reduce | flops 32 | bytes 256
  50.4 0.1 convert_reduce_fusion.2
  50.5 0.0 copy-done.4
  50.5 0.2 broadcast_multiply_fusion
  50.7 0.2 fusion.4
  50.9 3.6 %all-gather.5.cloned.1.call-done = bf16[16,4096,16]{1,2,0:T(8,128)(2,1)} async-done(((bf16[1,4096,16]{1,2,0:T(8,128)(2,1)}), bf16[16,4096,16]{1,2,0:T(8,128)(2,1)}) %all-gather.5.cloned.1.call-update) | async-done | bytes 2097168 | tf_op jit(solution)/shard_map/all_gather | solution.py:43
  54.5 2.2 %gather_fusion = bf16[2,4096,16]{1,2,0:T(8,128)(2,1)S(1)} fusion(bf16[16,4096,16]{1,2,0:T(8,128)(2,1)} %all-gather.5.cloned.1.call-done, s32[1024]{0:T(1024)S(1)} %pad_clamp_fusion), kind=kCustom, calls=%fused_computation | custom fusion | bytes 524296 | tf_op jit(solution)/shard_map/gather | solution.py:46
  56.7 0.0 copy-done.1
  56.7 0.6 fusion.5
  57.3 8.1 %all-reduce.1 = (bf16[2,128,16]{1,2,0:T(8,128)(2,1)S(1)}, bf16[2,128,16]{1,2,0:T(8,128)(2,1)S(1)}) all-reduce(bf16[2,128,16]{1,2,0:T(8,128)(2,1)S(1)} %fusion.5, bf16[2,128,16]{1,2,0:T(8,128)(2,1)S(1)} %fusion.4), channel_id=1, replica_groups=mesh['tensor'=2,'dp'=16] {'tensor'}, use_global_device_ids=true, to_apply=%region_0.0 | all-reduce | flops 8192 | bytes 32768 | tf_op jit(solution)/shard_map/psum | solution.py:57
  65.4 0.1 convolution_multiply_fusion.2
  65.5 0.6 convolution_convert_fusion.2
  66.1 0.9 copy.16
  66.9 3.6 %all-to-all-start.1 = ((bf16[16,16,512]{2,1,0:T(8,128)(2,1)}), bf16[16,16,512]{2,1,0:T(8,128)(2,1)S(1)}, u32[]{:S(2)}, u32[]{:S(2)}) async-start(bf16[16,16,512]{2,1,0:T(8,128)(2,1)} %copy.16), calls=%async_computation.2 | async-start | bytes 524288 | tf_op jit(solution)/shard_map/all_to_all | solution.py:102
  70.5 0.4 fusion
  70.9 2.4 %convolution_convert_fusion.1 = bf16[16,4096,16]{1,0,2:T(8,128)(2,1)S(1)} fusion(f32[2,4096,16]{1,2,0:T(8,128)S(1)} %fusion, s32[2]{0:T(128)S(1)} %copy-done.3), kind=kOutput, calls=%fused_computation.3 | convolution fusion | flops 26214432 | bytes 2621448 | tf_op jit(solution)/shard_map/ba,bdr->adr/dot_general | solution.py:94
  73.3 2.5 %copy.14 = bf16[16,4096,16]{1,2,0:T(8,128)(2,1)} copy(bf16[16,4096,16]{1,0,2:T(8,128)(2,1)S(1)} %convolution_convert_fusion.1) | data formatting | bytes 4194304 | tf_op jit(solution)/shard_map/convert_element_type | solution.py:100
  75.8 4.8 %all-to-all-done.1 = bf16[16,16,512]{2,1,0:T(8,128)(2,1)S(1)} async-done(((bf16[16,16,512]{2,1,0:T(8,128)(2,1)}), bf16[16,16,512]{2,1,0:T(8,128)(2,1)S(1)}, u32[]{:S(2)}, u32[]{:S(2)}) %all-to-all-start.1) | async-done | bytes 262176 | tf_op jit(solution)/shard_map/all_to_all | solution.py:102
  80.6 3.7 %all-to-all-start = ((bf16[16,4096,16]{1,2,0:T(8,128)(2,1)}), bf16[16,4096,16]{1,2,0:T(8,128)(2,1)S(1)}, u32[]{:S(2)}, u32[]{:S(2)}) async-start(bf16[16,4096,16]{1,2,0:T(8,128)(2,1)} %copy.14), calls=%async_computation.1 | async-start | bytes 4194304 | tf_op jit(solution)/shard_map/all_to_all | solution.py:99
  84.3 0.3 convolution_multiply_fusion.1
  84.6 2.7 %fusion.19 = f32[2,128,4096]{2,1,0:T(8,128)} fusion(bf16[2,128,16]{1,2,0:T(8,128)(2,1)S(1)} %get-tuple-element.5, bf16[2,4096,16]{1,2,0:T(8,128)(2,1)S(1)} %gather_fusion), kind=kOutput, calls=%fused_computation.40 | convolution fusion | flops 33554432 | bytes 4464640 | tf_op jit(solution)/shard_map/bnr,bdr->bnd/dot_general | solution.py:68
  87.3 24.4 %all-gather.3.cloned.1.call-done = bf16[256,8192]{1,0:T(8,128)(2,1)} async-done(((bf16[256,4096]{1,0:T(8,128)(2,1)}), bf16[256,8192]{1,0:T(8,128)(2,1)}) %all-gather.3.cloned.1.call-update) | async-done | bytes 4194320 | tf_op jit(solution)/shard_map/all_gather | solution.py:28
  111.7 7.7 %fusion.2 = bf16[256,512]{1,0:T(8,128)(2,1)} fusion(f32[256,512]{1,0:T(8,128)S(1)} %bitcast.48, bf16[256,8192]{1,0:T(8,128)(2,1)} %all-gather.3.cloned.1.call-done, bf16[8192,512]{1,0:T(8,128)(2,1)} %param.8), kind=kOutput, calls=%fused_computation.11 | convolution fusion | flops 2147745792 | bytes 13369344 | tf_op jit(solution)/shard_map/dot_general | solution.py:27
  119.4 0.7 convert_reduce_fusion.1
  120.1 5.3 %all-to-all-done = bf16[16,4096,16]{1,2,0:T(8,128)(2,1)S(1)} async-done(((bf16[16,4096,16]{1,2,0:T(8,128)(2,1)}), bf16[16,4096,16]{1,2,0:T(8,128)(2,1)S(1)}, u32[]{:S(2)}, u32[]{:S(2)}) %all-to-all-start) | async-done | bytes 2097184 | tf_op jit(solution)/shard_map/all_to_all | solution.py:99
  125.4 1.0 convert_reduce_fusion
  126.4 42.0 %reduce-scatter.2.cloned.1.call-done = bf16[256,4096]{1,0:T(8,128)(2,1)} async-done(((bf16[256,8192]{1,0:T(8,128)(2,1)}), bf16[256,4096]{1,0:T(8,128)(2,1)}) %reduce-scatter.2.cloned.1.call-update) | async-done | bytes 2097168 | tf_op jit(solution)/shard_map/reduce_scatter | solution.py:38
  168.4 4.7 %fusion.1 = bf16[256,4096]{1,0:T(8,128)(2,1)} fusion(f32[2,128,4096]{2,1,0:T(8,128)} %fusion.19, bf16[256,4096]{1,0:T(8,128)(2,1)} %reduce-scatter.2.cloned.1.call-done), kind=kLoop, calls=%fused_computation.7 | loop fusion | flops 3145728 | bytes 8388608 | tf_op jit(solution)/shard_map/convert_element_type | solution.py:71
  (4 shorter events, 0.0 us)
Async XLA Ops:
  7.2 1.5 copy-start
  7.2 47.3 %all-gather.5.cloned.1.call-start = ((), (), s32[]{:S(2)}) async-start(), calls=%async_computation.4 | async-start | bytes 2228224 | tf_op jit(solution)/shard_map/all_gather | solution.py:43
  7.9 103.8 %all-gather.3.cloned.1.call-start = ((), (), s32[]{:S(2)}) async-start(), calls=%async_computation.3 | async-start | bytes 6291456 | tf_op jit(solution)/shard_map/all_gather | solution.py:28
  8.7 159.7 %reduce-scatter.2.cloned.1.call-start = ((), (), s32[]{:S(2)}) async-start(), calls=%async_computation.5 | async-start | bytes 6291456 | tf_op jit(solution)/shard_map/reduce_scatter | solution.py:38
  16.4 0.7 copy-start.3
  16.5 0.7 copy-start.2
  16.5 25.4 %copy-start.5 = (u32[32]{0:T(128)S(1)}, u32[32]{0:T(128)}, u32[]{:S(2)}) copy-start(u32[32]{0:T(128)} %constant.19) | copy-start | bytes 388
  16.5 34.1 %copy-start.4 = (s32[16]{0:T(128)S(1)}, s32[16]{0:T(128)}, u32[]{:S(2)}) copy-start(s32[16]{0:T(128)} %param.13) | copy-start | bytes 196
  16.5 40.2 %copy-start.1 = (bf16[256,4096]{1,0:T(8,128)(2,1)S(1)}, bf16[256,4096]{1,0:T(8,128)(2,1)}, u32[]{:S(2)}) copy-start(bf16[256,4096]{1,0:T(8,128)(2,1)} %param.7) | copy-start | bytes 6291460
  66.9 13.7 %all-to-all-start.1 = ((bf16[16,16,512]{2,1,0:T(8,128)(2,1)}), bf16[16,16,512]{2,1,0:T(8,128)(2,1)S(1)}, u32[]{:S(2)}, u32[]{:S(2)}) async-start(bf16[16,16,512]{2,1,0:T(8,128)(2,1)} %copy.16), calls=%async_computation.2 | async-start | bytes 524288 | tf_op jit(solution)/shard_map/all_to_all | solution.py:102
  80.6 44.8 %all-to-all-start = ((bf16[16,4096,16]{1,2,0:T(8,128)(2,1)}), bf16[16,4096,16]{1,2,0:T(8,128)(2,1)S(1)}, u32[]{:S(2)}, u32[]{:S(2)}) async-start(bf16[16,4096,16]{1,2,0:T(8,128)(2,1)} %copy.14), calls=%async_computation.1 | async-start | bytes 4194304 | tf_op jit(solution)/shard_map/all_to_all | solution.py:99
Sparse Core Ops, SparseCore 0:
  10.2 44.2 all-gather.4
  56.1 55.6 all-gather.2
  114.0 54.2 reduce-scatter.1
where the time goes:
time: 180 us
  waiting for transfers between devices  81.6 us (45%)
  blocking collectives  39.2 us (22%)
  matrix products  22.8 us (13%)
  between operations  14.5 us (8%)
  local copies, waits for them, and re-layouts  7.54 us (4%)
  starting transfers between devices  7.44 us (4%)
  other arithmetic  6.53 us (4%)
    reduce_scatter x1, waiting for transfers between devices, on_device(): lax.psum_scatter(partial_value.astype(jnp.bfloat16), 'tensor', scatter_di...  42 us
    all_gather x1, waiting for transfers between devices, on_device(): lax.all_gather(inputs, 'tensor', axis=1, tiled=True)  24.4 us
    all_gather x1, blocking collectives, on_device(): lax.all_gather(adapter_up_matrix, 'dp', axis=0, tiled=True)  24.1 us
    psum x1, blocking collectives, on_device(): lax.psum(low_part.astype(jnp.bfloat16), 'tensor').astype(jnp.float32)  8.07 us
    dot_general x1, matrix products, on_device(): lax.dot_general(value_cotangent, frozen_value_weight, (((1,), (1,)), ((),...  7.73 us
    dot_general x1, matrix products, on_device(): jnp.dot(lax.all_gather(inputs, 'tensor', axis=1, tiled=True), frozen_valu...  7.69 us
    unnamed x1, blocking collectives  7.05 us
    all_to_all x1, waiting for transfers between devices, on_device(): lax.all_to_all(dense_a.astype(jnp.bfloat16), 'dp', split_axis=0, concat_a...  5.29 us
  transfers between devices with their start and end apart: 5, of which 5 were waited for; matrix products, arithmetic and copies ran while one was open for 18% of the time, Pallas kernels for 0%

commit v1 on v0

v1 whole, which is shorter than its diff:
```python
import functools

import jax
import jax.numpy as jnp
from jax import lax
from jax.experimental import pallas as pl
from jax.experimental.pallas import tpu as pltpu
from jax.sharding import PartitionSpec as P

ADAPTER_RANK = 16
BLOCK = 128
PIECES = 4
VMEM_LIMIT = 48 * 1024 * 1024

adapter_scale = 2.0

NT = (((1,), (1,)), ((), ()))


def dot(a, b):
    return jnp.dot(a, b, preferred_element_type=jnp.float32)


def dot_nt(a, b):
    return lax.dot_general(a, b, NT, preferred_element_type=jnp.float32)


def own_kernel(t_ref, x_ref, w_ref, cot_ref, v_ref, g_ref, acc):
    step = pl.program_id(0)

    @pl.when(step == 0)
    def _():
        acc[...] = jnp.zeros_like(acc)

    acc[...] += dot(x_ref[...], w_ref[...])
    g_ref[...] = dot_nt(cot_ref[...], w_ref[...]).astype(g_ref.dtype)

    @pl.when(step == pl.num_programs(0) - 1)
    def _():
        v_ref[...] = acc[...]


def own_columns(tensor_index, x, w, cot):
    rows, features = x.shape
    values = w.shape[1]
    chunk = min(1024, features)
    steps = features // chunk
    return pl.pallas_call(
        own_kernel,
        grid_spec=pltpu.PrefetchScalarGridSpec(
            num_scalar_prefetch=1,
            grid=(steps,),
            in_specs=[
                pl.BlockSpec((rows, chunk), lambda j, t: (0, j)),
                pl.BlockSpec((chunk, values), lambda j, t: (t[0] * steps + j, 0)),
                pl.BlockSpec((rows, values), lambda j, t: (0, 0)),
            ],
            out_specs=[
                pl.BlockSpec((rows, values), lambda j, t: (0, 0)),
                pl.BlockSpec((rows, chunk), lambda j, t: (0, j)),
            ],
            scratch_shapes=[pltpu.VMEM((rows, values), jnp.float32)],
        ),
        out_shape=[
            jax.ShapeDtypeStruct((rows, values), jnp.float32),
            jax.ShapeDtypeStruct((rows, features), jnp.bfloat16),
        ],
        compiler_params=pltpu.CompilerParams(vmem_limit_bytes=VMEM_LIMIT),
        cost_estimate=pl.CostEstimate(
            flops=4 * rows * features * values,
            bytes_accessed=2 * features * values + 4 * rows * features,
            transcendentals=0,
        ),
    )(tensor_index, x, w, cot)


def other_values_kernel(parts, chunk, off_ref, x_ref, *refs):
    w_refs, v_ref = refs[:parts], refs[parts]
    total = None
    for k in range(parts):
        at = pl.multiple_of(off_ref[k], chunk)
        term = dot(x_ref[:, pl.ds(at, chunk)], w_refs[k][...])
        total = term if total is None else total + term
    v_ref[...] = total.astype(v_ref.dtype)


def other_values(offsets, x, w_parts):
    rows, features = x.shape
    chunk, values = w_parts[0].shape
    whole = pl.BlockSpec(memory_space=pltpu.VMEM)
    return pl.pallas_call(
        functools.partial(other_values_kernel, len(w_parts), chunk),
        in_specs=[pl.BlockSpec(memory_space=pltpu.SMEM)] + [whole] * (1 + len(w_parts)),
        out_specs=whole,
        out_shape=jax.ShapeDtypeStruct((rows, values), jnp.bfloat16),
        compiler_params=pltpu.CompilerParams(vmem_limit_bytes=VMEM_LIMIT),
        cost_estimate=pl.CostEstimate(
            flops=2 * rows * features * values,
            bytes_accessed=2 * features * (rows + values),
            transcendentals=0,
        ),
    )(offsets, x, *w_parts)


def input_gradient_kernel(groups, parts, chunk, nblocks, off_ref, own_ref, low_ref, down_ref, *refs):
    cot_refs = refs[:groups]
    w_refs = refs[groups : groups + groups * parts]
    out_ref = refs[-1]
    for k in range(parts):
        at = pl.multiple_of(off_ref[k], chunk)
        here = pl.ds(at, chunk)
        total = own_ref[:, here].astype(jnp.float32)
        for group in range(groups):
            term = dot_nt(cot_refs[group][...], w_refs[group * parts + k][...])
            total = total + term.astype(jnp.bfloat16).astype(jnp.float32)
        for b in range(nblocks):
            rows = slice(b * BLOCK, (b + 1) * BLOCK)
            added = total[rows] + dot(low_ref[rows], down_ref[b, :, here])
            out_ref[rows, here] = added.astype(out_ref.dtype)


def input_gradient(offsets, own, grad_low, down_blocks, cots, w_groups):
    rows, features = own.shape
    parts = len(w_groups[0])
    chunk, values = w_groups[0][0].shape
    flat = [w for group in w_groups for w in group]
    whole = pl.BlockSpec(memory_space=pltpu.VMEM)
    return pl.pallas_call(
        functools.partial(
            input_gradient_kernel, len(cots), parts, chunk, down_blocks.shape[0]
        ),
        in_specs=[pl.BlockSpec(memory_space=pltpu.SMEM)] + [whole] * (3 + len(cots) + len(flat)),
        out_specs=whole,
        out_shape=jax.ShapeDtypeStruct((rows, features), jnp.bfloat16),
        compiler_params=pltpu.CompilerParams(vmem_limit_bytes=VMEM_LIMIT),
        cost_estimate=pl.CostEstimate(
            flops=2 * rows * features * values * len(cots),
            bytes_accessed=2 * features * values * len(cots) + 4 * rows * features,
            transcendentals=0,
        ),
    )(offsets, own, grad_low, down_blocks, *cots, *flat)


def on_device(
    inputs,
    frozen_value_weight,
    adapter_down_matrix,
    adapter_up_matrix,
    value_cotangent,
    tenant_of_block,
    quotas,
):
    token_rows, features = inputs.shape
    values = frozen_value_weight.shape[1]
    nblocks = tenant_of_block.shape[0]
    owned = adapter_down_matrix.shape[0]
    n_dp, n_tensor = lax.axis_size("dp"), lax.axis_size("tensor")
    adapter_count = owned * n_dp
    me, t = lax.axis_index("dp"), lax.axis_index("tensor")
    upper = n_dp // 4

    def flip(a, mask):
        return lax.ppermute(a, "dp", [(i, i ^ mask) for i in range(n_dp)])

    def turn(a, shift):
        return lax.ppermute(a, "tensor", [(i, (i + shift) % n_tensor) for i in range(n_tensor)])

    shifts = range(1, n_tensor)

    up_own = adapter_up_matrix.reshape(owned * ADAPTER_RANK, values)
    ids = jnp.zeros((16, values), jnp.bfloat16)
    ids = ids.at[:, :nblocks].set(tenant_of_block.astype(jnp.bfloat16)[None, :])
    message = jnp.concatenate([up_own, ids], axis=0)
    stack = jnp.stack([message] + [flip(message, 4 * m) for m in range(1, upper)])
    stack = jnp.stack([stack, flip(stack, 1)])
    stack = jnp.stack([stack, flip(stack, 2)])
    stack = stack.reshape((n_dp,) + message.shape)

    def place(owner):
        relative = owner ^ me
        return ((relative >> 1) & 1) * (2 * upper) + (relative & 1) * upper + (relative >> 2)

    tenants_rel = stack[:, owned * ADAPTER_RANK, :nblocks].astype(jnp.int32)
    adapter_ids = jnp.arange(adapter_count, dtype=jnp.int32)
    counts = jnp.sum((tenants_rel.reshape(-1)[:, None] == adapter_ids[None, :]).astype(jnp.float32), axis=0)
    scale_all = quotas.astype(jnp.float32) / jnp.maximum(counts * BLOCK, 1.0)
    scale = lax.dynamic_slice_in_dim(scale_all, me * owned, owned)
    partner_tenant = tenants_rel[2 * upper]

    tenant = tenant_of_block
    owner, slot = tenant // owned, tenant % owned
    ups = stack[:, : owned * ADAPTER_RANK].reshape(n_dp * owned, ADAPTER_RANK, values)
    up_blocks = ups[place(owner) * owned + slot]

    cot_blocks = value_cotangent.reshape(nblocks, BLOCK, values)
    grad_part = jnp.einsum("bnk,brk->bnr", cot_blocks, up_blocks, preferred_element_type=jnp.float32)
    grad_sum = grad_part
    for s in shifts:
        grad_sum = grad_sum + turn(grad_part, s)
    grad_low = (adapter_scale * grad_sum).astype(jnp.bfloat16)

    down_own = jnp.swapaxes(adapter_down_matrix, 1, 2)
    down = jnp.stack([down_own] + [flip(down_own, 4 * m) for m in range(1, upper)])
    down = jnp.stack([down, flip(down, 1)])
    down = down.reshape(2 * upper * owned, ADAPTER_RANK, features)

    def near(who):
        o = who // owned
        relative = o ^ me
        return ((relative & 1) * upper + (relative >> 2)) * owned + who % owned

    def on_my_side(who):
        return (((who // owned) ^ me) & 2) == 0

    from_partner = flip(down[near(partner_tenant)], 2)
    down_blocks = jnp.where(on_my_side(tenant)[:, None, None], down[near(tenant)], from_partner)

    input_blocks = inputs.reshape(nblocks, BLOCK, features)
    low_part = jnp.einsum("bnd,brd->bnr", input_blocks, down_blocks, preferred_element_type=jnp.float32)
    low_sum = low_part
    for s in shifts:
        low_sum = low_sum + turn(low_part, s)
    low = low_sum.astype(jnp.bfloat16)

    pieces = PIECES if features % (PIECES * 4 * 128) == 0 else 1
    chunk = features // (pieces * 4)
    offsets, w_groups = [], []
    for s in shifts:
        parts = []
        for p in range(pieces):
            bit = 1 + p % 2
            quarter = ((me >> bit) & 1) * 2 + (me & 1)
            start = ((t + s) % n_tensor) * features + p * 4 * chunk + quarter * chunk
            sent = lax.dynamic_slice_in_dim(frozen_value_weight, start, chunk, 0)
            first = turn(sent, s)
            second = flip(first, 1 << bit)
            both = jnp.stack([first, second])
            crossed = flip(both, 1)
            parts += [first, second, crossed[0], crossed[1]]
            if s == 1:
                offsets += [(p * 4 + (quarter ^ q)) * chunk for q in (0, 2, 1, 3)]
        w_groups.append(parts)
    offsets = jnp.stack(offsets).astype(jnp.int32)
    cots = [turn(value_cotangent, s) for s in shifts]

    value_own, gradient_own = own_columns(t.reshape(1).astype(jnp.int32), inputs, frozen_value_weight, value_cotangent)
    value_sum = value_own
    for s in shifts:
        value_sum = value_sum + turn(other_values(offsets, inputs, w_groups[s - 1]), -s).astype(jnp.float32)
    raised = jnp.einsum("bnr,brk->bnk", low.reshape(nblocks, BLOCK, ADAPTER_RANK), up_blocks, preferred_element_type=jnp.float32)
    adapted_values = (value_sum + adapter_scale * raised.reshape(token_rows, values)).astype(jnp.bfloat16)

    gradient_inputs = input_gradient(
        offsets,
        gradient_own,
        grad_low.reshape(token_rows, ADAPTER_RANK),
        down_blocks,
        cots,
        w_groups,
    )

    down_grad_blocks = jnp.einsum("bnr,bnd->brd", grad_low, input_blocks, preferred_element_type=jnp.float32).astype(jnp.bfloat16)
    partner_blocks = flip(down_grad_blocks, 2)
    four = jnp.concatenate([down_grad_blocks, partner_blocks]).astype(jnp.float32)
    four_tenants = jnp.concatenate([tenant, partner_tenant])
    where = jnp.where(on_my_side(four_tenants), near(four_tenants), -1)
    held = 2 * upper * owned
    weight = (jnp.arange(held, dtype=jnp.int32)[:, None] == where[None, :]).astype(jnp.float32)
    sums = jnp.sum(weight[:, :, None, None] * four[None], axis=1)
    sums = sums.reshape(2, upper, owned, ADAPTER_RANK, features)
    crossed = flip(sums[1].astype(jnp.bfloat16), 1)
    sums = sums[0] + crossed.astype(jnp.float32)
    down_total = sums[0]
    for m in range(1, upper):
        down_total = down_total + flip(sums[m].astype(jnp.bfloat16), 4 * m).astype(jnp.float32)
    down_grad = jnp.swapaxes(down_total * scale[:, None, None], 1, 2)

    up_grad_blocks = adapter_scale * jnp.einsum("bnr,bnk->brk", low, cot_blocks, preferred_element_type=jnp.float32)
    hot = (adapter_ids[:, None] == tenant[None, :]).astype(jnp.float32)
    dense = jnp.sum(hot[:, :, None, None] * up_grad_blocks[None], axis=1).astype(jnp.bfloat16)
    received = lax.all_to_all(dense, "dp", split_axis=0, concat_axis=0, tiled=True)
    received = received.reshape(n_dp, owned, ADAPTER_RANK, values).astype(jnp.float32)
    gradient_up_matrix = jnp.sum(received, axis=0) * scale[:, None, None]
    return (adapted_values, gradient_inputs, down_grad, gradient_up_matrix)


def solution(mesh):
    placed = (
        P("dp", "tensor"),
        P(None, "tensor"),
        P("dp", "tensor", None),
        P("dp", None, "tensor"),
        P("dp", "tensor"),
        P("dp"),
        P(),
    )
    return jax.shard_map(
        on_device,
        mesh=mesh,
        in_specs=placed,
        out_specs=(
            P("dp", "tensor"),
            P("dp", "tensor"),
            P("dp", "tensor", None),
            P("dp", None, "tensor"),
        ),
        check_vma=False,
    )
```

time: 180 us -> 125 us (0.69)
  waiting for transfers between devices: 81.6 us -> 25.4 us
  blocking collectives: 39.2 us -> 0 us
  starting transfers between devices: 7.44 us -> 38 us
  matrix products: 22.8 us -> 3.15 us
  other arithmetic: 6.53 us -> 23 us
  Pallas kernels: 0 us -> 13.6 us
  between operations: 14.5 us -> 1.04 us
  local copies, waits for them, and re-layouts: 7.54 us -> 20.2 us
    reduce_scatter x1 -> x0, waiting for transfers between devices: 42 us -> none  [on_device(): lax.psum_scatter(partial_value.astype(jnp.bfloat16), 'tensor', scatter_di...]
    ppermute x0 -> x31, starting transfers between devices: none -> 33.6 us  [the longest x23 25.3 us: flip(): return lax.ppermute(a, 'dp', [(i, i ^ mask) for i in range(n_dp)])]
    all_gather x2 -> x0, waiting for transfers between devices: 28.1 us -> none  [the longest x1 24.4 us: on_device(): lax.all_gather(inputs, 'tensor', axis=1, tiled=True)]
    ppermute x0 -> x31, waiting for transfers between devices: none -> 25.4 us  [the longest x23 21.5 us: flip(): return lax.ppermute(a, 'dp', [(i, i ^ mask) for i in range(n_dp)])]
    all_gather x1 -> x0, blocking collectives: 24.1 us -> none  [on_device(): lax.all_gather(adapter_up_matrix, 'dp', axis=0, tiled=True)]
    dot_general x11 -> x5, matrix products: 22.8 us -> 3.15 us  [the longest x1 1.1 us: on_device(): jnp.einsum('bnr,brk->bnk', low.reshape(nblocks, BLOCK, ADAPTER_RANK), up_...]
    pallas_call x0 -> x3, Pallas kernels: none -> 13.6 us  [the longest x1 5.51 us: input_gradient(): pl.pallas_call(functools.partial(input_gradient_kernel, len(cots), parts,...]
    another operation x0 -> x13, other arithmetic: none -> 13.5 us  [the longest x4 6.34 us: on_device(): both = jnp.stack([first, second])]
  transfers between devices with their start and end apart: 5 -> 32, of which waited for: 5 -> 8; matrix products, arithmetic and copies ran while one was open for 18% -> 32% of each run, Pallas kernels for 0% -> 11%
where the time goes in v1:
time: 125 us; the launch traced here: 124 us
  starting transfers between devices  38 us (30%)
  waiting for transfers between devices  25.4 us (20%)
  other arithmetic  23 us (18%)
  local copies, waits for them, and re-layouts  20.2 us (16%)
  Pallas kernels  13.6 us (11%)
  matrix products  3.15 us (3%)
    ppermute x23, starting transfers between devices, flip(): return lax.ppermute(a, 'dp', [(i, i ^ mask) for i in range(n_dp)])  25.3 us
    ppermute x23, waiting for transfers between devices, flip(): return lax.ppermute(a, 'dp', [(i, i ^ mask) for i in range(n_dp)])  21.5 us
    ppermute x8, starting transfers between devices, turn(): lax.ppermute(a, 'tensor', [(i, (i + shift) % n_tensor) for i in range(n_t...  8.26 us
    another operation x4, other arithmetic, on_device(): both = jnp.stack([first, second])  6.34 us
    pallas_call x1, Pallas kernels, input_gradient(): pl.pallas_call(functools.partial(input_gradient_kernel, len(cots), parts,...  5.51 us
    pallas_call x1, Pallas kernels, own_columns(): pl.pallas_call(own_kernel, grid_spec=pltpu.PrefetchScalarGridSpec(num_sca...  4.98 us
    unnamed x40, local copies, waits for them, and re-layouts  4.7 us
    all_to_all x1, starting transfers between devices, on_device(): lax.all_to_all(dense, 'dp', split_axis=0, concat_axis=0, tiled=True)  4.38 us
  transfers between devices with their start and end apart: 32, of which 8 were waited for; matrix products, arithmetic and copies ran while one was open for 32% of the time, Pallas kernels for 11%

profile of v1, /device:TPU:0, one launch (start us, length us, event | category | flops | bytes accessed | tf_op | source)
XLA Modules:
  0.0 124.5 jit_solution(12608729516645907251)
XLA Ops:
  0.6 5.1 %collective-permute-start.15 = (bf16[1,16,4096]{2,1,0:T(8,128)(2,1)}, bf16[1,16,4096]{2,1,0:T(8,128)(2,1)S(1)}, u32[]{:S(2)}, u32[]{:S(2)}) collective-permute-start(bf16[1,16,4096]{2,1,0:T(8,128)(2,1)} %bitcast.33), channel_id=1, source_target_pairs={{0,12},{1,13},{2,14},{3,15},{4,8},{5,9},{6,10},{7,11},{8,4},{9,5},... | collective-permute-start | bytes 393224 | tf_op jit(solution)/shard_map/ppermute | solution.py:163
  6.4 1.3 %broadcast_select_fusion.1 = bf16[2]{0:T(256)(128)(2,1)S(1)} fusion(pred[]{:T(512)} %compare_reduce_fusion, s32[2]{0:T(128)} %param.14), kind=kLoop, calls=%fused_computation.70 | loop fusion | flops 4 | bytes 13 | tf_op jit(solution)/shard_map/select.20
  8.4 1.9 %collective-permute-start.19 = (bf16[32,512]{1,0:T(8,128)(2,1)S(1)}, bf16[32,512]{1,0:T(8,128)(2,1)S(1)}, u32[]{:S(2)}, u32[]{:S(2)}) collective-permute-start(bf16[32,512]{1,0:T(8,128)(2,1)S(1)} %get-tuple-element.43), channel_id=1, source_target_pairs={{0,12},{1,13},{2,14},{3,15},{4,8},{5,9},{6,10},{7,11},{8,4},{9,5},... | collective-permute-start | bytes 98312 | tf_op jit(solution)/shard_map/ppermute | solution.py:163
  10.3 1.0 collective-permute-start.18
  11.4 1.5 %collective-permute-start.17 = (bf16[32,512]{1,0:T(8,128)(2,1)S(1)}, bf16[32,512]{1,0:T(8,128)(2,1)S(1)}, u32[]{:S(2)}, u32[]{:S(2)}) collective-permute-start(bf16[32,512]{1,0:T(8,128)(2,1)S(1)} %get-tuple-element.43), channel_id=1, source_target_pairs={{0,4},{1,5},{2,6},{3,7},{4,0},{5,1},{6,2},{7,3},{8,12},{9,13},{10,... | collective-permute-start | bytes 98312 | tf_op jit(solution)/shard_map/ppermute | solution.py:163
  14.8 1.6 %copy-done = bf16[256,4096]{1,0:T(8,128)(2,1)S(1)} copy-done((bf16[256,4096]{1,0:T(8,128)(2,1)S(1)}, bf16[256,4096]{1,0:T(8,128)(2,1)}, u32[]{:S(2)}) %copy-start) | copy-done | bytes 2097176
  16.4 0.9 copy-done.2
  17.3 5.0 %shard_map.102 = (f32[256,512]{1,0:T(8,128)S(1)}, bf16[256,4096]{1,0:T(8,128)(2,1)S(1)}) custom-call(s32[1]{0:T(128)} %bitcast.t_ref, bf16[256,4096]{1,0:T(8,128)(2,1)S(1)} %copy-done, bf16[8192,512]{1,0:T(8,128)(2,1)} %w_ref.1, bf16[256,512]{1,0:T(8,128)(2,1)S(1)} %copy-done.2), custom_call_target="tpu_custom_call" | custom-call | flops 2147483648 | bytes 8388608 | tf_op jit(solution)/shard_map/pallas_call | solution.py:48
  23.1 2.9 %constant_dynamic-slice_fusion = (bf16[256,512]{1,0:T(8,128)(2,1)}, bf16[256,512]{1,0:T(8,128)(2,1)}, bf16[256,512]{1,0:T(8,128)(2,1)}, bf16[256,512]{1,0:T(8,128)(2,1)}) fusion(bf16[8192,512]{1,0:T(8,128)(2,1)} %w_ref.1, s32[]{:T(128)S(6)} %select_n.96, s32[]{:T(128)S(6)} %select_n.94, s32[]{:T(128)S(6)} %select_n.93, s32[]{:T(128)S(6)} %select_n.95), kind=kLoop, calls=%fused_computation.66 | loop fusion | bytes 2097168 | tf_op jit(solution)/shard_map/dynamic_slice | solution.py:234
  26.6 1.5 %collective-permute-start = (bf16[256,512]{1,0:T(8,128)(2,1)}, bf16[256,512]{1,0:T(8,128)(2,1)S(1)}, u32[]{:S(2)}, u32[]{:S(2)}) collective-permute-start(bf16[256,512]{1,0:T(8,128)(2,1)} %get-tuple-element.22), channel_id=1, source_target_pairs={{0,16},{16,0},{1,17},{17,1},{2,18},{18,2},{3,19},{19,3},{4,20},{20... | collective-permute-start | bytes 786440 | tf_op jit(solution)/shard_map/ppermute | solution.py:166
  28.4 1.2 collective-permute-done.20
  30.8 1.5 %collective-permute-start.6 = (bf16[256,512]{1,0:T(8,128)(2,1)}, bf16[256,512]{1,0:T(8,128)(2,1)S(1)}, u32[]{:S(2)}, u32[]{:S(2)}) collective-permute-start(bf16[256,512]{1,0:T(8,128)(2,1)} %get-tuple-element.23), channel_id=1, source_target_pairs={{0,16},{16,0},{1,17},{17,1},{2,18},{18,2},{3,19},{19,3},{4,20},{20... | collective-permute-start | bytes 786440 | tf_op jit(solution)/shard_map/ppermute | solution.py:166
  33.5 1.5 %collective-permute-start.21 = (bf16[2,4,32,512]{3,2,1,0:T(8,128)(2,1)S(1)}, bf16[2,4,32,512]{3,2,1,0:T(8,128)(2,1)S(1)}, u32[]{:S(2)}, u32[]{:S(2)}) collective-permute-start(bf16[2,4,32,512]{3,2,1,0:T(8,128)(2,1)S(1)} %get-tuple-element.39), channel_id=1, source_target_pairs={{0,2},{1,3},{2,0},{3,1},{4,6},{5,7},{6,4},{7,5},{8,10},{9,11},{10,... | collective-permute-start | bytes 786440 | tf_op jit(solution)/shard_map/ppermute | solution.py:163
  35.0 2.1 %fusion.17 = (bf16[1,4,1,16,4096]{4,3,1,2,0:T(8,128)(2,1)}, bf16[4,1,16,4096]{3,2,1,0:T(8,128)(2,1)}) fusion(bf16[1,1,16,4096]{3,2,1,0:T(8,128)(2,1)} %bitcast.148, bf16[1,1,16,4096]{3,2,1,0:T(8,128)(2,1)} %bitcast.149, bf16[1,1,16,4096]{3,2,1,0:T(8,128)(2,1)} %bitcast.35, bf16[1,1,16,4096]{3,2,1,0:T(8,128)(2,1)} %bitcast.34), kind=kLoop, calls=%fused_computation.82 | loop fusion | flops 786432 | bytes 1572864 | tf_op jit(solution)/shard_map/stack | solution.py:204
  37.2 3.9 %collective-permute-done.21 = bf16[2,4,32,512]{3,2,1,0:T(8,128)(2,1)S(1)} collective-permute-done((bf16[2,4,32,512]{3,2,1,0:T(8,128)(2,1)S(1)}, bf16[2,4,32,512]{3,2,1,0:T(8,128)(2,1)S(1)}, u32[]{:S(2)}, u32[]{:S(2)}) %collective-permute-start.21) | collective-permute-done | bytes 262176 | tf_op jit(solution)/shard_map/ppermute | solution.py:163
  41.9 1.5 %gather_fusion.2 = bf16[2,16,512]{2,1,0:T(8,128)(2,1)S(1)} fusion(bf16[16,16,512]{2,1,0:T(8,128)(2,1)} %slice.111, s32[1024]{0:T(1024)S(1)} %pad_clamp_fusion), kind=kCustom, calls=%fused_computation.2 | custom fusion | bytes 65544 | tf_op jit(solution)/shard_map/gather | solution.py:193
  43.5 1.5 %collective-permute-start.24 = (f32[2,128,16]{1,2,0:T(8,128)S(1)}, f32[2,128,16]{1,2,0:T(8,128)S(1)}, u32[]{:S(2)}, u32[]{:S(2)}) collective-permute-start(f32[2,128,16]{1,2,0:T(8,128)S(1)} %convolution_bitcast_fusion), channel_id=1, source_target_pairs={{0,16},{16,0},{1,17},{17,1},{2,18},{18,2},{3,19},{19,3},{4,20},{20... | collective-permute-start | bytes 49160 | tf_op jit(solution)/shard_map/ppermute | solution.py:166
  46.0 1.6 %collective-permute-start.1 = (bf16[256,512]{1,0:T(8,128)(2,1)S(1)}, bf16[256,512]{1,0:T(8,128)(2,1)}, u32[]{:S(2)}, u32[]{:S(2)}) collective-permute-start(bf16[256,512]{1,0:T(8,128)(2,1)S(1)} %collective-permute-done.refs_0_.refs_1_), channel_id=1, source_target_pairs={{0,2},{1,3},{2,0},{3,1},{4,6},{5,7},{6,4},{7,5},{8,10},{9,11},{10,... | collective-permute-start | bytes 786440 | tf_op jit(solution)/shard_map/ppermute | solution.py:163
  47.6 1.5 %collective-permute-start.4 = (bf16[256,512]{1,0:T(8,128)(2,1)S(1)}, bf16[256,512]{1,0:T(8,128)(2,1)}, u32[]{:S(2)}, u32[]{:S(2)}) collective-permute-start(bf16[256,512]{1,0:T(8,128)(2,1)S(1)} %collective-permute-done.3.refs_4_.refs_5_), channel_id=1, source_target_pairs={{0,4},{1,5},{2,6},{3,7},{4,0},{5,1},{6,2},{7,3},{8,12},{9,13},{10,... | collective-permute-start | bytes 786440 | tf_op jit(solution)/shard_map/ppermute | solution.py:163
  49.1 1.6 %collective-permute-done.24 = f32[2,128,16]{1,2,0:T(8,128)S(1)} collective-permute-done((f32[2,128,16]{1,2,0:T(8,128)S(1)}, f32[2,128,16]{1,2,0:T(8,128)S(1)}, u32[]{:S(2)}, u32[]{:S(2)}) %collective-permute-start.24) | collective-permute-done | bytes 16416 | tf_op jit(solution)/shard_map/ppermute | solution.py:166
  50.7 1.5 %collective-permute-start.7 = (bf16[256,512]{1,0:T(8,128)(2,1)S(1)}, bf16[256,512]{1,0:T(8,128)(2,1)}, u32[]{:S(2)}, u32[]{:S(2)}) collective-permute-start(bf16[256,512]{1,0:T(8,128)(2,1)S(1)} %collective-permute-done.6.refs_8_.refs_9_), channel_id=1, source_target_pairs={{0,2},{1,3},{2,0},{3,1},{4,6},{5,7},{6,4},{7,5},{8,10},{9,11},{10,... | collective-permute-start | bytes 786440 | tf_op jit(solution)/shard_map/ppermute | solution.py:163
  52.2 1.1 convolution_convert_fusion
  53.5 1.6 %collective-permute-start.25 = (bf16[256,512]{1,0:T(8,128)(2,1)S(1)}, bf16[256,512]{1,0:T(8,128)(2,1)}, u32[]{:S(2)}, u32[]{:S(2)}) collective-permute-start(bf16[256,512]{1,0:T(8,128)(2,1)S(1)} %copy-done.3), channel_id=1, source_target_pairs={{0,16},{16,0},{1,17},{17,1},{2,18},{18,2},{3,19},{19,3},{4,20},{20... | collective-permute-start | bytes 786440 | tf_op jit(solution)/shard_map/ppermute | solution.py:166
  55.3 1.5 %collective-permute-start.10 = (bf16[256,512]{1,0:T(8,128)(2,1)S(1)}, bf16[256,512]{1,0:T(8,128)(2,1)S(1)}, u32[]{:S(2)}, u32[]{:S(2)}) collective-permute-start(bf16[256,512]{1,0:T(8,128)(2,1)S(1)} %collective-permute-done.9.refs_12_.refs_13_), channel_id=1, source_target_pairs={{0,4},{1,5},{2,6},{3,7},{4,0},{5,1},{6,2},{7,3},{8,12},{9,13},{10,... | collective-permute-start | bytes 786440 | tf_op jit(solution)/shard_map/ppermute | solution.py:163
  56.8 1.9 %pad_maximum_fusion.1 = bf16[2,256,512]{2,1,0:T(8,128)(2,1)} fusion(bf16[1,256,512]{2,1,0:T(8,128)(2,1)} %bitcast.18, bf16[1,256,512]{2,1,0:T(8,128)(2,1)S(1)} %bitcast.134), kind=kLoop, calls=%fused_computation.17 | loop fusion | flops 262144 | bytes 1048576 | tf_op jit(solution)/shard_map/stack | solution.py:237
  58.6 1.5 %collective-permute-start.26 = (bf16[2,16,4096]{2,1,0:T(8,128)(2,1)}, bf16[2,16,4096]{2,1,0:T(8,128)(2,1)}, u32[]{:S(2)}, u32[]{:S(2)}) collective-permute-start(bf16[2,16,4096]{2,1,0:T(8,128)(2,1)} %convolution_convert_fusion), channel_id=1, source_target_pairs={{0,2},{1,3},{2,0},{3,1},{4,6},{5,7},{6,4},{7,5},{8,10},{9,11},{10,... | collective-permute-start | bytes 786440 | tf_op jit(solution)/shard_map/ppermute | solution.py:163
  60.2 1.8 %pad_maximum_fusion.2 = bf16[2,256,512]{2,1,0:T(8,128)(2,1)} fusion(bf16[1,256,512]{2,1,0:T(8,128)(2,1)} %bitcast.22, bf16[1,256,512]{2,1,0:T(8,128)(2,1)S(1)} %bitcast.135), kind=kLoop, calls=%fused_computation.18 | loop fusion | flops 262144 | bytes 1048576 | tf_op jit(solution)/shard_map/stack | solution.py:237
  62.0 1.8 %pad_maximum_fusion.3 = bf16[2,256,512]{2,1,0:T(8,128)(2,1)} fusion(bf16[1,256,512]{2,1,0:T(8,128)(2,1)} %bitcast.26, bf16[1,256,512]{2,1,0:T(8,128)(2,1)S(1)} %bitcast.136), kind=kLoop, calls=%fused_computation.19 | loop fusion | flops 262144 | bytes 1048576 | tf_op jit(solution)/shard_map/stack | solution.py:237
  65.3 2.1 %pad_maximum_fusion = bf16[2,4,1,16,4096]{4,3,1,2,0:T(8,128)(2,1)} fusion(bf16[1,4,1,16,4096]{4,3,1,2,0:T(8,128)(2,1)} %bitcast.39, bf16[1,4,1,16,4096]{4,3,1,2,0:T(8,128)(2,1)S(1)} %copy-done.14), kind=kLoop, calls=%fused_computation.12 | loop fusion | flops 524288 | bytes 2097152 | tf_op jit(solution)/shard_map/stack | solution.py:204
  67.4 2.5 %gather_fusion = bf16[2,16,4096]{2,1,0:T(8,128)(2,1)} fusion(bf16[8,16,4096]{2,1,0:T(8,128)(2,1)} %bitcast.140, s32[1024]{0:T(1024)S(1)} %pad_clamp_fusion.2), kind=kCustom, calls=%fused_computation | custom fusion | bytes 524296 | tf_op jit(solution)/shard_map/gather | solution.py:216
  69.9 1.8 %gather_fusion.1 = bf16[2,16,4096]{2,1,0:T(8,128)(2,1)S(1)} fusion(bf16[8,16,4096]{2,1,0:T(8,128)(2,1)} %bitcast.141, s32[1024]{0:T(1024)S(1)} %pad_clamp_fusion.1), kind=kCustom, calls=%fused_computation.1 | custom fusion | bytes 524296 | tf_op jit(solution)/shard_map/gather | solution.py:215
  72.3 1.1 maximum_convert_fusion
  74.1 6.3 %collective-permute-done.22 = bf16[2,16,4096]{2,1,0:T(8,128)(2,1)S(1)} collective-permute-done((bf16[2,16,4096]{2,1,0:T(8,128)(2,1)S(1)}, bf16[2,16,4096]{2,1,0:T(8,128)(2,1)S(1)}, u32[]{:S(2)}, u32[]{:S(2)}) %collective-permute-start.22) | collective-permute-done | bytes 262176 | tf_op jit(solution)/shard_map/ppermute | solution.py:163
  82.6 2.3 %collective-permute-done.23 = f32[2,128,16]{1,2,0:T(8,128)S(1)} collective-permute-done((f32[2,128,16]{1,2,0:T(8,128)S(1)}, f32[2,128,16]{1,2,0:T(8,128)S(1)}, u32[]{:S(2)}, u32[]{:S(2)}) %collective-permute-start.23) | collective-permute-done | bytes 16416 | tf_op jit(solution)/shard_map/ppermute | solution.py:166
  84.9 1.1 convolution_multiply_fusion
  87.1 4.4 %all-to-all-start = ((bf16[16,16,512]{2,1,0:T(8,128)(2,1)}), bf16[16,16,512]{2,1,0:T(8,128)(2,1)}, u32[]{:S(2)}, u32[]{:S(2)}) async-start(bf16[16,16,512]{2,1,0:T(8,128)(2,1)} %multiply_reduce_fusion.1), calls=%async_computation | async-start | bytes 524288 | tf_op jit(solution)/shard_map/all_to_all | solution.py:281
  91.9 1.1 slice_bitcast_fusion.8
  93.0 1.1 slice_bitcast_fusion.6
  94.1 1.1 slice_bitcast_fusion.4
  95.2 1.1 slice_bitcast_fusion.2
  96.3 3.1 %shard_map.103 = bf16[256,512]{1,0:T(8,128)(2,1)S(1)} custom-call(s32[16]{0:T(128)S(1)} %stack.160.off_ref, bf16[256,4096]{1,0:T(8,128)(2,1)} %x_ref.3, bf16[256,512]{1,0:T(8,128)(2,1)S(1)} %collective-permute-done.refs_0_.refs_1_, bf16[256,512]{1,0:T(8,128)(2,1)} %collective-permute-done.1.refs_1_.refs_2_, ...), custom_call_target="tpu_custom_call" | custom-call | flops 1073741824 | bytes 6291456 | tf_op jit(solution)/shard_map/pallas_call | solution.py:91
  100.0 5.5 %shard_map.104 = bf16[256,4096]{1,0:T(8,128)(2,1)} custom-call(s32[16]{0:T(128)S(1)} %stack.160.off_ref, bf16[256,4096]{1,0:T(8,128)(2,1)} %copy-done.8, bf16[256,16]{1,0:T(8,128)(2,1)S(1)} %bitcast.139, bf16[2,16,4096]{2,1,0:T(8,128)(2,1)S(1)} %broadcast_select_fusion.down_ref, bf16[256,512]{1,0:T(8,128)(2,1)} %collective-permute-done.25.refs_0_, ...), custom_call_target="tpu_custom_call" | custom-call | flops 1073741824 | bytes 8388608 | tf_op jit(solution)/shard_map/pallas_call | solution.py:128
  105.7 3.6 %collective-permute-start.30 = (bf16[1,16,4096]{2,1,0:T(8,128)(2,1)S(1)}, bf16[1,16,4096]{2,1,0:T(8,128)(2,1)S(1)}, u32[]{:S(2)}, u32[]{:S(2)}) collective-permute-start(bf16[1,16,4096]{2,1,0:T(8,128)(2,1)S(1)} %slice_bitcast_fusion.10), channel_id=1, source_target_pairs={{0,12},{1,13},{2,14},{3,15},{4,8},{5,9},{6,10},{7,11},{8,4},{9,5},... | collective-permute-start | bytes 393224 | tf_op jit(solution)/shard_map/ppermute | solution.py:163
  111.1 2.9 %collective-permute-done.30 = bf16[1,16,4096]{2,1,0:T(8,128)(2,1)S(1)} collective-permute-done((bf16[1,16,4096]{2,1,0:T(8,128)(2,1)S(1)}, bf16[1,16,4096]{2,1,0:T(8,128)(2,1)S(1)}, u32[]{:S(2)}, u32[]{:S(2)}) %collective-permute-start.30) | collective-permute-done | bytes 131104 | tf_op jit(solution)/shard_map/ppermute | solution.py:163
  114.0 6.8 %collective-permute-done.29 = bf16[1,16,4096]{2,1,0:T(8,128)(2,1)S(1)} collective-permute-done((bf16[1,16,4096]{2,1,0:T(8,128)(2,1)S(1)}, bf16[1,16,4096]{2,1,0:T(8,128)(2,1)S(1)}, u32[]{:S(2)}, u32[]{:S(2)}) %collective-permute-start.29) | collective-permute-done | bytes 131104 | tf_op jit(solution)/shard_map/ppermute | solution.py:163
  120.8 1.4 %fusion.9 = f32[1,4096,16]{1,2,0:T(8,128)} fusion(f32[4,1,16,4096]{3,2,1,0:T(8,128)S(1)} %get-tuple-element.25, bf16[1,16,4096]{2,1,0:T(8,128)(2,1)S(1)} %collective-permute-done.30, bf16[1,16,4096]{2,1,0:T(8,128)(2,1)S(1)} %collective-permute-done.29, bf16[1,16,4096]{2,1,0:T(8,128)(2,1)S(1)} %collective-permute-done.28, f32[]{:T(128)} %bitcast.69), kind=kLoop, calls=%fused_computation.32 | loop fusion | flops 458752 | bytes 917508 | tf_op jit(solution)/shard_map/transpose | solution.py:276
  122.2 1.0 convert_reduce_fusion
  123.2 1.2 %multiply_bitcast_fusion = f32[1,16,512]{2,1,0:T(8,128)} fusion(f32[16,512]{1,0:T(8,128)S(1)} %convert_reduce_fusion, f32[]{:T(128)} %bitcast.69), kind=kLoop, calls=%fused_computation.48 | loop fusion | flops 8192 | bytes 65540 | tf_op jit(solution)/shard_map/mul | solution.py:283
  (119 shorter events, 18.7 us)
Async XLA Ops:
  0.6 29.5 %collective-permute-start.15 = (bf16[1,16,4096]{2,1,0:T(8,128)(2,1)}, bf16[1,16,4096]{2,1,0:T(8,128)(2,1)S(1)}, u32[]{:S(2)}, u32[]{:S(2)}) collective-permute-start(bf16[1,16,4096]{2,1,0:T(8,128)(2,1)} %bitcast.33), channel_id=1, source_target_pairs={{0,12},{1,13},{2,14},{3,15},{4,8},{5,9},{6,10},{7,11},{8,4},{9,5},... | collective-permute-start | bytes 393224 | tf_op jit(solution)/shard_map/ppermute | solution.py:163
  5.7 26.6 %collective-permute-start.14 = (bf16[1,16,4096]{2,1,0:T(8,128)(2,1)}, bf16[1,16,4096]{2,1,0:T(8,128)(2,1)S(1)}, u32[]{:S(2)}, u32[]{:S(2)}) collective-permute-start(bf16[1,16,4096]{2,1,0:T(8,128)(2,1)} %bitcast.33), channel_id=1, source_target_pairs={{0,8},{1,9},{2,10},{3,11},{4,12},{5,13},{6,14},{7,15},{8,0},{9,1},... | collective-permute-start | bytes 393224 | tf_op jit(solution)/shard_map/ppermute | solution.py:163
  8.4 17.6 %collective-permute-start.19 = (bf16[32,512]{1,0:T(8,128)(2,1)S(1)}, bf16[32,512]{1,0:T(8,128)(2,1)S(1)}, u32[]{:S(2)}, u32[]{:S(2)}) collective-permute-start(bf16[32,512]{1,0:T(8,128)(2,1)S(1)} %get-tuple-element.43), channel_id=1, source_target_pairs={{0,12},{1,13},{2,14},{3,15},{4,8},{5,9},{6,10},{7,11},{8,4},{9,5},... | collective-permute-start | bytes 98312 | tf_op jit(solution)/shard_map/ppermute | solution.py:163
  10.3 16.3 %collective-permute-start.18 = (bf16[32,512]{1,0:T(8,128)(2,1)S(1)}, bf16[32,512]{1,0:T(8,128)(2,1)S(1)}, u32[]{:S(2)}, u32[]{:S(2)}) collective-permute-start(bf16[32,512]{1,0:T(8,128)(2,1)S(1)} %get-tuple-element.43), channel_id=1, source_target_pairs={{0,8},{1,9},{2,10},{3,11},{4,12},{5,13},{6,14},{7,15},{8,0},{9,1},... | collective-permute-start | bytes 98312 | tf_op jit(solution)/shard_map/ppermute | solution.py:163
  11.4 16.8 %collective-permute-start.17 = (bf16[32,512]{1,0:T(8,128)(2,1)S(1)}, bf16[32,512]{1,0:T(8,128)(2,1)S(1)}, u32[]{:S(2)}, u32[]{:S(2)}) collective-permute-start(bf16[32,512]{1,0:T(8,128)(2,1)S(1)} %get-tuple-element.43), channel_id=1, source_target_pairs={{0,4},{1,5},{2,6},{3,7},{4,0},{5,1},{6,2},{7,3},{8,12},{9,13},{10,... | collective-permute-start | bytes 98312 | tf_op jit(solution)/shard_map/ppermute | solution.py:163
  14.8 1.6 %copy-start = (bf16[256,4096]{1,0:T(8,128)(2,1)S(1)}, bf16[256,4096]{1,0:T(8,128)(2,1)}, u32[]{:S(2)}) copy-start(bf16[256,4096]{1,0:T(8,128)(2,1)} %x_ref.3) | copy-start | bytes 6291460
  23.1 5.0 %copy-start.8 = (bf16[256,4096]{1,0:T(8,128)(2,1)}, bf16[256,4096]{1,0:T(8,128)(2,1)S(1)}, u32[]{:S(2)}) copy-start(bf16[256,4096]{1,0:T(8,128)(2,1)S(1)} %get-tuple-element.19.own_ref) | copy-start | bytes 6291460
  26.1 7.5 %collective-permute-start.13 = (bf16[1,16,4096]{2,1,0:T(8,128)(2,1)}, bf16[1,16,4096]{2,1,0:T(8,128)(2,1)}, u32[]{:S(2)}, u32[]{:S(2)}) collective-permute-start(bf16[1,16,4096]{2,1,0:T(8,128)(2,1)} %bitcast.33), channel_id=1, source_target_pairs={{0,4},{1,5},{2,6},{3,7},{4,0},{5,1},{6,2},{7,3},{8,12},{9,13},{10,... | collective-permute-start | bytes 393224 | tf_op jit(solution)/shard_map/ppermute | solution.py:163
  26.6 19.4 %collective-permute-start = (bf16[256,512]{1,0:T(8,128)(2,1)}, bf16[256,512]{1,0:T(8,128)(2,1)S(1)}, u32[]{:S(2)}, u32[]{:S(2)}) collective-permute-start(bf16[256,512]{1,0:T(8,128)(2,1)} %get-tuple-element.22), channel_id=1, source_target_pairs={{0,16},{16,0},{1,17},{17,1},{2,18},{18,2},{3,19},{19,3},{4,20},{20... | collective-permute-start | bytes 786440 | tf_op jit(solution)/shard_map/ppermute | solution.py:166
  28.2 15.2 %copy-start.3 = (bf16[256,512]{1,0:T(8,128)(2,1)S(1)}, bf16[256,512]{1,0:T(8,128)(2,1)}, u32[]{:S(2)}) copy-start(bf16[256,512]{1,0:T(8,128)(2,1)} %cot_ref.1) | copy-start | bytes 786436
  28.2 1.4 %collective-permute-start.20 = (bf16[4,32,512]{2,1,0:T(8,128)(2,1)S(1)}, bf16[4,32,512]{2,1,0:T(8,128)(2,1)S(1)}, u32[]{:S(2)}, u32[]{:S(2)}) collective-permute-start(bf16[4,32,512]{2,1,0:T(8,128)(2,1)S(1)} %get-tuple-element.41), channel_id=1, source_target_pairs={{0,1},{1,0},{2,3},{3,2},{4,5},{5,4},{6,7},{7,6},{8,9},{9,8},{10,11... | collective-permute-start | bytes 393224 | tf_op jit(solution)/shard_map/ppermute | solution.py:163
  29.6 16.4 %collective-permute-start.3 = (bf16[256,512]{1,0:T(8,128)(2,1)}, bf16[256,512]{1,0:T(8,128)(2,1)S(1)}, u32[]{:S(2)}, u32[]{:S(2)}) collective-permute-start(bf16[256,512]{1,0:T(8,128)(2,1)} %get-tuple-element.21), channel_id=1, source_target_pairs={{0,16},{16,0},{1,17},{17,1},{2,18},{18,2},{3,19},{19,3},{4,20},{20... | collective-permute-start | bytes 786440 | tf_op jit(solution)/shard_map/ppermute | solution.py:166
  30.1 14.9 %copy-start.18 = (s32[2]{0:T(128)S(1)}, s32[2]{0:T(128)}, u32[]{:S(2)}) copy-start(s32[2]{0:T(128)} %param.14) | copy-start | bytes 28
  30.1 15.2 %copy-start.19 = (s32[16]{0:T(128)S(1)}, s32[16]{0:T(128)}, u32[]{:S(2)}) copy-start(s32[16]{0:T(128)} %param.15) | copy-start | bytes 196
  30.1 22.1 %copy-start.1 = (bf16[256,4096]{1,0:T(8,128)(2,1)S(1)}, bf16[256,4096]{1,0:T(8,128)(2,1)}, u32[]{:S(2)}) copy-start(bf16[256,4096]{1,0:T(8,128)(2,1)} %x_ref.3) | copy-start | bytes 6291460
  30.8 16.8 %collective-permute-start.6 = (bf16[256,512]{1,0:T(8,128)(2,1)}, bf16[256,512]{1,0:T(8,128)(2,1)S(1)}, u32[]{:S(2)}, u32[]{:S(2)}) collective-permute-start(bf16[256,512]{1,0:T(8,128)(2,1)} %get-tuple-element.23), channel_id=1, source_target_pairs={{0,16},{16,0},{1,17},{17,1},{2,18},{18,2},{3,19},{19,3},{4,20},{20... | collective-permute-start | bytes 786440 | tf_op jit(solution)/shard_map/ppermute | solution.py:166
  33.0 20.5 %collective-permute-start.9 = (bf16[256,512]{1,0:T(8,128)(2,1)}, bf16[256,512]{1,0:T(8,128)(2,1)S(1)}, u32[]{:S(2)}, u32[]{:S(2)}) collective-permute-start(bf16[256,512]{1,0:T(8,128)(2,1)} %get-tuple-element.20), channel_id=1, source_target_pairs={{0,16},{16,0},{1,17},{17,1},{2,18},{18,2},{3,19},{19,3},{4,20},{20... | collective-permute-start | bytes 786440 | tf_op jit(solution)/shard_map/ppermute | solution.py:166
  33.5 7.5 %collective-permute-start.21 = (bf16[2,4,32,512]{3,2,1,0:T(8,128)(2,1)S(1)}, bf16[2,4,32,512]{3,2,1,0:T(8,128)(2,1)S(1)}, u32[]{:S(2)}, u32[]{:S(2)}) collective-permute-start(bf16[2,4,32,512]{3,2,1,0:T(8,128)(2,1)S(1)} %get-tuple-element.39), channel_id=1, source_target_pairs={{0,2},{1,3},{2,0},{3,1},{4,6},{5,7},{6,4},{7,5},{8,10},{9,11},{10,... | collective-permute-start | bytes 786440 | tf_op jit(solution)/shard_map/ppermute | solution.py:163
  43.5 7.2 %collective-permute-start.24 = (f32[2,128,16]{1,2,0:T(8,128)S(1)}, f32[2,128,16]{1,2,0:T(8,128)S(1)}, u32[]{:S(2)}, u32[]{:S(2)}) collective-permute-start(f32[2,128,16]{1,2,0:T(8,128)S(1)} %convolution_bitcast_fusion), channel_id=1, source_target_pairs={{0,16},{16,0},{1,17},{17,1},{2,18},{18,2},{3,19},{19,3},{4,20},{20... | collective-permute-start | bytes 49160 | tf_op jit(solution)/shard_map/ppermute | solution.py:166
  46.0 19.1 %collective-permute-start.16 = (bf16[4,1,16,4096]{3,2,1,0:T(8,128)(2,1)}, bf16[4,1,16,4096]{3,2,1,0:T(8,128)(2,1)}, u32[]{:S(2)}, u32[]{:S(2)}) collective-permute-start(bf16[4,1,16,4096]{3,2,1,0:T(8,128)(2,1)} %get-tuple-element.37), channel_id=1, source_target_pairs={{0,1},{1,0},{2,3},{3,2},{4,5},{5,4},{6,7},{7,6},{8,9},{9,8},{10,11... | collective-permute-start | bytes 1572872 | tf_op jit(solution)/shard_map/ppermute | solution.py:163
  46.0 9.3 %collective-permute-start.1 = (bf16[256,512]{1,0:T(8,128)(2,1)S(1)}, bf16[256,512]{1,0:T(8,128)(2,1)}, u32[]{:S(2)}, u32[]{:S(2)}) collective-permute-start(bf16[256,512]{1,0:T(8,128)(2,1)S(1)} %collective-permute-done.refs_0_.refs_1_), channel_id=1, source_target_pairs={{0,2},{1,3},{2,0},{3,1},{4,6},{5,7},{6,4},{7,5},{8,10},{9,11},{10,... | collective-permute-start | bytes 786440 | tf_op jit(solution)/shard_map/ppermute | solution.py:163
  47.6 11.0 %collective-permute-start.4 = (bf16[256,512]{1,0:T(8,128)(2,1)S(1)}, bf16[256,512]{1,0:T(8,128)(2,1)}, u32[]{:S(2)}, u32[]{:S(2)}) collective-permute-start(bf16[256,512]{1,0:T(8,128)(2,1)S(1)} %collective-permute-done.3.refs_4_.refs_5_), channel_id=1, source_target_pairs={{0,4},{1,5},{2,6},{3,7},{4,0},{5,1},{6,2},{7,3},{8,12},{9,13},{10,... | collective-permute-start | bytes 786440 | tf_op jit(solution)/shard_map/ppermute | solution.py:163
  50.7 11.3 %collective-permute-start.7 = (bf16[256,512]{1,0:T(8,128)(2,1)S(1)}, bf16[256,512]{1,0:T(8,128)(2,1)}, u32[]{:S(2)}, u32[]{:S(2)}) collective-permute-start(bf16[256,512]{1,0:T(8,128)(2,1)S(1)} %collective-permute-done.6.refs_8_.refs_9_), channel_id=1, source_target_pairs={{0,2},{1,3},{2,0},{3,1},{4,6},{5,7},{6,4},{7,5},{8,10},{9,11},{10,... | collective-permute-start | bytes 786440 | tf_op jit(solution)/shard_map/ppermute | solution.py:163
  53.5 11.7 %copy-start.4 = (bf16[256,512]{1,0:T(8,128)(2,1)}, bf16[256,512]{1,0:T(8,128)(2,1)S(1)}, u32[]{:S(2)}) copy-start(bf16[256,512]{1,0:T(8,128)(2,1)S(1)} %collective-permute-done.9.refs_12_.refs_13_) | copy-start | bytes 786436
  53.5 46.5 %collective-permute-start.25 = (bf16[256,512]{1,0:T(8,128)(2,1)S(1)}, bf16[256,512]{1,0:T(8,128)(2,1)}, u32[]{:S(2)}, u32[]{:S(2)}) collective-permute-start(bf16[256,512]{1,0:T(8,128)(2,1)S(1)} %copy-done.3), channel_id=1, source_target_pairs={{0,16},{16,0},{1,17},{17,1},{2,18},{18,2},{3,19},{19,3},{4,20},{20... | collective-permute-start | bytes 786440 | tf_op jit(solution)/shard_map/ppermute | solution.py:166
  55.3 8.5 %collective-permute-start.10 = (bf16[256,512]{1,0:T(8,128)(2,1)S(1)}, bf16[256,512]{1,0:T(8,128)(2,1)S(1)}, u32[]{:S(2)}, u32[]{:S(2)}) collective-permute-start(bf16[256,512]{1,0:T(8,128)(2,1)S(1)} %collective-permute-done.9.refs_12_.refs_13_), channel_id=1, source_target_pairs={{0,4},{1,5},{2,6},{3,7},{4,0},{5,1},{6,2},{7,3},{8,12},{9,13},{10,... | collective-permute-start | bytes 786440 | tf_op jit(solution)/shard_map/ppermute | solution.py:163
  56.8 8.5 %copy-start.14 = (bf16[1,4,1,16,4096]{4,3,1,2,0:T(8,128)(2,1)S(1)}, bf16[1,4,1,16,4096]{4,3,1,2,0:T(8,128)(2,1)}, u32[]{:S(2)}) copy-start(bf16[1,4,1,16,4096]{4,3,1,2,0:T(8,128)(2,1)} %get-tuple-element.36) | copy-start | bytes 1572868
  58.6 13.0 %collective-permute-start.26 = (bf16[2,16,4096]{2,1,0:T(8,128)(2,1)}, bf16[2,16,4096]{2,1,0:T(8,128)(2,1)}, u32[]{:S(2)}, u32[]{:S(2)}) collective-permute-start(bf16[2,16,4096]{2,1,0:T(8,128)(2,1)} %convolution_convert_fusion), channel_id=1, source_target_pairs={{0,2},{1,3},{2,0},{3,1},{4,6},{5,7},{6,4},{7,5},{8,10},{9,11},{10,... | collective-permute-start | bytes 786440 | tf_op jit(solution)/shard_map/ppermute | solution.py:163
  62.0 29.5 %collective-permute-start.2 = (bf16[2,256,512]{2,1,0:T(8,128)(2,1)}, bf16[2,256,512]{2,1,0:T(8,128)(2,1)}, u32[]{:S(2)}, u32[]{:S(2)}) collective-permute-start(bf16[2,256,512]{2,1,0:T(8,128)(2,1)} %pad_maximum_fusion.1), channel_id=1, source_target_pairs={{0,1},{1,0},{2,3},{3,2},{4,5},{5,4},{6,7},{7,6},{8,9},{9,8},{10,11... | collective-permute-start | bytes 1572872 | tf_op jit(solution)/shard_map/ppermute | solution.py:163
  63.8 1.4 %copy-start.6 = (bf16[256,512]{1,0:T(8,128)(2,1)}, bf16[256,512]{1,0:T(8,128)(2,1)S(1)}, u32[]{:S(2)}) copy-start(bf16[256,512]{1,0:T(8,128)(2,1)S(1)} %collective-permute-done.10.refs_13_.refs_14_) | copy-start | bytes 786436
  63.8 29.2 %collective-permute-start.5 = (bf16[2,256,512]{2,1,0:T(8,128)(2,1)}, bf16[2,256,512]{2,1,0:T(8,128)(2,1)}, u32[]{:S(2)}, u32[]{:S(2)}) collective-permute-start(bf16[2,256,512]{2,1,0:T(8,128)(2,1)} %pad_maximum_fusion.2), channel_id=1, source_target_pairs={{0,1},{1,0},{2,3},{3,2},{4,5},{5,4},{6,7},{7,6},{8,9},{9,8},{10,11... | collective-permute-start | bytes 1572872 | tf_op jit(solution)/shard_map/ppermute | solution.py:163
  65.2 28.9 %collective-permute-start.8 = (bf16[2,256,512]{2,1,0:T(8,128)(2,1)}, bf16[2,256,512]{2,1,0:T(8,128)(2,1)}, u32[]{:S(2)}, u32[]{:S(2)}) collective-permute-start(bf16[2,256,512]{2,1,0:T(8,128)(2,1)} %pad_maximum_fusion.3), channel_id=1, source_target_pairs={{0,1},{1,0},{2,3},{3,2},{4,5},{5,4},{6,7},{7,6},{8,9},{9,8},{10,11... | collective-permute-start | bytes 1572872 | tf_op jit(solution)/shard_map/ppermute | solution.py:163
  71.7 8.8 %copy-start.15 = (bf16[2,16,4096]{2,1,0:T(8,128)(2,1)S(1)}, bf16[2,16,4096]{2,1,0:T(8,128)(2,1)}, u32[]{:S(2)}) copy-start(bf16[2,16,4096]{2,1,0:T(8,128)(2,1)} %gather_fusion) | copy-start | bytes 786436
  71.7 8.7 %collective-permute-start.22 = (bf16[2,16,4096]{2,1,0:T(8,128)(2,1)S(1)}, bf16[2,16,4096]{2,1,0:T(8,128)(2,1)S(1)}, u32[]{:S(2)}, u32[]{:S(2)}) collective-permute-start(bf16[2,16,4096]{2,1,0:T(8,128)(2,1)S(1)} %gather_fusion.1), channel_id=1, source_target_pairs={{0,2},{1,3},{2,0},{3,1},{4,6},{5,7},{6,4},{7,5},{8,10},{9,11},{10,... | collective-permute-start | bytes 786440 | tf_op jit(solution)/shard_map/ppermute | solution.py:163
  74.1 8.5 %copy-start.11 = (f32[8,16,4096]{2,1,0:T(8,128)}, f32[8,16,4096]{2,1,0:T(8,128)S(1)}, u32[]{:S(2)}) copy-start(f32[8,16,4096]{2,1,0:T(8,128)S(1)} %multiply_reduce_fusion) | copy-start | bytes 6291460
  81.2 3.8 %collective-permute-start.23 = (f32[2,128,16]{1,2,0:T(8,128)S(1)}, f32[2,128,16]{1,2,0:T(8,128)S(1)}, u32[]{:S(2)}, u32[]{:S(2)}) collective-permute-start(f32[2,128,16]{1,2,0:T(8,128)S(1)} %convolution_bitcast_fusion.1), channel_id=1, source_target_pairs={{0,16},{16,0},{1,17},{17,1},{2,18},{18,2},{3,19},{19,3},{4,20},{20... | collective-permute-start | bytes 49160 | tf_op jit(solution)/shard_map/ppermute | solution.py:166
  84.9 10.2 %collective-permute-start.11 = (bf16[2,256,512]{2,1,0:T(8,128)(2,1)}, bf16[2,256,512]{2,1,0:T(8,128)(2,1)}, u32[]{:S(2)}, u32[]{:S(2)}) collective-permute-start(bf16[2,256,512]{2,1,0:T(8,128)(2,1)} %pad_maximum_fusion.4), channel_id=1, source_target_pairs={{0,1},{1,0},{2,3},{3,2},{4,5},{5,4},{6,7},{7,6},{8,9},{9,8},{10,11... | collective-permute-start | bytes 1572872 | tf_op jit(solution)/shard_map/ppermute | solution.py:163
  87.1 35.1 %all-to-all-start = ((bf16[16,16,512]{2,1,0:T(8,128)(2,1)}), bf16[16,16,512]{2,1,0:T(8,128)(2,1)}, u32[]{:S(2)}, u32[]{:S(2)}) async-start(bf16[16,16,512]{2,1,0:T(8,128)(2,1)} %multiply_reduce_fusion.1), calls=%async_computation | async-start | bytes 524288 | tf_op jit(solution)/shard_map/all_to_all | solution.py:281
  91.5 4.8 %copy-start.5 = (bf16[256,512]{1,0:T(8,128)(2,1)S(1)}, bf16[256,512]{1,0:T(8,128)(2,1)}, u32[]{:S(2)}) copy-start(bf16[256,512]{1,0:T(8,128)(2,1)} %copy-done.4) | copy-start | bytes 786436
  91.5 4.8 %copy-start.7 = (bf16[256,512]{1,0:T(8,128)(2,1)S(1)}, bf16[256,512]{1,0:T(8,128)(2,1)}, u32[]{:S(2)}) copy-start(bf16[256,512]{1,0:T(8,128)(2,1)} %copy-done.6) | copy-start | bytes 786436
  91.5 14.0 %collective-permute-start.27 = (bf16[4,1,16,4096]{3,2,0,1:T(8,128)(2,1)}, bf16[4,1,16,4096]{3,2,0,1:T(8,128)(2,1)S(1)}, u32[]{:S(2)}, u32[]{:S(2)}) collective-permute-start(bf16[4,1,16,4096]{3,2,0,1:T(8,128)(2,1)} %fusion.3), channel_id=1, source_target_pairs={{0,1},{1,0},{2,3},{3,2},{4,5},{5,4},{6,7},{7,6},{8,9},{9,8},{10,11... | collective-permute-start | bytes 1572872 | tf_op jit(solution)/shard_map/ppermute | solution.py:163
  99.4 10.8 %collective-permute-start.12 = (bf16[256,512]{1,0:T(8,128)(2,1)S(1)}, bf16[256,512]{1,0:T(8,128)(2,1)S(1)}, u32[]{:S(2)}, u32[]{:S(2)}) collective-permute-start(bf16[256,512]{1,0:T(8,128)(2,1)S(1)} %shard_map.103), channel_id=1, source_target_pairs={{0,16},{16,0},{1,17},{17,1},{2,18},{18,2},{3,19},{19,3},{4,20},{20... | collective-permute-start | bytes 786440 | tf_op jit(solution)/shard_map/ppermute | solution.py:166
  100.0 5.5 %copy-start.12 = (f32[8,16,4096]{2,1,0:T(8,128)S(1)}, f32[8,16,4096]{2,1,0:T(8,128)}, u32[]{:S(2)}) copy-start(f32[8,16,4096]{2,1,0:T(8,128)} %copy-done.11) | copy-start | bytes 6291460
  105.5 4.7 %copy-start.10 = (f32[256,512]{1,0:T(8,128)S(1)}, f32[256,512]{1,0:T(8,128)}, u32[]{:S(2)}) copy-start(f32[256,512]{1,0:T(8,128)} %copy-done.9) | copy-start | bytes 1572868
  105.5 4.7 %copy-start.13 = (f32[2,128,512]{2,1,0:T(8,128)S(1)}, f32[2,128,512]{2,1,0:T(8,128)}, u32[]{:S(2)}) copy-start(f32[2,128,512]{2,1,0:T(8,128)} %convolution_multiply_fusion) | copy-start | bytes 1572868
  105.7 8.3 %collective-permute-start.30 = (bf16[1,16,4096]{2,1,0:T(8,128)(2,1)S(1)}, bf16[1,16,4096]{2,1,0:T(8,128)(2,1)S(1)}, u32[]{:S(2)}, u32[]{:S(2)}) collective-permute-start(bf16[1,16,4096]{2,1,0:T(8,128)(2,1)S(1)} %slice_bitcast_fusion.10), channel_id=1, source_target_pairs={{0,12},{1,13},{2,14},{3,15},{4,8},{5,9},{6,10},{7,11},{8,4},{9,5},... | collective-permute-start | bytes 393224 | tf_op jit(solution)/shard_map/ppermute | solution.py:163
  109.3 11.5 %collective-permute-start.29 = (bf16[1,16,4096]{2,1,0:T(8,128)(2,1)S(1)}, bf16[1,16,4096]{2,1,0:T(8,128)(2,1)S(1)}, u32[]{:S(2)}, u32[]{:S(2)}) collective-permute-start(bf16[1,16,4096]{2,1,0:T(8,128)(2,1)S(1)} %get-tuple-element.27), channel_id=1, source_target_pairs={{0,8},{1,9},{2,10},{3,11},{4,12},{5,13},{6,14},{7,15},{8,0},{9,1},... | collective-permute-start | bytes 393224 | tf_op jit(solution)/shard_map/ppermute | solution.py:163
  109.3 11.5 %collective-permute-start.28 = (bf16[1,16,4096]{2,1,0:T(8,128)(2,1)S(1)}, bf16[1,16,4096]{2,1,0:T(8,128)(2,1)S(1)}, u32[]{:S(2)}, u32[]{:S(2)}) collective-permute-start(bf16[1,16,4096]{2,1,0:T(8,128)(2,1)S(1)} %get-tuple-element.26), channel_id=1, source_target_pairs={{0,4},{1,5},{2,6},{3,7},{4,0},{5,1},{6,2},{7,3},{8,12},{9,13},{10,... | collective-permute-start | bytes 393224 | tf_op jit(solution)/shard_map/ppermute | solution.py:163
  (4 other events, 3.1 us)

commit v2 on v0

v2 whole, which is shorter than its diff:
```python
import functools

import jax
import jax.numpy as jnp
from jax import lax
from jax.experimental import pallas as pl
from jax.experimental.pallas import tpu as pltpu
from jax.sharding import PartitionSpec as P

RANK = 16
BLOCK = 128
PIECES = 2
HOPPING = 2
HALVES = 2
COUNT = 128
VMEM_LIMIT = 20 * 1024 * 1024

adapter_scale = 2.0

NT = (((1,), (1,)), ((), ()))
TN = (((0,), (0,)), ((), ()))

f32, bf16 = jnp.float32, jnp.bfloat16


def dot(a, b):
    return jnp.dot(a, b, preferred_element_type=f32)


def dot_nt(a, b):
    return lax.dot_general(a, b, NT, preferred_element_type=f32)


def dot_tn(a, b):
    return lax.dot_general(a, b, TN, preferred_element_type=f32)


SMEM = pl.BlockSpec(memory_space=pltpu.SMEM)
VMEM = pl.BlockSpec(memory_space=pltpu.VMEM)
HBM = pl.BlockSpec(memory_space=pltpu.HBM)


def call(kernel, in_specs, out_shape, out_specs, args, scratch=(), flops=0, moved=1 << 20, limit=VMEM_LIMIT, **settings):
    return pl.pallas_call(
        functools.partial(kernel, **settings),
        in_specs=in_specs,
        out_specs=out_specs,
        out_shape=out_shape,
        scratch_shapes=list(scratch),
        compiler_params=pltpu.CompilerParams(vmem_limit_bytes=limit),
        cost_estimate=pl.CostEstimate(flops=0, bytes_accessed=0, transcendentals=0),
    )(*args)


def like(shape, dtype):
    return jax.ShapeDtypeStruct(shape, dtype)


def message_kernel(down, up, message, sem):
    features = down.shape[2]
    copies = [
        pltpu.make_async_copy(down, message.at[:, :, pl.ds(0, features)], sem.at[0]),
        pltpu.make_async_copy(up, message.at[:, :, pl.ds(features, up.shape[2])], sem.at[1]),
    ]
    for copy in copies:
        copy.start()
    for copy in copies:
        copy.wait()


def weights_kernel(w, *refs, features, chunk, pieces, n_tensor):
    sent, sem = refs[:-1], refs[-1]
    t, me = lax.axis_index("tensor"), lax.axis_index("dp")
    copies = []
    for k, out in enumerate(sent):
        s, p = k // pieces + 1, k % pieces
        start = lax.rem(t + s, n_tensor) * features + first_row(me, p, 0, chunk)
        copies.append(pltpu.make_async_copy(w.at[pl.ds(pl.multiple_of(start, chunk), out.shape[0])], out, sem.at[k]))
    for copy in copies:
        copy.start()
    for copy in copies:
        copy.wait()


def first_row(me, p, q, chunk):
    if p < HOPPING:
        part = (((me >> 2) & 1) * 2 + (me & 1)) ^ q
    else:
        part = ((me & 1) ^ q) * 2
    return (p * 4 + part) * chunk


def part_offset(me, k, chunk):
    p, q = (k // 4, (0, 2, 1, 3)[k % 4]) if k < 4 * HOPPING else (HOPPING + (k - 4 * HOPPING) // 2, k % 2)
    return pl.multiple_of(first_row(me, p, q, chunk), chunk)


def near(who, me, upper, owned):
    relative = (who // owned) ^ me
    return ((relative & 1) * upper + (relative >> 2)) * owned + lax.rem(who, owned)


def on_my_side(who, me, owned):
    return (((who // owned) ^ me) & 2) == 0


def select_kernel(here, tenant, partner, *refs, upper, owned):
    held, (mine, partners) = refs[:-2], refs[-2:]
    me = here[1]
    for b in range(tenant.shape[0]):
        for who, out in ((partner[b], partners), (tenant[b], mine)):
            at = near(who, me, upper, owned)
            for k, group in enumerate(held):
                for o in range(owned):

                    @pl.when(at == k * owned + o)
                    def _(group=group, o=o, out=out, b=b):
                        out[b] = group[o]


def low_kernel(here, tenant, x, cot, mine, theirs, blocks, part, *, owned):
    me, features = here[1], x.shape[1]
    nblocks = tenant.shape[0]
    for b in range(nblocks):
        mine_here = on_my_side(tenant[b], me, owned)

        @pl.when(mine_here)
        def _(b=b):
            blocks[b] = mine[b]

        @pl.when(jnp.logical_not(mine_here))
        def _(b=b):
            blocks[b] = theirs[b]

        rows = slice(b * BLOCK, (b + 1) * BLOCK)
        part[b] = dot_nt(blocks[b, :, :features], x[rows, :])
        part[nblocks + b] = dot_nt(blocks[b, :, features:], cot[rows, :])


def gradient_kernel(x, cot, *refs):
    parts, (low, grad_low, out) = refs[:-3], refs[-3:]
    nblocks, features, values = low.shape[0], x.shape[1], cot.shape[1]
    for b in range(nblocks):
        low_sum, grad_sum = parts[0][b], parts[0][nblocks + b]
        for part in parts[1:]:
            low_sum, grad_sum = low_sum + part[b], grad_sum + part[nblocks + b]
        rows = slice(b * BLOCK, (b + 1) * BLOCK)
        low[b] = low_sum.astype(bf16)
        grad_low[b] = (adapter_scale * grad_sum).astype(bf16)
        out[b, :, :features] = dot(grad_low[b], x[rows, :]).astype(bf16)
        out[b, :, features : features + values] = (adapter_scale * dot(low[b], cot[rows, :])).astype(bf16)
        out[b, :, features + values :] = jnp.ones((RANK, COUNT), bf16)


def spread_kernel(here, tenant, partner, mine, theirs, keep, send, acc, *, upper, owned):
    me = here[1]
    acc[...] = jnp.zeros_like(acc)
    for b in range(tenant.shape[0]):
        for who, source in ((tenant[b], mine), (partner[b], theirs)):

            @pl.when(on_my_side(who, me, owned))
            def _(who=who, source=source, b=b):
                at = near(who, me, upper, owned)
                acc[at] = acc[at] + source[b].astype(f32)

    half = upper * owned
    keep[...] = acc[:half]
    send[...] = acc[half:].astype(bf16)


def cross_kernel(keep, received, first, *rest, owned):
    for o in range(owned):
        first[o] = keep[o] + received[o].astype(f32)
    for m, out in enumerate(rest, 1):
        for o in range(owned):
            out[o] = (keep[m * owned + o] + received[m * owned + o].astype(f32)).astype(bf16)


def final_kernel(here, quotas, first, *refs, owned):
    others, (down_grad, up_grad) = refs[:-2], refs[-2:]
    features, values = down_grad.shape[2], up_grad.shape[2]
    for o in range(owned):
        total = first[o]
        for other in others:
            total = total + other[o].astype(f32)
        rows = jnp.maximum(total[:, features + values : features + values + 1] * BLOCK, 1.0)
        scale = jnp.full(rows.shape, quotas[here[1] * owned + o]).astype(f32) / rows
        down_grad[o] = total[:, :features] * scale
        up_grad[o] = total[:, features : features + values] * scale


def own_values_kernel(here, x_ref, w_ref, out_ref):
    @pl.when(pl.program_id(0) == 0)
    def _():
        out_ref[...] = jnp.zeros_like(out_ref)

    out_ref[...] += dot(x_ref[...], w_ref[...])


def own_gradient_kernel(here, cot_ref, w_ref, out_ref):
    out_ref[...] = dot_nt(cot_ref[...], w_ref[...]).astype(out_ref.dtype)


def own_columns(kernel, here, a, a_spec, w, out_shape, out_spec, features, chunk):
    steps = features // chunk
    return pl.pallas_call(
        kernel,
        grid_spec=pltpu.PrefetchScalarGridSpec(
            num_scalar_prefetch=1,
            grid=(steps,),
            in_specs=[a_spec, pl.BlockSpec((chunk, w.shape[1]), lambda j, here: (here[0] * steps + j, 0))],
            out_specs=out_spec,
        ),
        out_shape=out_shape,
        compiler_params=pltpu.CompilerParams(vmem_limit_bytes=57 * 1024 * 1024),
        cost_estimate=pl.CostEstimate(flops=0, bytes_accessed=0, transcendentals=0),
    )(here, a, w)


def other_values_kernel(here, x, *refs, chunk):
    w_refs, outs = refs[:-HALVES], refs[-HALVES:]
    total = None
    for k, w in enumerate(w_refs):
        term = dot(x[:, pl.ds(part_offset(here[1], k, chunk), w.shape[0])], w[...])
        total = term if total is None else total + term
    width = outs[0].shape[1]
    for i, out in enumerate(outs):
        out[...] = total[:, i * width : (i + 1) * width].astype(out.dtype)


def input_gradient_kernel(here, own, grad_low, blocks, *refs, groups, parts, chunk):
    cots, ws, out = refs[:groups], refs[groups:-1], refs[-1]
    for k in range(parts):
        span = pl.ds(part_offset(here[1], k, chunk), ws[k].shape[0])
        total = own[:, span].astype(f32)
        for group in range(groups):
            term = dot_nt(cots[group][...], ws[group * parts + k][...])
            total = total + term.astype(bf16).astype(f32)
        for b in range(grad_low.shape[0]):
            rows = slice(b * BLOCK, (b + 1) * BLOCK)
            out[rows, span] = (total[rows] + dot_tn(grad_low[b], blocks[b, :, span])).astype(out.dtype)


def values_kernel(own, low, blocks, *refs):
    received, out = refs[:-1], refs[-1]
    features = blocks.shape[2] - own.shape[1]
    for b in range(low.shape[0]):
        rows = slice(b * BLOCK, (b + 1) * BLOCK)
        total = own[rows] + adapter_scale * dot_tn(low[b], blocks[b, :, features:])
        for i in range(HALVES):
            width = received[i].shape[1]
            span = slice(i * width, (i + 1) * width)
            part = total[:, span]
            for other in received[i::HALVES]:
                part = part + other[rows].astype(f32)
            out[rows, span] = part.astype(out.dtype)


def after(a, *first):
    return lax.optimization_barrier((a, *first))[0]


def on_device(
    inputs,
    frozen_value_weight,
    adapter_down_matrix,
    adapter_up_matrix,
    value_cotangent,
    tenant_of_block,
    quotas,
):
    token_rows, features = inputs.shape
    values = frozen_value_weight.shape[1]
    nblocks = tenant_of_block.shape[0]
    owned = adapter_down_matrix.shape[0]
    n_dp, n_tensor = lax.axis_size("dp"), lax.axis_size("tensor")
    upper = n_dp // 4
    shifts = range(1, n_tensor)
    here = jnp.stack([lax.axis_index("tensor"), lax.axis_index("dp")]).astype(jnp.int32)
    tenant = tenant_of_block

    def flip(a, mask):
        return lax.ppermute(a, "dp", [(i, i ^ mask) for i in range(n_dp)])

    def turn(a, shift):
        return lax.ppermute(a, "tensor", [(i, (i + shift) % n_tensor) for i in range(n_tensor)])

    def turns(a):
        return [turn(a, s) for s in shifts]

    pieces = PIECES if features % (PIECES * 4 * 128) == 0 else 1
    chunk = features // (pieces * 4)
    n_sent = len(shifts) * pieces
    width = features + values
    message = call(
        message_kernel,
        [HBM, HBM],
        like((owned, RANK, width), bf16),
        VMEM,
        (jnp.swapaxes(adapter_down_matrix, 1, 2), adapter_up_matrix),
        scratch=[pltpu.SemaphoreType.DMA((2,))],
        limit=52 * 1024 * 1024,
    )
    sent = call(
        weights_kernel,
        [HBM],
        [like((chunk * (1 if k % pieces < HOPPING else 2), values), bf16) for k in range(n_sent)],
        [VMEM] * n_sent,
        (frozen_value_weight,),
        scratch=[pltpu.SemaphoreType.DMA((n_sent,))],
        limit=52 * 1024 * 1024,
        features=features,
        chunk=chunk,
        pieces=pieces,
        n_tensor=n_tensor,
    )
    adapters = [message] + [flip(message, 4 * m) for m in range(1, upper)]
    first_w = [turn(sent[k], k // pieces + 1) for k in range(n_sent)]
    partner = flip(after(tenant, message), 2)

    def hopping(arrays):
        return [a for k, a in enumerate(arrays) if k % pieces < HOPPING]

    def of_piece(p):
        return [k for k in range(n_sent) if k % pieces == p]

    own_chunk = min(1024, features)
    rows_by_chunk = pl.BlockSpec((token_rows, own_chunk), lambda j, here: (0, j))
    rows_by_values = pl.BlockSpec((token_rows, values), lambda j, here: (0, 0))

    def own(kernel, at, a, a_spec, out_shape, out_spec):
        return own_columns(kernel, at, a, a_spec, frozen_value_weight, out_shape, out_spec, features, own_chunk)

    value_own = own(
        own_values_kernel,
        after(here, partner),
        inputs,
        rows_by_chunk,
        like((token_rows, values), f32),
        rows_by_values,
    )

    held = adapters + [flip(after(a, value_own), 1) for a in adapters]
    mine, partners = call(
        select_kernel,
        [SMEM, SMEM, SMEM] + [VMEM] * len(held),
        [like((nblocks, RANK, width), bf16)] * 2,
        [VMEM, VMEM],
        (here, tenant, after(partner, *[first_w[k] for k in of_piece(0)]), *held),
        upper=upper,
        owned=owned,
    )
    def hop(p, *first):
        return {k: flip(after(first_w[k], *first), 4) for k in of_piece(p) if p < HOPPING}

    hops = hop(0, partners)
    blocks, part = call(
        low_kernel,
        [SMEM, SMEM, VMEM, VMEM, VMEM, VMEM],
        [like((nblocks, RANK, width), bf16), like((2 * nblocks, RANK, BLOCK), f32)],
        [VMEM, VMEM],
        (here, tenant, inputs, value_cotangent, mine, flip(partners, 2)),
        owned=owned,
    )
    parts = [part] + turns(part)
    for p in range(1, pieces):
        hops.update(hop(p, part))
    low, grad_low, gradients = call(
        gradient_kernel,
        [VMEM] * (2 + len(parts)),
        [like((nblocks, RANK, BLOCK), bf16)] * 2 + [like((nblocks, RANK, width + COUNT), bf16)],
        [VMEM] * 3,
        (inputs, after(value_cotangent, *[hops[k] for k in of_piece(0)]), *parts),
    )

    cots = turns(after(value_cotangent, gradients))

    gradient_own = own(
        own_gradient_kernel,
        after(here, gradients),
        value_cotangent,
        rows_by_values,
        like((token_rows, features), bf16),
        rows_by_chunk,
    )

    keep, crossing = call(
        spread_kernel,
        [SMEM, SMEM, SMEM, VMEM, VMEM],
        [like((upper * owned, RANK, width + COUNT), f32), like((upper * owned, RANK, width + COUNT), bf16)],
        [VMEM, VMEM],
        (here, tenant, after(partner, gradient_own, *cots), gradients, flip(gradients, 2)),
        scratch=[pltpu.VMEM((2 * upper * owned, RANK, width + COUNT), f32)],
        upper=upper,
        owned=owned,
    )

    summed, *to_owners = call(
        cross_kernel,
        [VMEM, VMEM],
        [like((owned, RANK, width + COUNT), f32)] + [like((owned, RANK, width + COUNT), bf16)] * (upper - 1),
        [VMEM] * upper,
        (keep, after(flip(crossing, 1), *[hops[k] for k in of_piece(1) if k in hops])),
        owned=owned,
    )
    owners = [flip(a, 4 * m) for m, a in enumerate(to_owners, 1)]

    w_groups = []
    for s in shifts:
        group = []
        for k in range((s - 1) * pieces, s * pieces):
            held_here = [first_w[k], hops[k]] if k in hops else [first_w[k]]
            group += held_here + [flip(after(a, gradients), 1) for a in held_here]
        w_groups.append(group)
    value_parts = []
    for s in shifts:
        value_part = call(
            other_values_kernel,
            [SMEM, VMEM] + [VMEM] * len(w_groups[s - 1]),
            [like((token_rows, values // HALVES), bf16)] * HALVES,
            [VMEM] * HALVES,
            (after(here, summed), inputs, *w_groups[s - 1]),
            flops=2 * token_rows * features * values,
            moved=2 * features * (token_rows + values),
            chunk=chunk,
        )
        value_parts += value_part

    flat = [w for group in w_groups for w in group]
    gradient_inputs = call(
        input_gradient_kernel,
        [SMEM] + [VMEM] * (3 + len(cots) + len(flat)),
        like((token_rows, features), bf16),
        VMEM,
        (after(here, *value_parts), gradient_own, grad_low, blocks, *cots, *flat),
        flops=2 * token_rows * features * values * len(cots),
        moved=2 * features * values * len(cots) + 4 * token_rows * features,
        groups=len(cots),
        parts=len(w_groups[0]),
        chunk=chunk,
    )
    returned = [turn(a, -(i // HALVES + 1)) for i, a in enumerate(value_parts)]
    adapted_values = call(
        values_kernel,
        [VMEM] * (3 + len(returned)),
        like((token_rows, values), bf16),
        VMEM,
        (value_own, low, blocks, *returned),
    )
    down_grad, gradient_up_matrix = call(
        final_kernel,
        [SMEM, SMEM] + [VMEM] * upper,
        [like((owned, RANK, features), f32), like((owned, RANK, values), f32)],
        [VMEM, VMEM],
        (here, after(quotas, adapted_values), summed, *owners),
        moved=1 << 26,
        owned=owned,
    )
    return (adapted_values, gradient_inputs, jnp.swapaxes(down_grad, 1, 2), gradient_up_matrix)


def solution(mesh):
    placed = (
        P("dp", "tensor"),
        P(None, "tensor"),
        P("dp", "tensor", None),
        P("dp", None, "tensor"),
        P("dp", "tensor"),
        P("dp"),
        P(),
    )
    return jax.shard_map(
        on_device,
        mesh=mesh,
        in_specs=placed,
        out_specs=(
            P("dp", "tensor"),
            P("dp", "tensor"),
            P("dp", "tensor", None),
            P("dp", None, "tensor"),
        ),
        check_vma=False,
    )
```

time: 180 us -> 69.2 us (0.38)
  waiting for transfers between devices: 81.6 us -> 16.2 us
  blocking collectives: 39.2 us -> 0 us
  Pallas kernels: 0 us -> 25.4 us
  matrix products: 22.8 us -> 0 us
  starting transfers between devices: 7.44 us -> 25.9 us
  between operations: 14.5 us -> 0.75 us
  local copies, waits for them, and re-layouts: 7.54 us -> 0.04 us
  other arithmetic: 6.53 us -> 0.58 us
    reduce_scatter x1 -> x0, waiting for transfers between devices: 42 us -> none  [on_device(): lax.psum_scatter(partial_value.astype(jnp.bfloat16), 'tensor', scatter_di...]
    all_gather x2 -> x0, waiting for transfers between devices: 28.1 us -> none  [the longest x1 24.4 us: on_device(): lax.all_gather(inputs, 'tensor', axis=1, tiled=True)]
    ppermute x0 -> x26, starting transfers between devices: none -> 25.9 us  [the longest x20 19.2 us: flip(): return lax.ppermute(a, 'dp', [(i, i ^ mask) for i in range(n_dp)])]
    pallas_call x0 -> x13, Pallas kernels: none -> 25.4 us  [the longest x11 13.8 us: call(): pl.pallas_call(functools.partial(kernel, **settings), in_specs=in_specs,...]
    all_gather x1 -> x0, blocking collectives: 24.1 us -> none  [on_device(): lax.all_gather(adapter_up_matrix, 'dp', axis=0, tiled=True)]
    dot_general x11 -> x0, matrix products: 22.8 us -> none  [the longest x1 7.73 us: on_device(): lax.dot_general(value_cotangent, frozen_value_weight, (((1,), (1,)), ((),...]
    ppermute x0 -> x26, waiting for transfers between devices: none -> 16.2 us  [the longest x20 11.3 us: flip(): return lax.ppermute(a, 'dp', [(i, i ^ mask) for i in range(n_dp)])]
    all_to_all x2 -> x0, waiting for transfers between devices: 10.1 us -> none  [the longest x1 5.29 us: on_device(): lax.all_to_all(dense_a.astype(jnp.bfloat16), 'dp', split_axis=0, concat_a...]
  transfers between devices with their start and end apart: 5 -> 26, of which waited for: 5 -> 9; matrix products, arithmetic and copies ran while one was open for 18% -> 1% of each run, Pallas kernels for 0% -> 33%
where the time goes in v2:
time: 69.2 us; the launch traced here: 68.9 us
  starting transfers between devices  25.9 us (37%)
  Pallas kernels  25.4 us (37%)
  waiting for transfers between devices  16.2 us (23%)
  between operations  0.75 us (1%)
    ppermute x20, starting transfers between devices, flip(): return lax.ppermute(a, 'dp', [(i, i ^ mask) for i in range(n_dp)])  19.2 us
    pallas_call x11, Pallas kernels, call(): pl.pallas_call(functools.partial(kernel, **settings), in_specs=in_specs,...  13.8 us
    pallas_call x2, Pallas kernels, own_columns(): pl.pallas_call(kernel, grid_spec=pltpu.PrefetchScalarGridSpec(num_scalar_...  11.6 us
    ppermute x20, waiting for transfers between devices, flip(): return lax.ppermute(a, 'dp', [(i, i ^ mask) for i in range(n_dp)])  11.3 us
    ppermute x6, starting transfers between devices, turn(): lax.ppermute(a, 'tensor', [(i, (i + shift) % n_tensor) for i in range(n_t...  6.7 us
    ppermute x6, waiting for transfers between devices, turn(): lax.ppermute(a, 'tensor', [(i, (i + shift) % n_tensor) for i in range(n_t...  4.85 us
  transfers between devices with their start and end apart: 26, of which 9 were waited for; matrix products, arithmetic and copies ran while one was open for 1% of the time, Pallas kernels for 33%

profile of v2, /device:TPU:0, one launch (start us, length us, event | category | flops | bytes accessed | tf_op | source)
XLA Modules:
  0.0 68.9 jit_solution(10006402428978341253)
XLA Ops:
  0.7 1.3 %shard_map.104 = (bf16[512,512]{1,0:T(8,128)(2,1)S(1)}, bf16[512,512]{1,0:T(8,128)(2,1)S(1)}) custom-call(bf16[8192,512]{1,0:T(8,128)(2,1)} %w_ref.3), custom_call_target="tpu_custom_call" | custom-call | tf_op jit(solution)/shard_map/pallas_call | solution.py:44
  1.9 3.0 %collective-permute-start.1 = (bf16[512,512]{1,0:T(8,128)(2,1)S(1)}, bf16[512,512]{1,0:T(8,128)(2,1)S(1)}, u32[]{:S(2)}, u32[]{:S(2)}) collective-permute-start(bf16[512,512]{1,0:T(8,128)(2,1)S(1)} %get-tuple-element.46), channel_id=1, source_target_pairs={{0,16},{16,0},{1,17},{17,1},{2,18},{18,2},{3,19},{19,3},{4,20},{20... | collective-permute-start | bytes 1572872 | tf_op jit(solution)/shard_map/ppermute | solution.py:286
  5.0 0.1 shard_map.102.refs_0_
  5.1 1.6 %collective-permute-start.2 = (bf16[1,16,4608]{2,1,0:T(8,128)(2,1)S(1)}, bf16[1,16,4608]{2,1,0:T(8,128)(2,1)S(1)}, u32[]{:S(2)}, u32[]{:S(2)}) collective-permute-start(bf16[1,16,4608]{2,1,0:T(8,128)(2,1)S(1)} %shard_map.102.refs_0_), channel_id=1, source_target_pairs={{0,4},{1,5},{2,6},{3,7},{4,0},{5,1},{6,2},{7,3},{8,12},{9,13},{10,... | collective-permute-start | bytes 442376 | tf_op jit(solution)/shard_map/ppermute | solution.py:283
  6.7 2.6 %collective-permute-start.3 = (bf16[1,16,4608]{2,1,0:T(8,128)(2,1)S(1)}, bf16[1,16,4608]{2,1,0:T(8,128)(2,1)S(1)}, u32[]{:S(2)}, u32[]{:S(2)}) collective-permute-start(bf16[1,16,4608]{2,1,0:T(8,128)(2,1)S(1)} %shard_map.102.refs_0_), channel_id=1, source_target_pairs={{0,8},{1,9},{2,10},{3,11},{4,12},{5,13},{6,14},{7,15},{8,0},{9,1},... | collective-permute-start | bytes 442376 | tf_op jit(solution)/shard_map/ppermute | solution.py:283
  9.3 0.2 collective-permute-start.4
  9.5 1.5 %collective-permute-start = (s32[2]{0:T(128)S(1)}, s32[2]{0:T(128)S(1)}, u32[]{:S(2)}, u32[]{:S(2)}) collective-permute-start(s32[2]{0:T(128)S(1)} %copy-done.8), channel_id=1, source_target_pairs={{0,2},{1,3},{2,0},{3,1},{4,6},{5,7},{6,4},{7,5},{8,10},{9,11},{10,... | collective-permute-start | bytes 32 | tf_op jit(solution)/shard_map/ppermute | solution.py:283
  11.1 0.6 pad_add_fusion.here
  11.6 1.4 %collective-permute-done.partner = s32[2]{0:T(128)S(1)} collective-permute-done((s32[2]{0:T(128)S(1)}, s32[2]{0:T(128)S(1)}, u32[]{:S(2)}, u32[]{:S(2)}) %collective-permute-start) | collective-permute-done | bytes 40 | tf_op jit(solution)/shard_map/ppermute | solution.py:283
  13.1 5.9 %shard_map.103.own = f32[256,512]{1,0:T(8,128)} custom-call(s32[2]{0:T(128)} %pad_add_fusion.here, bf16[256,4096]{1,0:T(8,128)(2,1)} %x.5, bf16[8192,512]{1,0:T(8,128)(2,1)} %w_ref.3), custom_call_target="tpu_custom_call" | custom-call | tf_op jit(solution)/shard_map/pallas_call | solution.py:206
  19.0 0.5 collective-permute-start.6
  19.5 1.1 %collective-permute-done.3.refs_2_ = bf16[1,16,4608]{2,1,0:T(8,128)(2,1)S(1)} collective-permute-done((bf16[1,16,4608]{2,1,0:T(8,128)(2,1)S(1)}, bf16[1,16,4608]{2,1,0:T(8,128)(2,1)S(1)}, u32[]{:S(2)}, u32[]{:S(2)}) %collective-permute-start.3) | collective-permute-done | bytes 147488 | tf_op jit(solution)/shard_map/ppermute | solution.py:283
  20.6 0.5 collective-permute-start.8
  21.1 0.5 collective-permute-start.15
  21.7 0.3 collective-permute-done.7.refs_6_
  22.0 0.2 collective-permute-done.8.refs_7_
  22.2 0.7 %shard_map.105 = (bf16[2,16,4608]{2,1,0:T(8,128)(2,1)S(1)}, bf16[2,16,4608]{2,1,0:T(8,128)(2,1)S(1)}) custom-call(s32[2]{0:T(128)S(1)} %copy-done.5, s32[2]{0:T(128)S(1)} %copy-done.8, s32[2]{0:T(128)S(1)} %collective-permute-done.partner, bf16[1,16,4608]{2,1,0:T(8,128)(2,1)S(1)} %shard_map.102.refs_0_, ...), custom_call_target="tpu_custom_call" | custom-call | tf_op jit(solution)/shard_map/pallas_call | solution.py:44
  22.9 2.0 %collective-permute-start.9 = (bf16[512,512]{1,0:T(8,128)(2,1)S(1)}, bf16[512,512]{1,0:T(8,128)(2,1)S(1)}, u32[]{:S(2)}, u32[]{:S(2)}) collective-permute-start(bf16[512,512]{1,0:T(8,128)(2,1)S(1)} %collective-permute-done.1.refs_0_.refs_1_), channel_id=1, source_target_pairs={{0,4},{1,5},{2,6},{3,7},{4,0},{5,1},{6,2},{7,3},{8,12},{9,13},{10,... | collective-permute-start | bytes 1572872 | tf_op jit(solution)/shard_map/ppermute | solution.py:283
  24.9 1.5 %collective-permute-start.10 = (bf16[2,16,4608]{2,1,0:T(8,128)(2,1)S(1)}, bf16[2,16,4608]{2,1,0:T(8,128)(2,1)S(1)}, u32[]{:S(2)}, u32[]{:S(2)}) collective-permute-start(bf16[2,16,4608]{2,1,0:T(8,128)(2,1)S(1)} %get-tuple-element.52), channel_id=1, source_target_pairs={{0,2},{1,3},{2,0},{3,1},{4,6},{5,7},{6,4},{7,5},{8,10},{9,11},{10,... | collective-permute-start | bytes 884744 | tf_op jit(solution)/shard_map/ppermute | solution.py:283
  26.4 7.3 %collective-permute-done.10.theirs = bf16[2,16,4608]{2,1,0:T(8,128)(2,1)S(1)} collective-permute-done((bf16[2,16,4608]{2,1,0:T(8,128)(2,1)S(1)}, bf16[2,16,4608]{2,1,0:T(8,128)(2,1)S(1)}, u32[]{:S(2)}, u32[]{:S(2)}) %collective-permute-start.10) | collective-permute-done | bytes 294944 | tf_op jit(solution)/shard_map/ppermute | solution.py:283
  33.7 1.8 %shard_map.106 = (bf16[2,16,4608]{2,1,0:T(8,128)(2,1)S(1)}, f32[4,16,128]{2,1,0:T(8,128)S(1)}) custom-call(s32[2]{0:T(128)S(1)} %copy-done.5, s32[2]{0:T(128)S(1)} %copy-done.8, bf16[256,4096]{1,0:T(8,128)(2,1)S(1)} %copy-done, bf16[256,512]{1,0:T(8,128)(2,1)S(1)} %copy-done.2, bf16[2,16,4608]{2,1,0:T(8,128)(2,1)S(1)} %get-tuple-element.55.mine, ...), custom_call_target="tpu_custom_call" | custom-call | tf_op jit(solution)/shard_map/pallas_call | solution.py:44
  35.6 1.5 %collective-permute-start.16 = (bf16[512,512]{1,0:T(8,128)(2,1)S(1)}, bf16[512,512]{1,0:T(8,128)(2,1)S(1)}, u32[]{:S(2)}, u32[]{:S(2)}) collective-permute-start(bf16[512,512]{1,0:T(8,128)(2,1)S(1)} %collective-permute-done.15.refs_4_.refs_5_), channel_id=1, source_target_pairs={{0,4},{1,5},{2,6},{3,7},{4,0},{5,1},{6,2},{7,3},{8,12},{9,13},{10,... | collective-permute-start | bytes 1572872 | tf_op jit(solution)/shard_map/ppermute | solution.py:283
  37.1 0.5 collective-permute-start.11
  37.6 3.4 %collective-permute-done.11.refs_1_ = f32[4,16,128]{2,1,0:T(8,128)S(1)} collective-permute-done((f32[4,16,128]{2,1,0:T(8,128)S(1)}, f32[4,16,128]{2,1,0:T(8,128)S(1)}, u32[]{:S(2)}, u32[]{:S(2)}) %collective-permute-start.11) | collective-permute-done | bytes 32800 | tf_op jit(solution)/shard_map/ppermute | solution.py:286
  41.0 0.4 shard_map.107
  41.4 1.6 %collective-permute-start.13 = (bf16[2,16,4736]{2,1,0:T(8,128)(2,1)S(1)}, bf16[2,16,4736]{2,1,0:T(8,128)(2,1)S(1)}, u32[]{:S(2)}, u32[]{:S(2)}) collective-permute-start(bf16[2,16,4736]{2,1,0:T(8,128)(2,1)S(1)} %get-tuple-element.59.mine), channel_id=1, source_target_pairs={{0,2},{1,3},{2,0},{3,1},{4,6},{5,7},{6,4},{7,5},{8,10},{9,11},{10,... | collective-permute-start | bytes 909320 | tf_op jit(solution)/shard_map/ppermute | solution.py:283
  43.0 0.5 collective-permute-start.12
  43.5 5.8 %shard_map.108.own = bf16[256,4096]{1,0:T(8,128)(2,1)} custom-call(s32[2]{0:T(128)} %pad_add_fusion.here, bf16[256,512]{1,0:T(8,128)(2,1)} %cot_ref.1, bf16[8192,512]{1,0:T(8,128)(2,1)} %w_ref.3), custom_call_target="tpu_custom_call" | custom-call | tf_op jit(solution)/shard_map/pallas_call | solution.py:206
  49.3 0.2 collective-permute-done.12.refs_0_
  49.5 1.0 %shard_map.109 = (f32[4,16,4736]{2,1,0:T(8,128)S(1)}, bf16[4,16,4736]{2,1,0:T(8,128)(2,1)S(1)}) custom-call(s32[2]{0:T(128)S(1)} %copy-done.6, s32[2]{0:T(128)S(1)} %copy-done.8, s32[2]{0:T(128)S(1)} %collective-permute-done.partner, bf16[2,16,4736]{2,1,0:T(8,128)(2,1)S(1)} %get-tuple-element.59.mine, bf16[2,16,4736]{2,1,0:T(8,128)(2,1)S(1)} %collective-permute-done.13.theirs), custom_call_target="tpu_custom_call" | custom-call | tf_op jit(solution)/shard_map/pallas_call | solution.py:44
  50.5 0.1 collective-permute-start.14
  50.6 0.5 collective-permute-start.18
  51.1 0.1 collective-permute-start.17
  51.1 0.4 collective-permute-start.19
  51.6 0.1 collective-permute-start.20
  51.7 0.9 %collective-permute-done.14.received = bf16[4,16,4736]{2,1,0:T(8,128)(2,1)S(1)} collective-permute-done((bf16[4,16,4736]{2,1,0:T(8,128)(2,1)S(1)}, bf16[4,16,4736]{2,1,0:T(8,128)(2,1)S(1)}, u32[]{:S(2)}, u32[]{:S(2)}) %collective-permute-start.14) | collective-permute-done | bytes 606240 | tf_op jit(solution)/shard_map/ppermute | solution.py:283
  52.6 0.1 shard_map.110
  52.7 0.6 collective-permute-start.23
  53.3 2.4 %collective-permute-start.24 = (bf16[1,16,4736]{2,1,0:T(8,128)(2,1)S(1)}, bf16[1,16,4736]{2,1,0:T(8,128)(2,1)S(1)}, u32[]{:S(2)}, u32[]{:S(2)}) collective-permute-start(bf16[1,16,4736]{2,1,0:T(8,128)(2,1)S(1)} %get-tuple-element.80), channel_id=1, source_target_pairs={{0,8},{1,9},{2,10},{3,11},{4,12},{5,13},{6,14},{7,15},{8,0},{9,1},... | collective-permute-start | bytes 454664 | tf_op jit(solution)/shard_map/ppermute | solution.py:283
  55.7 1.4 %collective-permute-start.25 = (bf16[1,16,4736]{2,1,0:T(8,128)(2,1)S(1)}, bf16[1,16,4736]{2,1,0:T(8,128)(2,1)S(1)}, u32[]{:S(2)}, u32[]{:S(2)}) collective-permute-start(bf16[1,16,4736]{2,1,0:T(8,128)(2,1)S(1)} %get-tuple-element.81), channel_id=1, source_target_pairs={{0,12},{1,13},{2,14},{3,15},{4,8},{5,9},{6,10},{7,11},{8,4},{9,5},... | collective-permute-start | bytes 454664 | tf_op jit(solution)/shard_map/ppermute | solution.py:283
  57.2 1.8 %shard_map.111 = (bf16[256,256]{1,0:T(8,128)(2,1)S(1)}, bf16[256,256]{1,0:T(8,128)(2,1)S(1)}) custom-call(s32[2]{0:T(128)S(1)} %copy-done.6, bf16[256,4096]{1,0:T(8,128)(2,1)S(1)} %copy-done, bf16[512,512]{1,0:T(8,128)(2,1)S(1)} %collective-permute-done.1.refs_0_.refs_1_, bf16[512,512]{1,0:T(8,128)(2,1)S(1)} %collective-permute-done.9.refs_1_.refs_2_, ...), custom_call_target="tpu_custom_call" | custom-call | tf_op jit(solution)/shard_map/pallas_call | solution.py:44
  59.0 1.4 %collective-permute-start.21 = (bf16[256,256]{1,0:T(8,128)(2,1)S(1)}, bf16[256,256]{1,0:T(8,128)(2,1)S(1)}, u32[]{:S(2)}, u32[]{:S(2)}) collective-permute-start(bf16[256,256]{1,0:T(8,128)(2,1)S(1)} %get-tuple-element.74), channel_id=1, source_target_pairs={{0,16},{16,0},{1,17},{17,1},{2,18},{18,2},{3,19},{19,3},{4,20},{20... | collective-permute-start | bytes 393224 | tf_op jit(solution)/shard_map/ppermute | solution.py:286
  60.3 0.7 %collective-permute-start.22 = (bf16[256,256]{1,0:T(8,128)(2,1)S(1)}, bf16[256,256]{1,0:T(8,128)(2,1)S(1)}, u32[]{:S(2)}, u32[]{:S(2)}) collective-permute-start(bf16[256,256]{1,0:T(8,128)(2,1)S(1)} %get-tuple-element.75), channel_id=1, source_target_pairs={{0,16},{16,0},{1,17},{17,1},{2,18},{18,2},{3,19},{19,3},{4,20},{20... | collective-permute-start | bytes 393224 | tf_op jit(solution)/shard_map/ppermute | solution.py:286
  61.1 4.2 %shard_map.113 = bf16[256,4096]{1,0:T(8,128)(2,1)} custom-call(s32[2]{0:T(128)S(1)} %copy-done.6, bf16[256,4096]{1,0:T(8,128)(2,1)S(1)} %copy-done.1, bf16[2,16,128]{2,1,0:T(8,128)(2,1)S(1)} %get-tuple-element.77.grad_low, bf16[2,16,4608]{2,1,0:T(8,128)(2,1)S(1)} %get-tuple-element.58.blocks, bf16[256,512]{1,0:T(8,128)(2,1)S(1)} %collective-permute-done.12.refs_0_, ...), custom_call_target="tpu_custom_call" | custom-call | tf_op jit(solution)/shard_map/pallas_call | solution.py:44
  65.3 1.3 %collective-permute-done.22.refs_1_ = bf16[256,256]{1,0:T(8,128)(2,1)S(1)} collective-permute-done((bf16[256,256]{1,0:T(8,128)(2,1)S(1)}, bf16[256,256]{1,0:T(8,128)(2,1)S(1)}, u32[]{:S(2)}, u32[]{:S(2)}) %collective-permute-start.22) | collective-permute-done | bytes 131104 | tf_op jit(solution)/shard_map/ppermute | solution.py:286
  66.5 1.0 %shard_map.112 = bf16[256,512]{1,0:T(8,128)(2,1)} custom-call(f32[256,512]{1,0:T(8,128)S(1)} %copy-done.3, bf16[2,16,128]{2,1,0:T(8,128)(2,1)S(1)} %get-tuple-element.57.low, bf16[2,16,4608]{2,1,0:T(8,128)(2,1)S(1)} %get-tuple-element.58.blocks, bf16[256,256]{1,0:T(8,128)(2,1)S(1)} %collective-permute-done.21.refs_0_, ...), custom_call_target="tpu_custom_call" | custom-call | tf_op jit(solution)/shard_map/pallas_call | solution.py:44
  67.5 0.0 collective-permute-done.24.refs_1_
  67.6 1.4 %shard_map.114 = (f32[1,16,4096]{2,1,0:T(8,128)}, f32[1,16,512]{2,1,0:T(8,128)}) custom-call(s32[2]{0:T(128)S(1)} %copy-done.6, s32[16]{0:T(128)S(1)} %copy-done.9, f32[1,16,4736]{2,1,0:T(8,128)S(1)} %get-tuple-element.68.first, bf16[1,16,4736]{2,1,0:T(8,128)(2,1)S(1)} %collective-permute-done.23.refs_0_, ...), custom_call_target="tpu_custom_call" | custom-call | tf_op jit(solution)/shard_map/pallas_call | solution.py:44
  (38 shorter events, 0.1 us)
Async XLA Ops:
  0.6 4.3 %copy-start.4 = (bf16[1,4096,16]{1,2,0:T(8,128)(2,1)S(1)}, bf16[1,4096,16]{1,2,0:T(8,128)(2,1)}, u32[]{:S(2)}) copy-start(bf16[1,4096,16]{1,2,0:T(8,128)(2,1)} %param.9) | copy-start | bytes 393220
  0.6 4.3 %copy-start.7 = (bf16[1,16,512]{2,1,0:T(8,128)(2,1)S(1)}, bf16[1,16,512]{2,1,0:T(8,128)(2,1)}, u32[]{:S(2)}) copy-start(bf16[1,16,512]{2,1,0:T(8,128)(2,1)} %up.1) | copy-start | bytes 49156
  0.7 8.9 %copy-start.8 = (s32[2]{0:T(128)S(1)}, s32[2]{0:T(128)}, u32[]{:S(2)}) copy-start(s32[2]{0:T(128)} %tenant.5) | copy-start | bytes 28
  1.9 19.2 %collective-permute-start.1 = (bf16[512,512]{1,0:T(8,128)(2,1)S(1)}, bf16[512,512]{1,0:T(8,128)(2,1)S(1)}, u32[]{:S(2)}, u32[]{:S(2)}) collective-permute-start(bf16[512,512]{1,0:T(8,128)(2,1)S(1)} %get-tuple-element.46), channel_id=1, source_target_pairs={{0,16},{16,0},{1,17},{17,1},{2,18},{18,2},{3,19},{19,3},{4,20},{20... | collective-permute-start | bytes 1572872 | tf_op jit(solution)/shard_map/ppermute | solution.py:286
  5.1 13.9 %collective-permute-start.2 = (bf16[1,16,4608]{2,1,0:T(8,128)(2,1)S(1)}, bf16[1,16,4608]{2,1,0:T(8,128)(2,1)S(1)}, u32[]{:S(2)}, u32[]{:S(2)}) collective-permute-start(bf16[1,16,4608]{2,1,0:T(8,128)(2,1)S(1)} %shard_map.102.refs_0_), channel_id=1, source_target_pairs={{0,4},{1,5},{2,6},{3,7},{4,0},{5,1},{6,2},{7,3},{8,12},{9,13},{10,... | collective-permute-start | bytes 442376 | tf_op jit(solution)/shard_map/ppermute | solution.py:283
  6.7 13.9 %collective-permute-start.3 = (bf16[1,16,4608]{2,1,0:T(8,128)(2,1)S(1)}, bf16[1,16,4608]{2,1,0:T(8,128)(2,1)S(1)}, u32[]{:S(2)}, u32[]{:S(2)}) collective-permute-start(bf16[1,16,4608]{2,1,0:T(8,128)(2,1)S(1)} %shard_map.102.refs_0_), channel_id=1, source_target_pairs={{0,8},{1,9},{2,10},{3,11},{4,12},{5,13},{6,14},{7,15},{8,0},{9,1},... | collective-permute-start | bytes 442376 | tf_op jit(solution)/shard_map/ppermute | solution.py:283
  9.3 11.3 %collective-permute-start.4 = (bf16[1,16,4608]{2,1,0:T(8,128)(2,1)S(1)}, bf16[1,16,4608]{2,1,0:T(8,128)(2,1)S(1)}, u32[]{:S(2)}, u32[]{:S(2)}) collective-permute-start(bf16[1,16,4608]{2,1,0:T(8,128)(2,1)S(1)} %shard_map.102.refs_0_), channel_id=1, source_target_pairs={{0,12},{1,13},{2,14},{3,15},{4,8},{5,9},{6,10},{7,11},{8,4},{9,5},... | collective-permute-start | bytes 442376 | tf_op jit(solution)/shard_map/ppermute | solution.py:283
  9.5 3.5 %collective-permute-start = (s32[2]{0:T(128)S(1)}, s32[2]{0:T(128)S(1)}, u32[]{:S(2)}, u32[]{:S(2)}) collective-permute-start(s32[2]{0:T(128)S(1)} %copy-done.8), channel_id=1, source_target_pairs={{0,2},{1,3},{2,0},{3,1},{4,6},{5,7},{6,4},{7,5},{8,10},{9,11},{10,... | collective-permute-start | bytes 32 | tf_op jit(solution)/shard_map/ppermute | solution.py:283
  11.6 10.5 %copy-start.5 = (s32[2]{0:T(128)S(1)}, s32[2]{0:T(128)}, u32[]{:S(2)}) copy-start(s32[2]{0:T(128)} %pad_add_fusion.here) | copy-start | bytes 28
  11.6 22.1 %copy-start.2 = (bf16[256,512]{1,0:T(8,128)(2,1)S(1)}, bf16[256,512]{1,0:T(8,128)(2,1)}, u32[]{:S(2)}) copy-start(bf16[256,512]{1,0:T(8,128)(2,1)} %cot_ref.1) | copy-start | bytes 786436
  13.1 20.6 %copy-start = (bf16[256,4096]{1,0:T(8,128)(2,1)S(1)}, bf16[256,4096]{1,0:T(8,128)(2,1)}, u32[]{:S(2)}) copy-start(bf16[256,4096]{1,0:T(8,128)(2,1)} %x.5) | copy-start | bytes 6291460
  18.9 2.7 %collective-permute-start.5 = (bf16[1,16,4608]{2,1,0:T(8,128)(2,1)S(1)}, bf16[1,16,4608]{2,1,0:T(8,128)(2,1)S(1)}, u32[]{:S(2)}, u32[]{:S(2)}) collective-permute-start(bf16[1,16,4608]{2,1,0:T(8,128)(2,1)S(1)} %shard_map.102.refs_0_), channel_id=1, source_target_pairs={{0,1},{1,0},{2,3},{3,2},{4,5},{5,4},{6,7},{7,6},{8,9},{9,8},{10,11... | collective-permute-start | bytes 442376 | tf_op jit(solution)/shard_map/ppermute | solution.py:283
  19.0 2.7 %collective-permute-start.6 = (bf16[1,16,4608]{2,1,0:T(8,128)(2,1)S(1)}, bf16[1,16,4608]{2,1,0:T(8,128)(2,1)S(1)}, u32[]{:S(2)}, u32[]{:S(2)}) collective-permute-start(bf16[1,16,4608]{2,1,0:T(8,128)(2,1)S(1)} %collective-permute-done.2.refs_1_), channel_id=1, source_target_pairs={{0,1},{1,0},{2,3},{3,2},{4,5},{5,4},{6,7},{7,6},{8,9},{9,8},{10,11... | collective-permute-start | bytes 442376 | tf_op jit(solution)/shard_map/ppermute | solution.py:283
  20.6 1.4 %collective-permute-start.7 = (bf16[1,16,4608]{2,1,0:T(8,128)(2,1)S(1)}, bf16[1,16,4608]{2,1,0:T(8,128)(2,1)S(1)}, u32[]{:S(2)}, u32[]{:S(2)}) collective-permute-start(bf16[1,16,4608]{2,1,0:T(8,128)(2,1)S(1)} %collective-permute-done.3.refs_2_), channel_id=1, source_target_pairs={{0,1},{1,0},{2,3},{3,2},{4,5},{5,4},{6,7},{7,6},{8,9},{9,8},{10,11... | collective-permute-start | bytes 442376 | tf_op jit(solution)/shard_map/ppermute | solution.py:283
  20.6 1.6 %collective-permute-start.8 = (bf16[1,16,4608]{2,1,0:T(8,128)(2,1)S(1)}, bf16[1,16,4608]{2,1,0:T(8,128)(2,1)S(1)}, u32[]{:S(2)}, u32[]{:S(2)}) collective-permute-start(bf16[1,16,4608]{2,1,0:T(8,128)(2,1)S(1)} %collective-permute-done.4.refs_3_), channel_id=1, source_target_pairs={{0,1},{1,0},{2,3},{3,2},{4,5},{5,4},{6,7},{7,6},{8,9},{9,8},{10,11... | collective-permute-start | bytes 442376 | tf_op jit(solution)/shard_map/ppermute | solution.py:283
  21.1 14.4 %collective-permute-start.15 = (bf16[512,512]{1,0:T(8,128)(2,1)S(1)}, bf16[512,512]{1,0:T(8,128)(2,1)S(1)}, u32[]{:S(2)}, u32[]{:S(2)}) collective-permute-start(bf16[512,512]{1,0:T(8,128)(2,1)S(1)} %get-tuple-element.65), channel_id=1, source_target_pairs={{0,16},{16,0},{1,17},{17,1},{2,18},{18,2},{3,19},{19,3},{4,20},{20... | collective-permute-start | bytes 1572872 | tf_op jit(solution)/shard_map/ppermute | solution.py:286
  22.9 14.7 %collective-permute-start.9 = (bf16[512,512]{1,0:T(8,128)(2,1)S(1)}, bf16[512,512]{1,0:T(8,128)(2,1)S(1)}, u32[]{:S(2)}, u32[]{:S(2)}) collective-permute-start(bf16[512,512]{1,0:T(8,128)(2,1)S(1)} %collective-permute-done.1.refs_0_.refs_1_), channel_id=1, source_target_pairs={{0,4},{1,5},{2,6},{3,7},{4,0},{5,1},{6,2},{7,3},{8,12},{9,13},{10,... | collective-permute-start | bytes 1572872 | tf_op jit(solution)/shard_map/ppermute | solution.py:283
  24.9 8.8 %collective-permute-start.10 = (bf16[2,16,4608]{2,1,0:T(8,128)(2,1)S(1)}, bf16[2,16,4608]{2,1,0:T(8,128)(2,1)S(1)}, u32[]{:S(2)}, u32[]{:S(2)}) collective-permute-start(bf16[2,16,4608]{2,1,0:T(8,128)(2,1)S(1)} %get-tuple-element.52), channel_id=1, source_target_pairs={{0,2},{1,3},{2,0},{3,1},{4,6},{5,7},{6,4},{7,5},{8,10},{9,11},{10,... | collective-permute-start | bytes 884744 | tf_op jit(solution)/shard_map/ppermute | solution.py:283
  35.6 16.0 %collective-permute-start.16 = (bf16[512,512]{1,0:T(8,128)(2,1)S(1)}, bf16[512,512]{1,0:T(8,128)(2,1)S(1)}, u32[]{:S(2)}, u32[]{:S(2)}) collective-permute-start(bf16[512,512]{1,0:T(8,128)(2,1)S(1)} %collective-permute-done.15.refs_4_.refs_5_), channel_id=1, source_target_pairs={{0,4},{1,5},{2,6},{3,7},{4,0},{5,1},{6,2},{7,3},{8,12},{9,13},{10,... | collective-permute-start | bytes 1572872 | tf_op jit(solution)/shard_map/ppermute | solution.py:283
  37.1 3.9 %collective-permute-start.11 = (f32[4,16,128]{2,1,0:T(8,128)S(1)}, f32[4,16,128]{2,1,0:T(8,128)S(1)}, u32[]{:S(2)}, u32[]{:S(2)}) collective-permute-start(f32[4,16,128]{2,1,0:T(8,128)S(1)} %get-tuple-element.56.refs_0_), channel_id=1, source_target_pairs={{0,16},{16,0},{1,17},{17,1},{2,18},{18,2},{3,19},{19,3},{4,20},{20... | collective-permute-start | bytes 98312 | tf_op jit(solution)/shard_map/ppermute | solution.py:286
  41.4 8.1 %copy-start.6 = (s32[2]{0:T(128)S(1)}, s32[2]{0:T(128)}, u32[]{:S(2)}) copy-start(s32[2]{0:T(128)} %pad_add_fusion.here) | copy-start | bytes 28
  41.4 8.1 %collective-permute-start.13 = (bf16[2,16,4736]{2,1,0:T(8,128)(2,1)S(1)}, bf16[2,16,4736]{2,1,0:T(8,128)(2,1)S(1)}, u32[]{:S(2)}, u32[]{:S(2)}) collective-permute-start(bf16[2,16,4736]{2,1,0:T(8,128)(2,1)S(1)} %get-tuple-element.59.mine), channel_id=1, source_target_pairs={{0,2},{1,3},{2,0},{3,1},{4,6},{5,7},{6,4},{7,5},{8,10},{9,11},{10,... | collective-permute-start | bytes 909320 | tf_op jit(solution)/shard_map/ppermute | solution.py:283
  43.0 6.5 %collective-permute-start.12 = (bf16[256,512]{1,0:T(8,128)(2,1)S(1)}, bf16[256,512]{1,0:T(8,128)(2,1)S(1)}, u32[]{:S(2)}, u32[]{:S(2)}) collective-permute-start(bf16[256,512]{1,0:T(8,128)(2,1)S(1)} %copy-done.2), channel_id=1, source_target_pairs={{0,16},{16,0},{1,17},{17,1},{2,18},{18,2},{3,19},{19,3},{4,20},{20... | collective-permute-start | bytes 786440 | tf_op jit(solution)/shard_map/ppermute | solution.py:286
  50.5 2.1 %collective-permute-start.14 = (bf16[4,16,4736]{2,1,0:T(8,128)(2,1)S(1)}, bf16[4,16,4736]{2,1,0:T(8,128)(2,1)S(1)}, u32[]{:S(2)}, u32[]{:S(2)}) collective-permute-start(bf16[4,16,4736]{2,1,0:T(8,128)(2,1)S(1)} %get-tuple-element.64), channel_id=1, source_target_pairs={{0,1},{1,0},{2,3},{3,2},{4,5},{5,4},{6,7},{7,6},{8,9},{9,8},{10,11... | collective-permute-start | bytes 1818632 | tf_op jit(solution)/shard_map/ppermute | solution.py:283
  50.6 2.8 %collective-permute-start.18 = (bf16[512,512]{1,0:T(8,128)(2,1)S(1)}, bf16[512,512]{1,0:T(8,128)(2,1)S(1)}, u32[]{:S(2)}, u32[]{:S(2)}) collective-permute-start(bf16[512,512]{1,0:T(8,128)(2,1)S(1)} %collective-permute-done.9.refs_1_.refs_2_), channel_id=1, source_target_pairs={{0,1},{1,0},{2,3},{3,2},{4,5},{5,4},{6,7},{7,6},{8,9},{9,8},{10,11... | collective-permute-start | bytes 1572872 | tf_op jit(solution)/shard_map/ppermute | solution.py:283
  51.1 4.7 %collective-permute-start.17 = (bf16[512,512]{1,0:T(8,128)(2,1)S(1)}, bf16[512,512]{1,0:T(8,128)(2,1)S(1)}, u32[]{:S(2)}, u32[]{:S(2)}) collective-permute-start(bf16[512,512]{1,0:T(8,128)(2,1)S(1)} %collective-permute-done.1.refs_0_.refs_1_), channel_id=1, source_target_pairs={{0,1},{1,0},{2,3},{3,2},{4,5},{5,4},{6,7},{7,6},{8,9},{9,8},{10,11... | collective-permute-start | bytes 1572872 | tf_op jit(solution)/shard_map/ppermute | solution.py:283
  51.1 6.0 %collective-permute-start.19 = (bf16[512,512]{1,0:T(8,128)(2,1)S(1)}, bf16[512,512]{1,0:T(8,128)(2,1)S(1)}, u32[]{:S(2)}, u32[]{:S(2)}) collective-permute-start(bf16[512,512]{1,0:T(8,128)(2,1)S(1)} %collective-permute-done.15.refs_4_.refs_5_), channel_id=1, source_target_pairs={{0,1},{1,0},{2,3},{3,2},{4,5},{5,4},{6,7},{7,6},{8,9},{9,8},{10,11... | collective-permute-start | bytes 1572872 | tf_op jit(solution)/shard_map/ppermute | solution.py:283
  51.6 5.6 %collective-permute-start.20 = (bf16[512,512]{1,0:T(8,128)(2,1)S(1)}, bf16[512,512]{1,0:T(8,128)(2,1)S(1)}, u32[]{:S(2)}, u32[]{:S(2)}) collective-permute-start(bf16[512,512]{1,0:T(8,128)(2,1)S(1)} %collective-permute-done.16.refs_5_.refs_6_), channel_id=1, source_target_pairs={{0,1},{1,0},{2,3},{3,2},{4,5},{5,4},{6,7},{7,6},{8,9},{9,8},{10,11... | collective-permute-start | bytes 1572872 | tf_op jit(solution)/shard_map/ppermute | solution.py:283
  52.7 14.8 %collective-permute-start.23 = (bf16[1,16,4736]{2,1,0:T(8,128)(2,1)S(1)}, bf16[1,16,4736]{2,1,0:T(8,128)(2,1)S(1)}, u32[]{:S(2)}, u32[]{:S(2)}) collective-permute-start(bf16[1,16,4736]{2,1,0:T(8,128)(2,1)S(1)} %get-tuple-element.79), channel_id=1, source_target_pairs={{0,4},{1,5},{2,6},{3,7},{4,0},{5,1},{6,2},{7,3},{8,12},{9,13},{10,... | collective-permute-start | bytes 454664 | tf_op jit(solution)/shard_map/ppermute | solution.py:283
  53.3 14.2 %collective-permute-start.24 = (bf16[1,16,4736]{2,1,0:T(8,128)(2,1)S(1)}, bf16[1,16,4736]{2,1,0:T(8,128)(2,1)S(1)}, u32[]{:S(2)}, u32[]{:S(2)}) collective-permute-start(bf16[1,16,4736]{2,1,0:T(8,128)(2,1)S(1)} %get-tuple-element.80), channel_id=1, source_target_pairs={{0,8},{1,9},{2,10},{3,11},{4,12},{5,13},{6,14},{7,15},{8,0},{9,1},... | collective-permute-start | bytes 454664 | tf_op jit(solution)/shard_map/ppermute | solution.py:283
  55.7 11.8 %collective-permute-start.25 = (bf16[1,16,4736]{2,1,0:T(8,128)(2,1)S(1)}, bf16[1,16,4736]{2,1,0:T(8,128)(2,1)S(1)}, u32[]{:S(2)}, u32[]{:S(2)}) collective-permute-start(bf16[1,16,4736]{2,1,0:T(8,128)(2,1)S(1)} %get-tuple-element.81), channel_id=1, source_target_pairs={{0,12},{1,13},{2,14},{3,15},{4,8},{5,9},{6,10},{7,11},{8,4},{9,5},... | collective-permute-start | bytes 454664 | tf_op jit(solution)/shard_map/ppermute | solution.py:283
  57.1 3.9 %copy-start.1 = (bf16[256,4096]{1,0:T(8,128)(2,1)S(1)}, bf16[256,4096]{1,0:T(8,128)(2,1)}, u32[]{:S(2)}) copy-start(bf16[256,4096]{1,0:T(8,128)(2,1)} %shard_map.108.own) | copy-start | bytes 6291460
  59.0 6.3 %collective-permute-start.21 = (bf16[256,256]{1,0:T(8,128)(2,1)S(1)}, bf16[256,256]{1,0:T(8,128)(2,1)S(1)}, u32[]{:S(2)}, u32[]{:S(2)}) collective-permute-start(bf16[256,256]{1,0:T(8,128)(2,1)S(1)} %get-tuple-element.74), channel_id=1, source_target_pairs={{0,16},{16,0},{1,17},{17,1},{2,18},{18,2},{3,19},{19,3},{4,20},{20... | collective-permute-start | bytes 393224 | tf_op jit(solution)/shard_map/ppermute | solution.py:286
  60.3 6.2 %collective-permute-start.22 = (bf16[256,256]{1,0:T(8,128)(2,1)S(1)}, bf16[256,256]{1,0:T(8,128)(2,1)S(1)}, u32[]{:S(2)}, u32[]{:S(2)}) collective-permute-start(bf16[256,256]{1,0:T(8,128)(2,1)S(1)} %get-tuple-element.75), channel_id=1, source_target_pairs={{0,16},{16,0},{1,17},{17,1},{2,18},{18,2},{3,19},{19,3},{4,20},{20... | collective-permute-start | bytes 393224 | tf_op jit(solution)/shard_map/ppermute | solution.py:286
  61.1 5.5 %copy-start.3 = (f32[256,512]{1,0:T(8,128)S(1)}, f32[256,512]{1,0:T(8,128)}, u32[]{:S(2)}) copy-start(f32[256,512]{1,0:T(8,128)} %shard_map.103.own) | copy-start | bytes 1572868
  61.1 6.5 %copy-start.9 = (s32[16]{0:T(128)S(1)}, s32[16]{0:T(128)}, u32[]{:S(2)}) copy-start(s32[16]{0:T(128)} %quotas) | copy-start | bytes 196

commit v3 on v2

--- a/solution.py
+++ b/solution.py
@@ -12,6 +12,7 @@
 PIECES = 2
 HOPPING = 2
 HALVES = 2
+OWN_STEPS = 4
 COUNT = 128
 VMEM_LIMIT = 20 * 1024 * 1024
 
@@ -132,9 +133,13 @@
         def _(b=b):
             blocks[b] = theirs[b]
 
-        rows = slice(b * BLOCK, (b + 1) * BLOCK)
-        part[b] = dot_nt(blocks[b, :, :features], x[rows, :])
-        part[nblocks + b] = dot_nt(blocks[b, :, features:], cot[rows, :])
+    both = blocks[...].reshape(nblocks * RANK, blocks.shape[2])
+    lows = dot_nt(x[...], both[:, :features])
+    grads = dot_nt(cot[...], both[:, features:])
+    for b in range(nblocks):
+        rows, ranks = slice(b * BLOCK, (b + 1) * BLOCK), slice(b * RANK, (b + 1) * RANK)
+        part[b] = lows[rows, ranks].T
+        part[nblocks + b] = grads[rows, ranks].T
 
 
 def gradient_kernel(x, cot, *refs):
@@ -189,32 +194,29 @@
         up_grad[o] = total[:, features : features + values] * scale
 
 
-def own_values_kernel(here, x_ref, w_ref, out_ref):
-    @pl.when(pl.program_id(0) == 0)
-    def _():
-        out_ref[...] = jnp.zeros_like(out_ref)
-
-    out_ref[...] += dot(x_ref[...], w_ref[...])
-
-
-def own_gradient_kernel(here, cot_ref, w_ref, out_ref):
-    out_ref[...] = dot_nt(cot_ref[...], w_ref[...]).astype(out_ref.dtype)
-
-
-def own_columns(kernel, here, a, a_spec, w, out_shape, out_spec, features, chunk):
-    steps = features // chunk
-    return pl.pallas_call(
-        kernel,
-        grid_spec=pltpu.PrefetchScalarGridSpec(
-            num_scalar_prefetch=1,
-            grid=(steps,),
-            in_specs=[a_spec, pl.BlockSpec((chunk, w.shape[1]), lambda j, here: (here[0] * steps + j, 0))],
-            out_specs=out_spec,
-        ),
-        out_shape=out_shape,
-        compiler_params=pltpu.CompilerParams(vmem_limit_bytes=57 * 1024 * 1024),
-        cost_estimate=pl.CostEstimate(flops=0, bytes_accessed=0, transcendentals=0),
-    )(here, a, w)
+def own_weights(here, w, held, sem):
+    steps, chunk, _ = held.shape
+    copies = []
+    for j in range(steps):
+        start = pl.multiple_of(here[0] * (steps * chunk) + j * chunk, chunk)
+        copies.append(pltpu.make_async_copy(w.at[pl.ds(start, chunk)], held.at[j], sem.at[j]))
+        copies[-1].start()
+    for j in range(steps):
+        copies[j].wait()
+        yield slice(j * chunk, (j + 1) * chunk), held[j]
+
+
+def own_values_kernel(here, x, w, out, held, sem):
+    total = None
+    for span, part in own_weights(here, w, held, sem):
+        term = dot(x[:, span], part)
+        total = term if total is None else total + term
+    out[...] = total
+
+
+def own_gradient_kernel(here, cot, w, out, held, sem):
+    for span, part in own_weights(here, w, held, sem):
+        out[:, span] = dot_nt(cot[...], part).astype(out.dtype)
 
 
 def other_values_kernel(here, x, *refs, chunk):
@@ -324,42 +326,44 @@
     def of_piece(p):
         return [k for k in range(n_sent) if k % pieces == p]
 
-    own_chunk = min(1024, features)
-    rows_by_chunk = pl.BlockSpec((token_rows, own_chunk), lambda j, here: (0, j))
-    rows_by_values = pl.BlockSpec((token_rows, values), lambda j, here: (0, 0))
-
-    def own(kernel, at, a, a_spec, out_shape, out_spec):
-        return own_columns(kernel, at, a, a_spec, frozen_value_weight, out_shape, out_spec, features, own_chunk)
-
-    value_own = own(
-        own_values_kernel,
-        after(here, partner),
-        inputs,
-        rows_by_chunk,
-        like((token_rows, values), f32),
-        rows_by_values,
-    )
-
-    held = adapters + [flip(after(a, value_own), 1) for a in adapters]
+    own_steps = OWN_STEPS if features % (OWN_STEPS * 128) == 0 else 1
+
+    def own(kernel, at, a, out_shape):
+        return call(
+            kernel,
+            [SMEM, VMEM, HBM],
+            out_shape,
+            VMEM,
+            (at, a, frozen_value_weight),
+            scratch=[
+                pltpu.VMEM((own_steps, features // own_steps, values), bf16),
+                pltpu.SemaphoreType.DMA((own_steps,)),
+            ],
+            limit=52 * 1024 * 1024,
+        )
+
+
+    held = adapters + [flip(a, 1) for a in adapters]
     mine, partners = call(
         select_kernel,
         [SMEM, SMEM, SMEM] + [VMEM] * len(held),
         [like((nblocks, RANK, width), bf16)] * 2,
         [VMEM, VMEM],
-        (here, tenant, after(partner, *[first_w[k] for k in of_piece(0)]), *held),
+        (here, tenant, partner, *held),
         upper=upper,
         owned=owned,
     )
     def hop(p, *first):
         return {k: flip(after(first_w[k], *first), 4) for k in of_piece(p) if p < HOPPING}
 
-    hops = hop(0, partners)
+    hops = hop(0, *adapters)
+    value_own = own(own_values_kernel, after(here, partners), inputs, like((token_rows, values), f32))
     blocks, part = call(
         low_kernel,
         [SMEM, SMEM, VMEM, VMEM, VMEM, VMEM],
         [like((nblocks, RANK, width), bf16), like((2 * nblocks, RANK, BLOCK), f32)],
         [VMEM, VMEM],
-        (here, tenant, inputs, value_cotangent, mine, flip(partners, 2)),
+        (here, after(tenant, value_own), inputs, value_cotangent, mine, flip(partners, 2)),
         owned=owned,
     )
     parts = [part] + turns(part)
@@ -376,12 +380,7 @@
     cots = turns(after(value_cotangent, gradients))
 
     gradient_own = own(
-        own_gradient_kernel,
-        after(here, gradients),
-        value_cotangent,
-        rows_by_values,
-        like((token_rows, features), bf16),
-        rows_by_chunk,
+        own_gradient_kernel, after(here, gradients), value_cotangent, like((token_rows, features), bf16)
     )
 
     keep, crossing = call(

time: 69.2 us -> 67.7 us (0.978)
  Pallas kernels: 25.4 us -> 22.9 us
  waiting for transfers between devices: 16.2 us -> 18.3 us
    pallas_call x2 -> x0, Pallas kernels: 11.6 us -> none  [own_columns(): pl.pallas_call(kernel, grid_spec=pltpu.PrefetchScalarGridSpec(num_scalar_...]
    pallas_call x11 -> x13, Pallas kernels: 13.8 us -> 22.9 us  [call(): pl.pallas_call(functools.partial(kernel, **settings), in_specs=in_specs,...]
    ppermute x20, waiting for transfers between devices: 11.3 us -> 12.9 us  [flip(): return lax.ppermute(a, 'dp', [(i, i ^ mask) for i in range(n_dp)])]
  transfers between devices with their start and end apart: 26 -> 26, of which waited for: 9 -> 7; matrix products, arithmetic and copies ran while one was open for 1% -> 0% of each run, Pallas kernels for 33% -> 30%
where the time goes in v3:
time: 67.7 us; the launch traced here: 67.5 us
  starting transfers between devices  25.4 us (38%)
  Pallas kernels  22.9 us (34%)
  waiting for transfers between devices  18.3 us (27%)
  between operations  0.78 us (1%)
    pallas_call x13, Pallas kernels, call(): pl.pallas_call(functools.partial(kernel, **settings), in_specs=in_specs,...  22.9 us
    ppermute x20, starting transfers between devices, flip(): return lax.ppermute(a, 'dp', [(i, i ^ mask) for i in range(n_dp)])  18.9 us
    ppermute x20, waiting for transfers between devices, flip(): return lax.ppermute(a, 'dp', [(i, i ^ mask) for i in range(n_dp)])  12.9 us
    ppermute x6, starting transfers between devices, turn(): lax.ppermute(a, 'tensor', [(i, (i + shift) % n_tensor) for i in range(n_t...  6.49 us
    ppermute x6, waiting for transfers between devices, turn(): lax.ppermute(a, 'tensor', [(i, (i + shift) % n_tensor) for i in range(n_t...  5.46 us
  transfers between devices with their start and end apart: 26, of which 7 were waited for; matrix products, arithmetic and copies ran while one was open for 0% of the time, Pallas kernels for 30%

profile of v3, /device:TPU:0, one launch (start us, length us, event | category | flops | bytes accessed | tf_op | source)
XLA Modules:
  0.0 67.5 jit_solution(9312704264744375184)
XLA Ops:
  0.7 1.3 %shard_map.105 = (bf16[512,512]{1,0:T(8,128)(2,1)S(1)}, bf16[512,512]{1,0:T(8,128)(2,1)S(1)}) custom-call(bf16[8192,512]{1,0:T(8,128)(2,1)} %w.5), custom_call_target="tpu_custom_call" | custom-call | tf_op jit(solution)/shard_map/pallas_call | solution.py:45
  1.9 3.0 %collective-permute-start.8 = (bf16[512,512]{1,0:T(8,128)(2,1)S(1)}, bf16[512,512]{1,0:T(8,128)(2,1)S(1)}, u32[]{:S(2)}, u32[]{:S(2)}) collective-permute-start(bf16[512,512]{1,0:T(8,128)(2,1)S(1)} %get-tuple-element.43), channel_id=1, source_target_pairs={{0,16},{16,0},{1,17},{17,1},{2,18},{18,2},{3,19},{19,3},{4,20},{20... | collective-permute-start | bytes 1572872 | tf_op jit(solution)/shard_map/ppermute | solution.py:288
  5.0 0.1 shard_map.102.refs_0_
  5.1 1.6 %collective-permute-start.1 = (bf16[1,16,4608]{2,1,0:T(8,128)(2,1)S(1)}, bf16[1,16,4608]{2,1,0:T(8,128)(2,1)S(1)}, u32[]{:S(2)}, u32[]{:S(2)}) collective-permute-start(bf16[1,16,4608]{2,1,0:T(8,128)(2,1)S(1)} %shard_map.102.refs_0_), channel_id=1, source_target_pairs={{0,4},{1,5},{2,6},{3,7},{4,0},{5,1},{6,2},{7,3},{8,12},{9,13},{10,... | collective-permute-start | bytes 442376 | tf_op jit(solution)/shard_map/ppermute | solution.py:285
  6.7 2.6 %collective-permute-start.2 = (bf16[1,16,4608]{2,1,0:T(8,128)(2,1)S(1)}, bf16[1,16,4608]{2,1,0:T(8,128)(2,1)S(1)}, u32[]{:S(2)}, u32[]{:S(2)}) collective-permute-start(bf16[1,16,4608]{2,1,0:T(8,128)(2,1)S(1)} %shard_map.102.refs_0_), channel_id=1, source_target_pairs={{0,8},{1,9},{2,10},{3,11},{4,12},{5,13},{6,14},{7,15},{8,0},{9,1},... | collective-permute-start | bytes 442376 | tf_op jit(solution)/shard_map/ppermute | solution.py:285
  9.3 0.2 collective-permute-start.3
  9.5 1.5 %collective-permute-start = (s32[2]{0:T(128)S(1)}, s32[2]{0:T(128)S(1)}, u32[]{:S(2)}, u32[]{:S(2)}) collective-permute-start(s32[2]{0:T(128)S(1)} %copy-done.5), channel_id=1, source_target_pairs={{0,2},{1,3},{2,0},{3,1},{4,6},{5,7},{6,4},{7,5},{8,10},{9,11},{10,... | collective-permute-start | bytes 32 | tf_op jit(solution)/shard_map/ppermute | solution.py:285
  11.1 2.0 %collective-permute-done.partner = s32[2]{0:T(128)S(1)} collective-permute-done((s32[2]{0:T(128)S(1)}, s32[2]{0:T(128)S(1)}, u32[]{:S(2)}, u32[]{:S(2)}) %collective-permute-start) | collective-permute-done | bytes 40 | tf_op jit(solution)/shard_map/ppermute | solution.py:285
  13.1 0.3 collective-permute-start.15
  13.4 7.2 %collective-permute-done.2.refs_2_ = bf16[1,16,4608]{2,1,0:T(8,128)(2,1)S(1)} collective-permute-done((bf16[1,16,4608]{2,1,0:T(8,128)(2,1)S(1)}, bf16[1,16,4608]{2,1,0:T(8,128)(2,1)S(1)}, u32[]{:S(2)}, u32[]{:S(2)}) %collective-permute-start.2) | collective-permute-done | bytes 147488 | tf_op jit(solution)/shard_map/ppermute | solution.py:285
  20.6 0.5 collective-permute-start.6
  21.1 0.1 collective-permute-start.7
  21.2 2.1 %collective-permute-start.9 = (bf16[512,512]{1,0:T(8,128)(2,1)S(1)}, bf16[512,512]{1,0:T(8,128)(2,1)S(1)}, u32[]{:S(2)}, u32[]{:S(2)}) collective-permute-start(bf16[512,512]{1,0:T(8,128)(2,1)S(1)} %collective-permute-done.8.refs_0_.refs_1_), channel_id=1, source_target_pairs={{0,4},{1,5},{2,6},{3,7},{4,0},{5,1},{6,2},{7,3},{8,12},{9,13},{10,... | collective-permute-start | bytes 1572872 | tf_op jit(solution)/shard_map/ppermute | solution.py:285
  23.3 0.1 pad_add_fusion.here
  23.3 0.7 %shard_map.103 = (bf16[2,16,4608]{2,1,0:T(8,128)(2,1)S(1)}, bf16[2,16,4608]{2,1,0:T(8,128)(2,1)S(1)}) custom-call(s32[2]{0:T(128)S(1)} %pad_add_fusion.here, s32[2]{0:T(128)S(1)} %copy-done.5, s32[2]{0:T(128)S(1)} %collective-permute-done.partner, bf16[1,16,4608]{2,1,0:T(8,128)(2,1)S(1)} %shard_map.102.refs_0_, ...), custom_call_target="tpu_custom_call" | custom-call | tf_op jit(solution)/shard_map/pallas_call | solution.py:45
  24.1 0.0 copy-start
  24.1 0.0 copy-start.2
  24.1 1.6 %collective-permute-start.10 = (bf16[2,16,4608]{2,1,0:T(8,128)(2,1)S(1)}, bf16[2,16,4608]{2,1,0:T(8,128)(2,1)S(1)}, u32[]{:S(2)}, u32[]{:S(2)}) collective-permute-start(bf16[2,16,4608]{2,1,0:T(8,128)(2,1)S(1)} %get-tuple-element.41), channel_id=1, source_target_pairs={{0,2},{1,3},{2,0},{3,1},{4,6},{5,7},{6,4},{7,5},{8,10},{9,11},{10,... | collective-permute-start | bytes 884744 | tf_op jit(solution)/shard_map/ppermute | solution.py:285
  25.7 4.5 %shard_map.104.own = f32[256,512]{1,0:T(8,128)S(1)} custom-call(s32[2]{0:T(128)S(1)} %pad_add_fusion.here, bf16[256,4096]{1,0:T(8,128)(2,1)} %x.7, bf16[8192,512]{1,0:T(8,128)(2,1)} %w.5), custom_call_target="tpu_custom_call" | custom-call | tf_op jit(solution)/shard_map/pallas_call | solution.py:45
  30.2 2.6 %collective-permute-done.10.theirs = bf16[2,16,4608]{2,1,0:T(8,128)(2,1)S(1)} collective-permute-done((bf16[2,16,4608]{2,1,0:T(8,128)(2,1)S(1)}, bf16[2,16,4608]{2,1,0:T(8,128)(2,1)S(1)}, u32[]{:S(2)}, u32[]{:S(2)}) %collective-permute-start.10) | collective-permute-done | bytes 294944 | tf_op jit(solution)/shard_map/ppermute | solution.py:285
  32.9 1.5 %shard_map.106 = (bf16[2,16,4608]{2,1,0:T(8,128)(2,1)S(1)}, f32[4,16,128]{2,1,0:T(8,128)S(1)}) custom-call(s32[2]{0:T(128)S(1)} %pad_add_fusion.here, s32[2]{0:T(128)S(1)} %copy-done.5, bf16[256,4096]{1,0:T(8,128)(2,1)S(1)} %copy-done, bf16[256,512]{1,0:T(8,128)(2,1)S(1)} %copy-done.2, bf16[2,16,4608]{2,1,0:T(8,128)(2,1)S(1)} %get-tuple-element.47.mine, ...), custom_call_target="tpu_custom_call" | custom-call | tf_op jit(solution)/shard_map/pallas_call | solution.py:45
  34.4 1.5 %collective-permute-start.16 = (bf16[512,512]{1,0:T(8,128)(2,1)S(1)}, bf16[512,512]{1,0:T(8,128)(2,1)S(1)}, u32[]{:S(2)}, u32[]{:S(2)}) collective-permute-start(bf16[512,512]{1,0:T(8,128)(2,1)S(1)} %collective-permute-done.15.refs_4_.refs_5_), channel_id=1, source_target_pairs={{0,4},{1,5},{2,6},{3,7},{4,0},{5,1},{6,2},{7,3},{8,12},{9,13},{10,... | collective-permute-start | bytes 1572872 | tf_op jit(solution)/shard_map/ppermute | solution.py:285
  35.9 0.5 collective-permute-start.11
  36.4 3.4 %collective-permute-done.11.refs_1_ = f32[4,16,128]{2,1,0:T(8,128)S(1)} collective-permute-done((f32[4,16,128]{2,1,0:T(8,128)S(1)}, f32[4,16,128]{2,1,0:T(8,128)S(1)}, u32[]{:S(2)}, u32[]{:S(2)}) %collective-permute-start.11) | collective-permute-done | bytes 32800 | tf_op jit(solution)/shard_map/ppermute | solution.py:288
  39.8 0.4 shard_map.107
  40.2 1.6 %collective-permute-start.13 = (bf16[2,16,4736]{2,1,0:T(8,128)(2,1)S(1)}, bf16[2,16,4736]{2,1,0:T(8,128)(2,1)S(1)}, u32[]{:S(2)}, u32[]{:S(2)}) collective-permute-start(bf16[2,16,4736]{2,1,0:T(8,128)(2,1)S(1)} %get-tuple-element.51.mine), channel_id=1, source_target_pairs={{0,2},{1,3},{2,0},{3,1},{4,6},{5,7},{6,4},{7,5},{8,10},{9,11},{10,... | collective-permute-start | bytes 909320 | tf_op jit(solution)/shard_map/ppermute | solution.py:285
  41.8 0.5 collective-permute-start.12
  42.3 5.0 %shard_map.108.own = bf16[256,4096]{1,0:T(8,128)(2,1)} custom-call(s32[2]{0:T(128)S(1)} %pad_add_fusion.here, bf16[256,512]{1,0:T(8,128)(2,1)S(1)} %copy-done.2, bf16[8192,512]{1,0:T(8,128)(2,1)} %w.5), custom_call_target="tpu_custom_call" | custom-call | tf_op jit(solution)/shard_map/pallas_call | solution.py:45
  47.3 0.8 %collective-permute-done.12.refs_0_ = bf16[256,512]{1,0:T(8,128)(2,1)S(1)} collective-permute-done((bf16[256,512]{1,0:T(8,128)(2,1)S(1)}, bf16[256,512]{1,0:T(8,128)(2,1)S(1)}, u32[]{:S(2)}, u32[]{:S(2)}) %collective-permute-start.12) | collective-permute-done | bytes 262176 | tf_op jit(solution)/shard_map/ppermute | solution.py:288
  48.2 0.9 %shard_map.109 = (f32[4,16,4736]{2,1,0:T(8,128)S(1)}, bf16[4,16,4736]{2,1,0:T(8,128)(2,1)S(1)}) custom-call(s32[2]{0:T(128)S(1)} %pad_add_fusion.here, s32[2]{0:T(128)S(1)} %copy-done.5, s32[2]{0:T(128)S(1)} %collective-permute-done.partner, bf16[2,16,4736]{2,1,0:T(8,128)(2,1)S(1)} %get-tuple-element.51.mine, ...), custom_call_target="tpu_custom_call" | custom-call | tf_op jit(solution)/shard_map/pallas_call | solution.py:45
  49.1 0.1 collective-permute-start.14
  49.2 0.5 collective-permute-start.18
  49.7 0.1 collective-permute-start.17
  49.7 0.4 collective-permute-start.19
  50.2 0.1 collective-permute-start.20
  50.3 0.9 %collective-permute-done.14.received = bf16[4,16,4736]{2,1,0:T(8,128)(2,1)S(1)} collective-permute-done((bf16[4,16,4736]{2,1,0:T(8,128)(2,1)S(1)}, bf16[4,16,4736]{2,1,0:T(8,128)(2,1)S(1)}, u32[]{:S(2)}, u32[]{:S(2)}) %collective-permute-start.14) | collective-permute-done | bytes 606240 | tf_op jit(solution)/shard_map/ppermute | solution.py:285
  51.2 0.1 shard_map.110
  51.3 0.6 collective-permute-start.23
  51.9 2.5 %collective-permute-start.24 = (bf16[1,16,4736]{2,1,0:T(8,128)(2,1)S(1)}, bf16[1,16,4736]{2,1,0:T(8,128)(2,1)S(1)}, u32[]{:S(2)}, u32[]{:S(2)}) collective-permute-start(bf16[1,16,4736]{2,1,0:T(8,128)(2,1)S(1)} %get-tuple-element.72), channel_id=1, source_target_pairs={{0,8},{1,9},{2,10},{3,11},{4,12},{5,13},{6,14},{7,15},{8,0},{9,1},... | collective-permute-start | bytes 454664 | tf_op jit(solution)/shard_map/ppermute | solution.py:285
  54.5 1.3 %collective-permute-start.25 = (bf16[1,16,4736]{2,1,0:T(8,128)(2,1)S(1)}, bf16[1,16,4736]{2,1,0:T(8,128)(2,1)S(1)}, u32[]{:S(2)}, u32[]{:S(2)}) collective-permute-start(bf16[1,16,4736]{2,1,0:T(8,128)(2,1)S(1)} %get-tuple-element.73), channel_id=1, source_target_pairs={{0,12},{1,13},{2,14},{3,15},{4,8},{5,9},{6,10},{7,11},{8,4},{9,5},... | collective-permute-start | bytes 454664 | tf_op jit(solution)/shard_map/ppermute | solution.py:285
  55.8 1.8 %shard_map.111 = (bf16[256,256]{1,0:T(8,128)(2,1)S(1)}, bf16[256,256]{1,0:T(8,128)(2,1)S(1)}) custom-call(s32[2]{0:T(128)S(1)} %pad_add_fusion.here, bf16[256,4096]{1,0:T(8,128)(2,1)S(1)} %copy-done, bf16[512,512]{1,0:T(8,128)(2,1)S(1)} %collective-permute-done.8.refs_0_.refs_1_, bf16[512,512]{1,0:T(8,128)(2,1)S(1)} %collective-permute-done.9.refs_1_.refs_2_, ...), custom_call_target="tpu_custom_call" | custom-call | tf_op jit(solution)/shard_map/pallas_call | solution.py:45
  57.6 0.8 %collective-permute-start.21 = (bf16[256,256]{1,0:T(8,128)(2,1)S(1)}, bf16[256,256]{1,0:T(8,128)(2,1)S(1)}, u32[]{:S(2)}, u32[]{:S(2)}) collective-permute-start(bf16[256,256]{1,0:T(8,128)(2,1)S(1)} %get-tuple-element.66), channel_id=1, source_target_pairs={{0,16},{16,0},{1,17},{17,1},{2,18},{18,2},{3,19},{19,3},{4,20},{20... | collective-permute-start | bytes 393224 | tf_op jit(solution)/shard_map/ppermute | solution.py:288
  58.4 1.3 %collective-permute-start.22 = (bf16[256,256]{1,0:T(8,128)(2,1)S(1)}, bf16[256,256]{1,0:T(8,128)(2,1)S(1)}, u32[]{:S(2)}, u32[]{:S(2)}) collective-permute-start(bf16[256,256]{1,0:T(8,128)(2,1)S(1)} %get-tuple-element.67), channel_id=1, source_target_pairs={{0,16},{16,0},{1,17},{17,1},{2,18},{18,2},{3,19},{19,3},{4,20},{20... | collective-permute-start | bytes 393224 | tf_op jit(solution)/shard_map/ppermute | solution.py:288
  59.7 4.2 %shard_map.113 = bf16[256,4096]{1,0:T(8,128)(2,1)} custom-call(s32[2]{0:T(128)S(1)} %pad_add_fusion.here, bf16[256,4096]{1,0:T(8,128)(2,1)S(1)} %copy-done.1, bf16[2,16,128]{2,1,0:T(8,128)(2,1)S(1)} %get-tuple-element.69.grad_low, bf16[2,16,4608]{2,1,0:T(8,128)(2,1)S(1)} %get-tuple-element.50.blocks, bf16[256,512]{1,0:T(8,128)(2,1)S(1)} %collective-permute-done.12.refs_0_, ...), custom_call_target="tpu_custom_call" | custom-call | tf_op jit(solution)/shard_map/pallas_call | solution.py:45
  63.9 1.3 %collective-permute-done.22.refs_1_ = bf16[256,256]{1,0:T(8,128)(2,1)S(1)} collective-permute-done((bf16[256,256]{1,0:T(8,128)(2,1)S(1)}, bf16[256,256]{1,0:T(8,128)(2,1)S(1)}, u32[]{:S(2)}, u32[]{:S(2)}) %collective-permute-start.22) | collective-permute-done | bytes 131104 | tf_op jit(solution)/shard_map/ppermute | solution.py:288
  65.2 1.0 %shard_map.112 = bf16[256,512]{1,0:T(8,128)(2,1)} custom-call(f32[256,512]{1,0:T(8,128)S(1)} %shard_map.104.own, bf16[2,16,128]{2,1,0:T(8,128)(2,1)S(1)} %get-tuple-element.49.low, bf16[2,16,4608]{2,1,0:T(8,128)(2,1)S(1)} %get-tuple-element.50.blocks, bf16[256,256]{1,0:T(8,128)(2,1)S(1)} %collective-permute-done.21.refs_0_, ...), custom_call_target="tpu_custom_call" | custom-call | tf_op jit(solution)/shard_map/pallas_call | solution.py:45
  66.1 0.0 collective-permute-done.24.refs_1_
  66.2 1.4 %shard_map.114 = (f32[1,16,4096]{2,1,0:T(8,128)}, f32[1,16,512]{2,1,0:T(8,128)}) custom-call(s32[2]{0:T(128)S(1)} %pad_add_fusion.here, s32[16]{0:T(128)S(1)} %copy-done.6, f32[1,16,4736]{2,1,0:T(8,128)S(1)} %get-tuple-element.60.first, bf16[1,16,4736]{2,1,0:T(8,128)(2,1)S(1)} %collective-permute-done.23.refs_0_, ...), custom_call_target="tpu_custom_call" | custom-call | tf_op jit(solution)/shard_map/pallas_call | solution.py:45
  (32 shorter events, 0.1 us)
Async XLA Ops:
  0.6 4.3 %copy-start.3 = (bf16[1,4096,16]{1,2,0:T(8,128)(2,1)S(1)}, bf16[1,4096,16]{1,2,0:T(8,128)(2,1)}, u32[]{:S(2)}) copy-start(bf16[1,4096,16]{1,2,0:T(8,128)(2,1)} %param.9) | copy-start | bytes 393220
  0.6 4.3 %copy-start.4 = (bf16[1,16,512]{2,1,0:T(8,128)(2,1)S(1)}, bf16[1,16,512]{2,1,0:T(8,128)(2,1)}, u32[]{:S(2)}) copy-start(bf16[1,16,512]{2,1,0:T(8,128)(2,1)} %up.1) | copy-start | bytes 49156
  0.7 8.9 %copy-start.5 = (s32[2]{0:T(128)S(1)}, s32[2]{0:T(128)}, u32[]{:S(2)}) copy-start(s32[2]{0:T(128)} %tenant.4) | copy-start | bytes 28
  1.9 19.2 %collective-permute-start.8 = (bf16[512,512]{1,0:T(8,128)(2,1)S(1)}, bf16[512,512]{1,0:T(8,128)(2,1)S(1)}, u32[]{:S(2)}, u32[]{:S(2)}) collective-permute-start(bf16[512,512]{1,0:T(8,128)(2,1)S(1)} %get-tuple-element.43), channel_id=1, source_target_pairs={{0,16},{16,0},{1,17},{17,1},{2,18},{18,2},{3,19},{19,3},{4,20},{20... | collective-permute-start | bytes 1572872 | tf_op jit(solution)/shard_map/ppermute | solution.py:288
  5.1 8.0 %collective-permute-start.1 = (bf16[1,16,4608]{2,1,0:T(8,128)(2,1)S(1)}, bf16[1,16,4608]{2,1,0:T(8,128)(2,1)S(1)}, u32[]{:S(2)}, u32[]{:S(2)}) collective-permute-start(bf16[1,16,4608]{2,1,0:T(8,128)(2,1)S(1)} %shard_map.102.refs_0_), channel_id=1, source_target_pairs={{0,4},{1,5},{2,6},{3,7},{4,0},{5,1},{6,2},{7,3},{8,12},{9,13},{10,... | collective-permute-start | bytes 442376 | tf_op jit(solution)/shard_map/ppermute | solution.py:285
  6.7 13.9 %collective-permute-start.2 = (bf16[1,16,4608]{2,1,0:T(8,128)(2,1)S(1)}, bf16[1,16,4608]{2,1,0:T(8,128)(2,1)S(1)}, u32[]{:S(2)}, u32[]{:S(2)}) collective-permute-start(bf16[1,16,4608]{2,1,0:T(8,128)(2,1)S(1)} %shard_map.102.refs_0_), channel_id=1, source_target_pairs={{0,8},{1,9},{2,10},{3,11},{4,12},{5,13},{6,14},{7,15},{8,0},{9,1},... | collective-permute-start | bytes 442376 | tf_op jit(solution)/shard_map/ppermute | solution.py:285
  9.3 11.3 %collective-permute-start.3 = (bf16[1,16,4608]{2,1,0:T(8,128)(2,1)S(1)}, bf16[1,16,4608]{2,1,0:T(8,128)(2,1)S(1)}, u32[]{:S(2)}, u32[]{:S(2)}) collective-permute-start(bf16[1,16,4608]{2,1,0:T(8,128)(2,1)S(1)} %shard_map.102.refs_0_), channel_id=1, source_target_pairs={{0,12},{1,13},{2,14},{3,15},{4,8},{5,9},{6,10},{7,11},{8,4},{9,5},... | collective-permute-start | bytes 442376 | tf_op jit(solution)/shard_map/ppermute | solution.py:285
  9.5 3.5 %collective-permute-start = (s32[2]{0:T(128)S(1)}, s32[2]{0:T(128)S(1)}, u32[]{:S(2)}, u32[]{:S(2)}) collective-permute-start(s32[2]{0:T(128)S(1)} %copy-done.5), channel_id=1, source_target_pairs={{0,2},{1,3},{2,0},{3,1},{4,6},{5,7},{6,4},{7,5},{8,10},{9,11},{10,... | collective-permute-start | bytes 32 | tf_op jit(solution)/shard_map/ppermute | solution.py:285
  13.1 8.1 %collective-permute-start.4 = (bf16[1,16,4608]{2,1,0:T(8,128)(2,1)S(1)}, bf16[1,16,4608]{2,1,0:T(8,128)(2,1)S(1)}, u32[]{:S(2)}, u32[]{:S(2)}) collective-permute-start(bf16[1,16,4608]{2,1,0:T(8,128)(2,1)S(1)} %shard_map.102.refs_0_), channel_id=1, source_target_pairs={{0,1},{1,0},{2,3},{3,2},{4,5},{5,4},{6,7},{7,6},{8,9},{9,8},{10,11... | collective-permute-start | bytes 442376 | tf_op jit(solution)/shard_map/ppermute | solution.py:285
  13.1 21.3 %collective-permute-start.15 = (bf16[512,512]{1,0:T(8,128)(2,1)S(1)}, bf16[512,512]{1,0:T(8,128)(2,1)S(1)}, u32[]{:S(2)}, u32[]{:S(2)}) collective-permute-start(bf16[512,512]{1,0:T(8,128)(2,1)S(1)} %get-tuple-element.57), channel_id=1, source_target_pairs={{0,16},{16,0},{1,17},{17,1},{2,18},{18,2},{3,19},{19,3},{4,20},{20... | collective-permute-start | bytes 1572872 | tf_op jit(solution)/shard_map/ppermute | solution.py:288
  20.6 2.7 %collective-permute-start.5 = (bf16[1,16,4608]{2,1,0:T(8,128)(2,1)S(1)}, bf16[1,16,4608]{2,1,0:T(8,128)(2,1)S(1)}, u32[]{:S(2)}, u32[]{:S(2)}) collective-permute-start(bf16[1,16,4608]{2,1,0:T(8,128)(2,1)S(1)} %collective-permute-done.1.refs_1_), channel_id=1, source_target_pairs={{0,1},{1,0},{2,3},{3,2},{4,5},{5,4},{6,7},{7,6},{8,9},{9,8},{10,11... | collective-permute-start | bytes 442376 | tf_op jit(solution)/shard_map/ppermute | solution.py:285
  20.6 2.7 %collective-permute-start.6 = (bf16[1,16,4608]{2,1,0:T(8,128)(2,1)S(1)}, bf16[1,16,4608]{2,1,0:T(8,128)(2,1)S(1)}, u32[]{:S(2)}, u32[]{:S(2)}) collective-permute-start(bf16[1,16,4608]{2,1,0:T(8,128)(2,1)S(1)} %collective-permute-done.2.refs_2_), channel_id=1, source_target_pairs={{0,1},{1,0},{2,3},{3,2},{4,5},{5,4},{6,7},{7,6},{8,9},{9,8},{10,11... | collective-permute-start | bytes 442376 | tf_op jit(solution)/shard_map/ppermute | solution.py:285
  21.1 2.2 %collective-permute-start.7 = (bf16[1,16,4608]{2,1,0:T(8,128)(2,1)S(1)}, bf16[1,16,4608]{2,1,0:T(8,128)(2,1)S(1)}, u32[]{:S(2)}, u32[]{:S(2)}) collective-permute-start(bf16[1,16,4608]{2,1,0:T(8,128)(2,1)S(1)} %collective-permute-done.3.refs_3_), channel_id=1, source_target_pairs={{0,1},{1,0},{2,3},{3,2},{4,5},{5,4},{6,7},{7,6},{8,9},{9,8},{10,11... | collective-permute-start | bytes 442376 | tf_op jit(solution)/shard_map/ppermute | solution.py:285
  21.2 15.2 %collective-permute-start.9 = (bf16[512,512]{1,0:T(8,128)(2,1)S(1)}, bf16[512,512]{1,0:T(8,128)(2,1)S(1)}, u32[]{:S(2)}, u32[]{:S(2)}) collective-permute-start(bf16[512,512]{1,0:T(8,128)(2,1)S(1)} %collective-permute-done.8.refs_0_.refs_1_), channel_id=1, source_target_pairs={{0,4},{1,5},{2,6},{3,7},{4,0},{5,1},{6,2},{7,3},{8,12},{9,13},{10,... | collective-permute-start | bytes 1572872 | tf_op jit(solution)/shard_map/ppermute | solution.py:285
  24.1 8.8 %copy-start = (bf16[256,4096]{1,0:T(8,128)(2,1)S(1)}, bf16[256,4096]{1,0:T(8,128)(2,1)}, u32[]{:S(2)}) copy-start(bf16[256,4096]{1,0:T(8,128)(2,1)} %x.7) | copy-start | bytes 6291460
  24.1 8.8 %copy-start.2 = (bf16[256,512]{1,0:T(8,128)(2,1)S(1)}, bf16[256,512]{1,0:T(8,128)(2,1)}, u32[]{:S(2)}) copy-start(bf16[256,512]{1,0:T(8,128)(2,1)} %cot.4) | copy-start | bytes 786436
  24.1 8.8 %collective-permute-start.10 = (bf16[2,16,4608]{2,1,0:T(8,128)(2,1)S(1)}, bf16[2,16,4608]{2,1,0:T(8,128)(2,1)S(1)}, u32[]{:S(2)}, u32[]{:S(2)}) collective-permute-start(bf16[2,16,4608]{2,1,0:T(8,128)(2,1)S(1)} %get-tuple-element.41), channel_id=1, source_target_pairs={{0,2},{1,3},{2,0},{3,1},{4,6},{5,7},{6,4},{7,5},{8,10},{9,11},{10,... | collective-permute-start | bytes 884744 | tf_op jit(solution)/shard_map/ppermute | solution.py:285
  34.4 15.8 %collective-permute-start.16 = (bf16[512,512]{1,0:T(8,128)(2,1)S(1)}, bf16[512,512]{1,0:T(8,128)(2,1)S(1)}, u32[]{:S(2)}, u32[]{:S(2)}) collective-permute-start(bf16[512,512]{1,0:T(8,128)(2,1)S(1)} %collective-permute-done.15.refs_4_.refs_5_), channel_id=1, source_target_pairs={{0,4},{1,5},{2,6},{3,7},{4,0},{5,1},{6,2},{7,3},{8,12},{9,13},{10,... | collective-permute-start | bytes 1572872 | tf_op jit(solution)/shard_map/ppermute | solution.py:285
  35.9 3.9 %collective-permute-start.11 = (f32[4,16,128]{2,1,0:T(8,128)S(1)}, f32[4,16,128]{2,1,0:T(8,128)S(1)}, u32[]{:S(2)}, u32[]{:S(2)}) collective-permute-start(f32[4,16,128]{2,1,0:T(8,128)S(1)} %get-tuple-element.48.refs_0_), channel_id=1, source_target_pairs={{0,16},{16,0},{1,17},{17,1},{2,18},{18,2},{3,19},{19,3},{4,20},{20... | collective-permute-start | bytes 98312 | tf_op jit(solution)/shard_map/ppermute | solution.py:288
  40.2 8.0 %collective-permute-start.13 = (bf16[2,16,4736]{2,1,0:T(8,128)(2,1)S(1)}, bf16[2,16,4736]{2,1,0:T(8,128)(2,1)S(1)}, u32[]{:S(2)}, u32[]{:S(2)}) collective-permute-start(bf16[2,16,4736]{2,1,0:T(8,128)(2,1)S(1)} %get-tuple-element.51.mine), channel_id=1, source_target_pairs={{0,2},{1,3},{2,0},{3,1},{4,6},{5,7},{6,4},{7,5},{8,10},{9,11},{10,... | collective-permute-start | bytes 909320 | tf_op jit(solution)/shard_map/ppermute | solution.py:285
  41.8 6.4 %collective-permute-start.12 = (bf16[256,512]{1,0:T(8,128)(2,1)S(1)}, bf16[256,512]{1,0:T(8,128)(2,1)S(1)}, u32[]{:S(2)}, u32[]{:S(2)}) collective-permute-start(bf16[256,512]{1,0:T(8,128)(2,1)S(1)} %copy-done.2), channel_id=1, source_target_pairs={{0,16},{16,0},{1,17},{17,1},{2,18},{18,2},{3,19},{19,3},{4,20},{20... | collective-permute-start | bytes 786440 | tf_op jit(solution)/shard_map/ppermute | solution.py:288
  49.1 2.1 %collective-permute-start.14 = (bf16[4,16,4736]{2,1,0:T(8,128)(2,1)S(1)}, bf16[4,16,4736]{2,1,0:T(8,128)(2,1)S(1)}, u32[]{:S(2)}, u32[]{:S(2)}) collective-permute-start(bf16[4,16,4736]{2,1,0:T(8,128)(2,1)S(1)} %get-tuple-element.56), channel_id=1, source_target_pairs={{0,1},{1,0},{2,3},{3,2},{4,5},{5,4},{6,7},{7,6},{8,9},{9,8},{10,11... | collective-permute-start | bytes 1818632 | tf_op jit(solution)/shard_map/ppermute | solution.py:285
  49.2 2.8 %collective-permute-start.18 = (bf16[512,512]{1,0:T(8,128)(2,1)S(1)}, bf16[512,512]{1,0:T(8,128)(2,1)S(1)}, u32[]{:S(2)}, u32[]{:S(2)}) collective-permute-start(bf16[512,512]{1,0:T(8,128)(2,1)S(1)} %collective-permute-done.9.refs_1_.refs_2_), channel_id=1, source_target_pairs={{0,1},{1,0},{2,3},{3,2},{4,5},{5,4},{6,7},{7,6},{8,9},{9,8},{10,11... | collective-permute-start | bytes 1572872 | tf_op jit(solution)/shard_map/ppermute | solution.py:285
  49.7 4.8 %collective-permute-start.17 = (bf16[512,512]{1,0:T(8,128)(2,1)S(1)}, bf16[512,512]{1,0:T(8,128)(2,1)S(1)}, u32[]{:S(2)}, u32[]{:S(2)}) collective-permute-start(bf16[512,512]{1,0:T(8,128)(2,1)S(1)} %collective-permute-done.8.refs_0_.refs_1_), channel_id=1, source_target_pairs={{0,1},{1,0},{2,3},{3,2},{4,5},{5,4},{6,7},{7,6},{8,9},{9,8},{10,11... | collective-permute-start | bytes 1572872 | tf_op jit(solution)/shard_map/ppermute | solution.py:285
  49.7 6.0 %collective-permute-start.19 = (bf16[512,512]{1,0:T(8,128)(2,1)S(1)}, bf16[512,512]{1,0:T(8,128)(2,1)S(1)}, u32[]{:S(2)}, u32[]{:S(2)}) collective-permute-start(bf16[512,512]{1,0:T(8,128)(2,1)S(1)} %collective-permute-done.15.refs_4_.refs_5_), channel_id=1, source_target_pairs={{0,1},{1,0},{2,3},{3,2},{4,5},{5,4},{6,7},{7,6},{8,9},{9,8},{10,11... | collective-permute-start | bytes 1572872 | tf_op jit(solution)/shard_map/ppermute | solution.py:285
  50.2 5.6 %collective-permute-start.20 = (bf16[512,512]{1,0:T(8,128)(2,1)S(1)}, bf16[512,512]{1,0:T(8,128)(2,1)S(1)}, u32[]{:S(2)}, u32[]{:S(2)}) collective-permute-start(bf16[512,512]{1,0:T(8,128)(2,1)S(1)} %collective-permute-done.16.refs_5_.refs_6_), channel_id=1, source_target_pairs={{0,1},{1,0},{2,3},{3,2},{4,5},{5,4},{6,7},{7,6},{8,9},{9,8},{10,11... | collective-permute-start | bytes 1572872 | tf_op jit(solution)/shard_map/ppermute | solution.py:285
  51.3 14.8 %collective-permute-start.23 = (bf16[1,16,4736]{2,1,0:T(8,128)(2,1)S(1)}, bf16[1,16,4736]{2,1,0:T(8,128)(2,1)S(1)}, u32[]{:S(2)}, u32[]{:S(2)}) collective-permute-start(bf16[1,16,4736]{2,1,0:T(8,128)(2,1)S(1)} %get-tuple-element.71), channel_id=1, source_target_pairs={{0,4},{1,5},{2,6},{3,7},{4,0},{5,1},{6,2},{7,3},{8,12},{9,13},{10,... | collective-permute-start | bytes 454664 | tf_op jit(solution)/shard_map/ppermute | solution.py:285
  51.9 14.2 %collective-permute-start.24 = (bf16[1,16,4736]{2,1,0:T(8,128)(2,1)S(1)}, bf16[1,16,4736]{2,1,0:T(8,128)(2,1)S(1)}, u32[]{:S(2)}, u32[]{:S(2)}) collective-permute-start(bf16[1,16,4736]{2,1,0:T(8,128)(2,1)S(1)} %get-tuple-element.72), channel_id=1, source_target_pairs={{0,8},{1,9},{2,10},{3,11},{4,12},{5,13},{6,14},{7,15},{8,0},{9,1},... | collective-permute-start | bytes 454664 | tf_op jit(solution)/shard_map/ppermute | solution.py:285
  54.5 11.7 %collective-permute-start.25 = (bf16[1,16,4736]{2,1,0:T(8,128)(2,1)S(1)}, bf16[1,16,4736]{2,1,0:T(8,128)(2,1)S(1)}, u32[]{:S(2)}, u32[]{:S(2)}) collective-permute-start(bf16[1,16,4736]{2,1,0:T(8,128)(2,1)S(1)} %get-tuple-element.73), channel_id=1, source_target_pairs={{0,12},{1,13},{2,14},{3,15},{4,8},{5,9},{6,10},{7,11},{8,4},{9,5},... | collective-permute-start | bytes 454664 | tf_op jit(solution)/shard_map/ppermute | solution.py:285
  55.8 3.9 %copy-start.1 = (bf16[256,4096]{1,0:T(8,128)(2,1)S(1)}, bf16[256,4096]{1,0:T(8,128)(2,1)}, u32[]{:S(2)}) copy-start(bf16[256,4096]{1,0:T(8,128)(2,1)} %shard_map.108.own) | copy-start | bytes 6291460
  57.6 6.3 %collective-permute-start.21 = (bf16[256,256]{1,0:T(8,128)(2,1)S(1)}, bf16[256,256]{1,0:T(8,128)(2,1)S(1)}, u32[]{:S(2)}, u32[]{:S(2)}) collective-permute-start(bf16[256,256]{1,0:T(8,128)(2,1)S(1)} %get-tuple-element.66), channel_id=1, source_target_pairs={{0,16},{16,0},{1,17},{17,1},{2,18},{18,2},{3,19},{19,3},{4,20},{20... | collective-permute-start | bytes 393224 | tf_op jit(solution)/shard_map/ppermute | solution.py:288
  58.4 6.8 %collective-permute-start.22 = (bf16[256,256]{1,0:T(8,128)(2,1)S(1)}, bf16[256,256]{1,0:T(8,128)(2,1)S(1)}, u32[]{:S(2)}, u32[]{:S(2)}) collective-permute-start(bf16[256,256]{1,0:T(8,128)(2,1)S(1)} %get-tuple-element.67), channel_id=1, source_target_pairs={{0,16},{16,0},{1,17},{17,1},{2,18},{18,2},{3,19},{19,3},{4,20},{20... | collective-permute-start | bytes 393224 | tf_op jit(solution)/shard_map/ppermute | solution.py:288
  59.7 6.5 %copy-start.6 = (s32[16]{0:T(128)S(1)}, s32[16]{0:T(128)}, u32[]{:S(2)}) copy-start(s32[16]{0:T(128)} %quotas) | copy-start | bytes 196

commit v4 on v3

--- a/solution.py
+++ b/solution.py
@@ -12,7 +12,7 @@
 PIECES = 2
 HOPPING = 2
 HALVES = 2
-OWN_STEPS = 4
+OWN_STEPS = 8
 COUNT = 128
 VMEM_LIMIT = 20 * 1024 * 1024
 
@@ -316,7 +316,10 @@
         pieces=pieces,
         n_tensor=n_tensor,
     )
-    adapters = [message] + [flip(message, 4 * m) for m in range(1, upper)]
+    adapters = {0: message}
+    for bit in reversed(range(upper.bit_length() - 1)):
+        adapters.update({m | 1 << bit: flip(a, 4 << bit) for m, a in adapters.items()})
+    adapters = [adapters[m] for m in range(upper)]
     first_w = [turn(sent[k], k // pieces + 1) for k in range(n_sent)]
     partner = flip(after(tenant, message), 2)
 
@@ -343,7 +346,7 @@
         )
 
 
-    held = adapters + [flip(a, 1) for a in adapters]
+    held = adapters + [flip(after(a, partner), 1) for a in adapters]
     mine, partners = call(
         select_kernel,
         [SMEM, SMEM, SMEM] + [VMEM] * len(held),
@@ -356,8 +359,10 @@
     def hop(p, *first):
         return {k: flip(after(first_w[k], *first), 4) for k in of_piece(p) if p < HOPPING}
 
-    hops = hop(0, *adapters)
+    hops = hop(0, adapters[1], partner)
     value_own = own(own_values_kernel, after(here, partners), inputs, like((token_rows, values), f32))
+    for p in range(1, pieces):
+        hops.update(hop(p, value_own))
     blocks, part = call(
         low_kernel,
         [SMEM, SMEM, VMEM, VMEM, VMEM, VMEM],
@@ -367,8 +372,6 @@
         owned=owned,
     )
     parts = [part] + turns(part)
-    for p in range(1, pieces):
-        hops.update(hop(p, part))
     low, grad_low, gradients = call(
         gradient_kernel,
         [VMEM] * (2 + len(parts)),

time: 67.7 us -> 67.3 us (level)
  waiting for transfers between devices: 18.3 us -> 16.3 us
  starting transfers between devices: 25.4 us -> 26.5 us
    ppermute x20, waiting for transfers between devices: 12.9 us -> 8.57 us  [flip(): return lax.ppermute(a, 'dp', [(i, i ^ mask) for i in range(n_dp)])]
    ppermute x6, waiting for transfers between devices: 5.46 us -> 7.77 us  [turn(): lax.ppermute(a, 'tensor', [(i, (i + shift) % n_tensor) for i in range(n_t...]
  transfers between devices with their start and end apart: 26 -> 26, of which waited for: 7 -> 11; matrix products, arithmetic and copies ran while one was open for 0% -> 0% of each run, Pallas kernels for 30% -> 31%
where the time goes in v4:
time: 67.3 us; the launch traced here: 67.1 us
  starting transfers between devices  26.5 us (39%)
  Pallas kernels  23.4 us (35%)
  waiting for transfers between devices  16.3 us (24%)
  between operations  0.8 us (1%)
    pallas_call x13, Pallas kernels, call(): pl.pallas_call(functools.partial(kernel, **settings), in_specs=in_specs,...  23.4 us
    ppermute x20, starting transfers between devices, flip(): return lax.ppermute(a, 'dp', [(i, i ^ mask) for i in range(n_dp)])  19.4 us
    ppermute x20, waiting for transfers between devices, flip(): return lax.ppermute(a, 'dp', [(i, i ^ mask) for i in range(n_dp)])  8.57 us
    ppermute x6, waiting for transfers between devices, turn(): lax.ppermute(a, 'tensor', [(i, (i + shift) % n_tensor) for i in range(n_t...  7.77 us
    ppermute x6, starting transfers between devices, turn(): lax.ppermute(a, 'tensor', [(i, (i + shift) % n_tensor) for i in range(n_t...  7.06 us
  transfers between devices with their start and end apart: 26, of which 11 were waited for; matrix products, arithmetic and copies ran while one was open for 0% of the time, Pallas kernels for 31%

profile of v4, /device:TPU:0, one launch (start us, length us, event | category | flops | bytes accessed | tf_op | source)
XLA Modules:
  0.0 67.1 jit_solution(12156881129124218846)
XLA Ops:
  0.7 1.3 %shard_map.105 = (bf16[512,512]{1,0:T(8,128)(2,1)S(1)}, bf16[512,512]{1,0:T(8,128)(2,1)S(1)}) custom-call(bf16[8192,512]{1,0:T(8,128)(2,1)} %w.5), custom_call_target="tpu_custom_call" | custom-call | tf_op jit(solution)/shard_map/pallas_call | solution.py:45
  1.9 3.0 %collective-permute-start.8 = (bf16[512,512]{1,0:T(8,128)(2,1)S(1)}, bf16[512,512]{1,0:T(8,128)(2,1)S(1)}, u32[]{:S(2)}, u32[]{:S(2)}) collective-permute-start(bf16[512,512]{1,0:T(8,128)(2,1)S(1)} %get-tuple-element.51), channel_id=1, source_target_pairs={{0,16},{16,0},{1,17},{17,1},{2,18},{18,2},{3,19},{19,3},{4,20},{20... | collective-permute-start | bytes 1572872 | tf_op jit(solution)/shard_map/ppermute | solution.py:288
  5.0 0.1 shard_map.102.refs_0_
  5.1 2.7 %collective-permute-start.2 = (bf16[1,16,4608]{2,1,0:T(8,128)(2,1)S(1)}, bf16[1,16,4608]{2,1,0:T(8,128)(2,1)S(1)}, u32[]{:S(2)}, u32[]{:S(2)}) collective-permute-start(bf16[1,16,4608]{2,1,0:T(8,128)(2,1)S(1)} %shard_map.102.refs_0_), channel_id=1, source_target_pairs={{0,8},{1,9},{2,10},{3,11},{4,12},{5,13},{6,14},{7,15},{8,0},{9,1},... | collective-permute-start | bytes 442376 | tf_op jit(solution)/shard_map/ppermute | solution.py:285
  7.7 1.6 %collective-permute-start.1 = (bf16[1,16,4608]{2,1,0:T(8,128)(2,1)S(1)}, bf16[1,16,4608]{2,1,0:T(8,128)(2,1)S(1)}, u32[]{:S(2)}, u32[]{:S(2)}) collective-permute-start(bf16[1,16,4608]{2,1,0:T(8,128)(2,1)S(1)} %shard_map.102.refs_0_), channel_id=1, source_target_pairs={{0,4},{1,5},{2,6},{3,7},{4,0},{5,1},{6,2},{7,3},{8,12},{9,13},{10,... | collective-permute-start | bytes 442376 | tf_op jit(solution)/shard_map/ppermute | solution.py:285
  9.3 0.5 collective-permute-start.15
  9.8 1.5 %collective-permute-start = (s32[2]{0:T(128)S(1)}, s32[2]{0:T(128)S(1)}, u32[]{:S(2)}, u32[]{:S(2)}) collective-permute-start(s32[2]{0:T(128)S(1)} %copy-done.5), channel_id=1, source_target_pairs={{0,2},{1,3},{2,0},{3,1},{4,6},{5,7},{6,4},{7,5},{8,10},{9,11},{10,... | collective-permute-start | bytes 32 | tf_op jit(solution)/shard_map/ppermute | solution.py:285
  11.4 3.2 %collective-permute-done.2.refs_2_ = bf16[1,16,4608]{2,1,0:T(8,128)(2,1)S(1)} collective-permute-done((bf16[1,16,4608]{2,1,0:T(8,128)(2,1)S(1)}, bf16[1,16,4608]{2,1,0:T(8,128)(2,1)S(1)}, u32[]{:S(2)}, u32[]{:S(2)}) %collective-permute-start.2) | collective-permute-done | bytes 147488 | tf_op jit(solution)/shard_map/ppermute | solution.py:285
  14.6 0.6 collective-permute-start.3
  15.2 2.5 %collective-permute-done.8.refs_0_.refs_1_ = bf16[512,512]{1,0:T(8,128)(2,1)S(1)} collective-permute-done((bf16[512,512]{1,0:T(8,128)(2,1)S(1)}, bf16[512,512]{1,0:T(8,128)(2,1)S(1)}, u32[]{:S(2)}, u32[]{:S(2)}) %collective-permute-start.8) | collective-permute-done | bytes 524320 | tf_op jit(solution)/shard_map/ppermute | solution.py:288
  17.7 2.1 %collective-permute-start.9 = (bf16[512,512]{1,0:T(8,128)(2,1)S(1)}, bf16[512,512]{1,0:T(8,128)(2,1)S(1)}, u32[]{:S(2)}, u32[]{:S(2)}) collective-permute-start(bf16[512,512]{1,0:T(8,128)(2,1)S(1)} %collective-permute-done.8.refs_0_.refs_1_), channel_id=1, source_target_pairs={{0,4},{1,5},{2,6},{3,7},{4,0},{5,1},{6,2},{7,3},{8,12},{9,13},{10,... | collective-permute-start | bytes 1572872 | tf_op jit(solution)/shard_map/ppermute | solution.py:285
  19.9 1.0 %collective-permute-done.3.refs_3_ = bf16[1,16,4608]{2,1,0:T(8,128)(2,1)S(1)} collective-permute-done((bf16[1,16,4608]{2,1,0:T(8,128)(2,1)S(1)}, bf16[1,16,4608]{2,1,0:T(8,128)(2,1)S(1)}, u32[]{:S(2)}, u32[]{:S(2)}) %collective-permute-start.3) | collective-permute-done | bytes 147488 | tf_op jit(solution)/shard_map/ppermute | solution.py:285
  20.8 0.5 collective-permute-start.7
  21.3 0.1 pad_add_fusion.here
  21.4 0.8 %collective-permute-done.6.refs_6_ = bf16[1,16,4608]{2,1,0:T(8,128)(2,1)S(1)} collective-permute-done((bf16[1,16,4608]{2,1,0:T(8,128)(2,1)S(1)}, bf16[1,16,4608]{2,1,0:T(8,128)(2,1)S(1)}, u32[]{:S(2)}, u32[]{:S(2)}) %collective-permute-start.6) | collective-permute-done | bytes 147488 | tf_op jit(solution)/shard_map/ppermute | solution.py:285
  22.2 0.2 collective-permute-done.7.refs_7_
  22.4 0.7 %shard_map.103 = (bf16[2,16,4608]{2,1,0:T(8,128)(2,1)S(1)}, bf16[2,16,4608]{2,1,0:T(8,128)(2,1)S(1)}) custom-call(s32[2]{0:T(128)S(1)} %pad_add_fusion.here, s32[2]{0:T(128)S(1)} %copy-done.5, s32[2]{0:T(128)S(1)} %collective-permute-done.partner, bf16[1,16,4608]{2,1,0:T(8,128)(2,1)S(1)} %shard_map.102.refs_0_, ...), custom_call_target="tpu_custom_call" | custom-call | tf_op jit(solution)/shard_map/pallas_call | solution.py:45
  23.2 1.7 %collective-permute-start.10 = (bf16[2,16,4608]{2,1,0:T(8,128)(2,1)S(1)}, bf16[2,16,4608]{2,1,0:T(8,128)(2,1)S(1)}, u32[]{:S(2)}, u32[]{:S(2)}) collective-permute-start(bf16[2,16,4608]{2,1,0:T(8,128)(2,1)S(1)} %get-tuple-element.49), channel_id=1, source_target_pairs={{0,2},{1,3},{2,0},{3,1},{4,6},{5,7},{6,4},{7,5},{8,10},{9,11},{10,... | collective-permute-start | bytes 884744 | tf_op jit(solution)/shard_map/ppermute | solution.py:285
  24.8 4.4 %shard_map.104.own = f32[256,512]{1,0:T(8,128)S(1)} custom-call(s32[2]{0:T(128)S(1)} %pad_add_fusion.here, bf16[256,4096]{1,0:T(8,128)(2,1)} %x.7, bf16[8192,512]{1,0:T(8,128)(2,1)} %w.5), custom_call_target="tpu_custom_call" | custom-call | tf_op jit(solution)/shard_map/pallas_call | solution.py:45
  29.3 0.7 %collective-permute-start.16 = (bf16[512,512]{1,0:T(8,128)(2,1)S(1)}, bf16[512,512]{1,0:T(8,128)(2,1)S(1)}, u32[]{:S(2)}, u32[]{:S(2)}) collective-permute-start(bf16[512,512]{1,0:T(8,128)(2,1)S(1)} %collective-permute-done.15.refs_4_.refs_5_), channel_id=1, source_target_pairs={{0,4},{1,5},{2,6},{3,7},{4,0},{5,1},{6,2},{7,3},{8,12},{9,13},{10,... | collective-permute-start | bytes 1572872 | tf_op jit(solution)/shard_map/ppermute | solution.py:285
  30.0 2.4 %collective-permute-done.10.theirs = bf16[2,16,4608]{2,1,0:T(8,128)(2,1)S(1)} collective-permute-done((bf16[2,16,4608]{2,1,0:T(8,128)(2,1)S(1)}, bf16[2,16,4608]{2,1,0:T(8,128)(2,1)S(1)}, u32[]{:S(2)}, u32[]{:S(2)}) %collective-permute-start.10) | collective-permute-done | bytes 294944 | tf_op jit(solution)/shard_map/ppermute | solution.py:285
  32.5 1.5 %shard_map.106 = (bf16[2,16,4608]{2,1,0:T(8,128)(2,1)S(1)}, f32[4,16,128]{2,1,0:T(8,128)S(1)}) custom-call(s32[2]{0:T(128)S(1)} %pad_add_fusion.here, s32[2]{0:T(128)S(1)} %copy-done.5, bf16[256,4096]{1,0:T(8,128)(2,1)S(1)} %copy-done, bf16[256,512]{1,0:T(8,128)(2,1)S(1)} %copy-done.2, bf16[2,16,4608]{2,1,0:T(8,128)(2,1)S(1)} %get-tuple-element.55.mine, ...), custom_call_target="tpu_custom_call" | custom-call | tf_op jit(solution)/shard_map/pallas_call | solution.py:45
  33.9 0.8 %collective-permute-start.11 = (f32[4,16,128]{2,1,0:T(8,128)S(1)}, f32[4,16,128]{2,1,0:T(8,128)S(1)}, u32[]{:S(2)}, u32[]{:S(2)}) collective-permute-start(f32[4,16,128]{2,1,0:T(8,128)S(1)} %get-tuple-element.56.refs_0_), channel_id=1, source_target_pairs={{0,16},{16,0},{1,17},{17,1},{2,18},{18,2},{3,19},{19,3},{4,20},{20... | collective-permute-start | bytes 98312 | tf_op jit(solution)/shard_map/ppermute | solution.py:288
  34.7 3.2 %collective-permute-done.11.refs_1_ = f32[4,16,128]{2,1,0:T(8,128)S(1)} collective-permute-done((f32[4,16,128]{2,1,0:T(8,128)S(1)}, f32[4,16,128]{2,1,0:T(8,128)S(1)}, u32[]{:S(2)}, u32[]{:S(2)}) %collective-permute-start.11) | collective-permute-done | bytes 32800 | tf_op jit(solution)/shard_map/ppermute | solution.py:288
  37.9 0.4 shard_map.107
  38.3 1.7 %collective-permute-start.13 = (bf16[2,16,4736]{2,1,0:T(8,128)(2,1)S(1)}, bf16[2,16,4736]{2,1,0:T(8,128)(2,1)S(1)}, u32[]{:S(2)}, u32[]{:S(2)}) collective-permute-start(bf16[2,16,4736]{2,1,0:T(8,128)(2,1)S(1)} %get-tuple-element.59.mine), channel_id=1, source_target_pairs={{0,2},{1,3},{2,0},{3,1},{4,6},{5,7},{6,4},{7,5},{8,10},{9,11},{10,... | collective-permute-start | bytes 909320 | tf_op jit(solution)/shard_map/ppermute | solution.py:285
  39.9 0.7 collective-permute-start.12
  40.6 5.7 %shard_map.108.own = bf16[256,4096]{1,0:T(8,128)(2,1)} custom-call(s32[2]{0:T(128)S(1)} %pad_add_fusion.here, bf16[256,512]{1,0:T(8,128)(2,1)S(1)} %copy-done.2, bf16[8192,512]{1,0:T(8,128)(2,1)} %w.5), custom_call_target="tpu_custom_call" | custom-call | tf_op jit(solution)/shard_map/pallas_call | solution.py:45
  46.3 0.3 collective-permute-done.12.refs_0_
  46.5 0.9 %shard_map.109 = (f32[4,16,4736]{2,1,0:T(8,128)S(1)}, bf16[4,16,4736]{2,1,0:T(8,128)(2,1)S(1)}) custom-call(s32[2]{0:T(128)S(1)} %pad_add_fusion.here, s32[2]{0:T(128)S(1)} %copy-done.5, s32[2]{0:T(128)S(1)} %collective-permute-done.partner, bf16[2,16,4736]{2,1,0:T(8,128)(2,1)S(1)} %get-tuple-element.59.mine, ...), custom_call_target="tpu_custom_call" | custom-call | tf_op jit(solution)/shard_map/pallas_call | solution.py:45
  47.4 0.1 collective-permute-start.14
  47.5 0.5 collective-permute-start.20
  48.0 0.1 collective-permute-start.18
  48.1 0.4 collective-permute-start.17
  48.5 0.1 collective-permute-start.19
  48.6 0.9 %collective-permute-done.14.received = bf16[4,16,4736]{2,1,0:T(8,128)(2,1)S(1)} collective-permute-done((bf16[4,16,4736]{2,1,0:T(8,128)(2,1)S(1)}, bf16[4,16,4736]{2,1,0:T(8,128)(2,1)S(1)}, u32[]{:S(2)}, u32[]{:S(2)}) %collective-permute-start.14) | collective-permute-done | bytes 606240 | tf_op jit(solution)/shard_map/ppermute | solution.py:285
  49.5 0.1 shard_map.110
  49.6 0.8 %collective-permute-start.23 = (bf16[1,16,4736]{2,1,0:T(8,128)(2,1)S(1)}, bf16[1,16,4736]{2,1,0:T(8,128)(2,1)S(1)}, u32[]{:S(2)}, u32[]{:S(2)}) collective-permute-start(bf16[1,16,4736]{2,1,0:T(8,128)(2,1)S(1)} %get-tuple-element.79), channel_id=1, source_target_pairs={{0,4},{1,5},{2,6},{3,7},{4,0},{5,1},{6,2},{7,3},{8,12},{9,13},{10,... | collective-permute-start | bytes 454664 | tf_op jit(solution)/shard_map/ppermute | solution.py:285
  50.4 3.7 %collective-permute-start.24 = (bf16[1,16,4736]{2,1,0:T(8,128)(2,1)S(1)}, bf16[1,16,4736]{2,1,0:T(8,128)(2,1)S(1)}, u32[]{:S(2)}, u32[]{:S(2)}) collective-permute-start(bf16[1,16,4736]{2,1,0:T(8,128)(2,1)S(1)} %get-tuple-element.80), channel_id=1, source_target_pairs={{0,8},{1,9},{2,10},{3,11},{4,12},{5,13},{6,14},{7,15},{8,0},{9,1},... | collective-permute-start | bytes 454664 | tf_op jit(solution)/shard_map/ppermute | solution.py:285
  54.1 0.7 %collective-permute-start.25 = (bf16[1,16,4736]{2,1,0:T(8,128)(2,1)S(1)}, bf16[1,16,4736]{2,1,0:T(8,128)(2,1)S(1)}, u32[]{:S(2)}, u32[]{:S(2)}) collective-permute-start(bf16[1,16,4736]{2,1,0:T(8,128)(2,1)S(1)} %get-tuple-element.81), channel_id=1, source_target_pairs={{0,12},{1,13},{2,14},{3,15},{4,8},{5,9},{6,10},{7,11},{8,4},{9,5},... | collective-permute-start | bytes 454664 | tf_op jit(solution)/shard_map/ppermute | solution.py:285
  54.9 1.8 %shard_map.111 = (bf16[256,256]{1,0:T(8,128)(2,1)S(1)}, bf16[256,256]{1,0:T(8,128)(2,1)S(1)}) custom-call(s32[2]{0:T(128)S(1)} %pad_add_fusion.here, bf16[256,4096]{1,0:T(8,128)(2,1)S(1)} %copy-done, bf16[512,512]{1,0:T(8,128)(2,1)S(1)} %collective-permute-done.8.refs_0_.refs_1_, bf16[512,512]{1,0:T(8,128)(2,1)S(1)} %collective-permute-done.9.refs_1_.refs_2_, ...), custom_call_target="tpu_custom_call" | custom-call | tf_op jit(solution)/shard_map/pallas_call | solution.py:45
  56.7 1.2 %collective-permute-start.21 = (bf16[256,256]{1,0:T(8,128)(2,1)S(1)}, bf16[256,256]{1,0:T(8,128)(2,1)S(1)}, u32[]{:S(2)}, u32[]{:S(2)}) collective-permute-start(bf16[256,256]{1,0:T(8,128)(2,1)S(1)} %get-tuple-element.74), channel_id=1, source_target_pairs={{0,16},{16,0},{1,17},{17,1},{2,18},{18,2},{3,19},{19,3},{4,20},{20... | collective-permute-start | bytes 393224 | tf_op jit(solution)/shard_map/ppermute | solution.py:288
  57.9 0.9 %collective-permute-start.22 = (bf16[256,256]{1,0:T(8,128)(2,1)S(1)}, bf16[256,256]{1,0:T(8,128)(2,1)S(1)}, u32[]{:S(2)}, u32[]{:S(2)}) collective-permute-start(bf16[256,256]{1,0:T(8,128)(2,1)S(1)} %get-tuple-element.75), channel_id=1, source_target_pairs={{0,16},{16,0},{1,17},{17,1},{2,18},{18,2},{3,19},{19,3},{4,20},{20... | collective-permute-start | bytes 393224 | tf_op jit(solution)/shard_map/ppermute | solution.py:288
  58.8 4.2 %shard_map.113 = bf16[256,4096]{1,0:T(8,128)(2,1)} custom-call(s32[2]{0:T(128)S(1)} %pad_add_fusion.here, bf16[256,4096]{1,0:T(8,128)(2,1)S(1)} %copy-done.1, bf16[2,16,128]{2,1,0:T(8,128)(2,1)S(1)} %get-tuple-element.77.grad_low, bf16[2,16,4608]{2,1,0:T(8,128)(2,1)S(1)} %get-tuple-element.58.blocks, bf16[256,512]{1,0:T(8,128)(2,1)S(1)} %collective-permute-done.12.refs_0_, ...), custom_call_target="tpu_custom_call" | custom-call | tf_op jit(solution)/shard_map/pallas_call | solution.py:45
  63.0 0.1 collective-permute-done.21.refs_0_
  63.1 1.7 %collective-permute-done.22.refs_1_ = bf16[256,256]{1,0:T(8,128)(2,1)S(1)} collective-permute-done((bf16[256,256]{1,0:T(8,128)(2,1)S(1)}, bf16[256,256]{1,0:T(8,128)(2,1)S(1)}, u32[]{:S(2)}, u32[]{:S(2)}) %collective-permute-start.22) | collective-permute-done | bytes 131104 | tf_op jit(solution)/shard_map/ppermute | solution.py:288
  64.8 1.0 %shard_map.112 = bf16[256,512]{1,0:T(8,128)(2,1)} custom-call(f32[256,512]{1,0:T(8,128)S(1)} %shard_map.104.own, bf16[2,16,128]{2,1,0:T(8,128)(2,1)S(1)} %get-tuple-element.57.low, bf16[2,16,4608]{2,1,0:T(8,128)(2,1)S(1)} %get-tuple-element.58.blocks, bf16[256,256]{1,0:T(8,128)(2,1)S(1)} %collective-permute-done.21.refs_0_, ...), custom_call_target="tpu_custom_call" | custom-call | tf_op jit(solution)/shard_map/pallas_call | solution.py:45
  65.8 1.4 %shard_map.114 = (f32[1,16,4096]{2,1,0:T(8,128)}, f32[1,16,512]{2,1,0:T(8,128)}) custom-call(s32[2]{0:T(128)S(1)} %pad_add_fusion.here, s32[16]{0:T(128)S(1)} %copy-done.6, f32[1,16,4736]{2,1,0:T(8,128)S(1)} %get-tuple-element.68.first, bf16[1,16,4736]{2,1,0:T(8,128)(2,1)S(1)} %collective-permute-done.23.refs_0_, ...), custom_call_target="tpu_custom_call" | custom-call | tf_op jit(solution)/shard_map/pallas_call | solution.py:45
  (32 shorter events, 0.1 us)
Async XLA Ops:
  0.6 4.3 %copy-start.3 = (bf16[1,4096,16]{1,2,0:T(8,128)(2,1)S(1)}, bf16[1,4096,16]{1,2,0:T(8,128)(2,1)}, u32[]{:S(2)}) copy-start(bf16[1,4096,16]{1,2,0:T(8,128)(2,1)} %param.9) | copy-start | bytes 393220
  0.6 4.3 %copy-start.4 = (bf16[1,16,512]{2,1,0:T(8,128)(2,1)S(1)}, bf16[1,16,512]{2,1,0:T(8,128)(2,1)}, u32[]{:S(2)}) copy-start(bf16[1,16,512]{2,1,0:T(8,128)(2,1)} %up.1) | copy-start | bytes 49156
  0.7 9.2 %copy-start.5 = (s32[2]{0:T(128)S(1)}, s32[2]{0:T(128)}, u32[]{:S(2)}) copy-start(s32[2]{0:T(128)} %tenant.4) | copy-start | bytes 28
  1.9 15.8 %collective-permute-start.8 = (bf16[512,512]{1,0:T(8,128)(2,1)S(1)}, bf16[512,512]{1,0:T(8,128)(2,1)S(1)}, u32[]{:S(2)}, u32[]{:S(2)}) collective-permute-start(bf16[512,512]{1,0:T(8,128)(2,1)S(1)} %get-tuple-element.51), channel_id=1, source_target_pairs={{0,16},{16,0},{1,17},{17,1},{2,18},{18,2},{3,19},{19,3},{4,20},{20... | collective-permute-start | bytes 1572872 | tf_op jit(solution)/shard_map/ppermute | solution.py:288
  5.1 9.5 %collective-permute-start.2 = (bf16[1,16,4608]{2,1,0:T(8,128)(2,1)S(1)}, bf16[1,16,4608]{2,1,0:T(8,128)(2,1)S(1)}, u32[]{:S(2)}, u32[]{:S(2)}) collective-permute-start(bf16[1,16,4608]{2,1,0:T(8,128)(2,1)S(1)} %shard_map.102.refs_0_), channel_id=1, source_target_pairs={{0,8},{1,9},{2,10},{3,11},{4,12},{5,13},{6,14},{7,15},{8,0},{9,1},... | collective-permute-start | bytes 442376 | tf_op jit(solution)/shard_map/ppermute | solution.py:285
  7.7 7.5 %collective-permute-start.1 = (bf16[1,16,4608]{2,1,0:T(8,128)(2,1)S(1)}, bf16[1,16,4608]{2,1,0:T(8,128)(2,1)S(1)}, u32[]{:S(2)}, u32[]{:S(2)}) collective-permute-start(bf16[1,16,4608]{2,1,0:T(8,128)(2,1)S(1)} %shard_map.102.refs_0_), channel_id=1, source_target_pairs={{0,4},{1,5},{2,6},{3,7},{4,0},{5,1},{6,2},{7,3},{8,12},{9,13},{10,... | collective-permute-start | bytes 442376 | tf_op jit(solution)/shard_map/ppermute | solution.py:285
  9.3 20.0 %collective-permute-start.15 = (bf16[512,512]{1,0:T(8,128)(2,1)S(1)}, bf16[512,512]{1,0:T(8,128)(2,1)S(1)}, u32[]{:S(2)}, u32[]{:S(2)}) collective-permute-start(bf16[512,512]{1,0:T(8,128)(2,1)S(1)} %get-tuple-element.65), channel_id=1, source_target_pairs={{0,16},{16,0},{1,17},{17,1},{2,18},{18,2},{3,19},{19,3},{4,20},{20... | collective-permute-start | bytes 1572872 | tf_op jit(solution)/shard_map/ppermute | solution.py:288
  9.8 5.3 %collective-permute-start = (s32[2]{0:T(128)S(1)}, s32[2]{0:T(128)S(1)}, u32[]{:S(2)}, u32[]{:S(2)}) collective-permute-start(s32[2]{0:T(128)S(1)} %copy-done.5), channel_id=1, source_target_pairs={{0,2},{1,3},{2,0},{3,1},{4,6},{5,7},{6,4},{7,5},{8,10},{9,11},{10,... | collective-permute-start | bytes 32 | tf_op jit(solution)/shard_map/ppermute | solution.py:285
  14.6 6.2 %collective-permute-start.3 = (bf16[1,16,4608]{2,1,0:T(8,128)(2,1)S(1)}, bf16[1,16,4608]{2,1,0:T(8,128)(2,1)S(1)}, u32[]{:S(2)}, u32[]{:S(2)}) collective-permute-start(bf16[1,16,4608]{2,1,0:T(8,128)(2,1)S(1)} %collective-permute-done.2.refs_2_), channel_id=1, source_target_pairs={{0,4},{1,5},{2,6},{3,7},{4,0},{5,1},{6,2},{7,3},{8,12},{9,13},{10,... | collective-permute-start | bytes 442376 | tf_op jit(solution)/shard_map/ppermute | solution.py:285
  15.2 5.6 %collective-permute-start.4 = (bf16[1,16,4608]{2,1,0:T(8,128)(2,1)S(1)}, bf16[1,16,4608]{2,1,0:T(8,128)(2,1)S(1)}, u32[]{:S(2)}, u32[]{:S(2)}) collective-permute-start(bf16[1,16,4608]{2,1,0:T(8,128)(2,1)S(1)} %shard_map.102.refs_0_), channel_id=1, source_target_pairs={{0,1},{1,0},{2,3},{3,2},{4,5},{5,4},{6,7},{7,6},{8,9},{9,8},{10,11... | collective-permute-start | bytes 442376 | tf_op jit(solution)/shard_map/ppermute | solution.py:285
  17.7 17.0 %collective-permute-start.9 = (bf16[512,512]{1,0:T(8,128)(2,1)S(1)}, bf16[512,512]{1,0:T(8,128)(2,1)S(1)}, u32[]{:S(2)}, u32[]{:S(2)}) collective-permute-start(bf16[512,512]{1,0:T(8,128)(2,1)S(1)} %collective-permute-done.8.refs_0_.refs_1_), channel_id=1, source_target_pairs={{0,4},{1,5},{2,6},{3,7},{4,0},{5,1},{6,2},{7,3},{8,12},{9,13},{10,... | collective-permute-start | bytes 1572872 | tf_op jit(solution)/shard_map/ppermute | solution.py:285
  19.9 1.6 %collective-permute-start.5 = (bf16[1,16,4608]{2,1,0:T(8,128)(2,1)S(1)}, bf16[1,16,4608]{2,1,0:T(8,128)(2,1)S(1)}, u32[]{:S(2)}, u32[]{:S(2)}) collective-permute-start(bf16[1,16,4608]{2,1,0:T(8,128)(2,1)S(1)} %collective-permute-done.1.refs_1_), channel_id=1, source_target_pairs={{0,1},{1,0},{2,3},{3,2},{4,5},{5,4},{6,7},{7,6},{8,9},{9,8},{10,11... | collective-permute-start | bytes 442376 | tf_op jit(solution)/shard_map/ppermute | solution.py:285
  20.8 1.4 %collective-permute-start.6 = (bf16[1,16,4608]{2,1,0:T(8,128)(2,1)S(1)}, bf16[1,16,4608]{2,1,0:T(8,128)(2,1)S(1)}, u32[]{:S(2)}, u32[]{:S(2)}) collective-permute-start(bf16[1,16,4608]{2,1,0:T(8,128)(2,1)S(1)} %collective-permute-done.2.refs_2_), channel_id=1, source_target_pairs={{0,1},{1,0},{2,3},{3,2},{4,5},{5,4},{6,7},{7,6},{8,9},{9,8},{10,11... | collective-permute-start | bytes 442376 | tf_op jit(solution)/shard_map/ppermute | solution.py:285
  20.8 1.6 %collective-permute-start.7 = (bf16[1,16,4608]{2,1,0:T(8,128)(2,1)S(1)}, bf16[1,16,4608]{2,1,0:T(8,128)(2,1)S(1)}, u32[]{:S(2)}, u32[]{:S(2)}) collective-permute-start(bf16[1,16,4608]{2,1,0:T(8,128)(2,1)S(1)} %collective-permute-done.3.refs_3_), channel_id=1, source_target_pairs={{0,1},{1,0},{2,3},{3,2},{4,5},{5,4},{6,7},{7,6},{8,9},{9,8},{10,11... | collective-permute-start | bytes 442376 | tf_op jit(solution)/shard_map/ppermute | solution.py:285
  23.1 9.3 %copy-start = (bf16[256,4096]{1,0:T(8,128)(2,1)S(1)}, bf16[256,4096]{1,0:T(8,128)(2,1)}, u32[]{:S(2)}) copy-start(bf16[256,4096]{1,0:T(8,128)(2,1)} %x.7) | copy-start | bytes 6291460
  23.2 9.3 %copy-start.2 = (bf16[256,512]{1,0:T(8,128)(2,1)S(1)}, bf16[256,512]{1,0:T(8,128)(2,1)}, u32[]{:S(2)}) copy-start(bf16[256,512]{1,0:T(8,128)(2,1)} %cot.4) | copy-start | bytes 786436
  23.2 9.3 %collective-permute-start.10 = (bf16[2,16,4608]{2,1,0:T(8,128)(2,1)S(1)}, bf16[2,16,4608]{2,1,0:T(8,128)(2,1)S(1)}, u32[]{:S(2)}, u32[]{:S(2)}) collective-permute-start(bf16[2,16,4608]{2,1,0:T(8,128)(2,1)S(1)} %get-tuple-element.49), channel_id=1, source_target_pairs={{0,2},{1,3},{2,0},{3,1},{4,6},{5,7},{6,4},{7,5},{8,10},{9,11},{10,... | collective-permute-start | bytes 884744 | tf_op jit(solution)/shard_map/ppermute | solution.py:285
  29.3 18.2 %collective-permute-start.16 = (bf16[512,512]{1,0:T(8,128)(2,1)S(1)}, bf16[512,512]{1,0:T(8,128)(2,1)S(1)}, u32[]{:S(2)}, u32[]{:S(2)}) collective-permute-start(bf16[512,512]{1,0:T(8,128)(2,1)S(1)} %collective-permute-done.15.refs_4_.refs_5_), channel_id=1, source_target_pairs={{0,4},{1,5},{2,6},{3,7},{4,0},{5,1},{6,2},{7,3},{8,12},{9,13},{10,... | collective-permute-start | bytes 1572872 | tf_op jit(solution)/shard_map/ppermute | solution.py:285
  33.9 4.0 %collective-permute-start.11 = (f32[4,16,128]{2,1,0:T(8,128)S(1)}, f32[4,16,128]{2,1,0:T(8,128)S(1)}, u32[]{:S(2)}, u32[]{:S(2)}) collective-permute-start(f32[4,16,128]{2,1,0:T(8,128)S(1)} %get-tuple-element.56.refs_0_), channel_id=1, source_target_pairs={{0,16},{16,0},{1,17},{17,1},{2,18},{18,2},{3,19},{19,3},{4,20},{20... | collective-permute-start | bytes 98312 | tf_op jit(solution)/shard_map/ppermute | solution.py:288
  38.3 8.2 %collective-permute-start.13 = (bf16[2,16,4736]{2,1,0:T(8,128)(2,1)S(1)}, bf16[2,16,4736]{2,1,0:T(8,128)(2,1)S(1)}, u32[]{:S(2)}, u32[]{:S(2)}) collective-permute-start(bf16[2,16,4736]{2,1,0:T(8,128)(2,1)S(1)} %get-tuple-element.59.mine), channel_id=1, source_target_pairs={{0,2},{1,3},{2,0},{3,1},{4,6},{5,7},{6,4},{7,5},{8,10},{9,11},{10,... | collective-permute-start | bytes 909320 | tf_op jit(solution)/shard_map/ppermute | solution.py:285
  39.9 6.6 %collective-permute-start.12 = (bf16[256,512]{1,0:T(8,128)(2,1)S(1)}, bf16[256,512]{1,0:T(8,128)(2,1)S(1)}, u32[]{:S(2)}, u32[]{:S(2)}) collective-permute-start(bf16[256,512]{1,0:T(8,128)(2,1)S(1)} %copy-done.2), channel_id=1, source_target_pairs={{0,16},{16,0},{1,17},{17,1},{2,18},{18,2},{3,19},{19,3},{4,20},{20... | collective-permute-start | bytes 786440 | tf_op jit(solution)/shard_map/ppermute | solution.py:288
  47.4 2.1 %collective-permute-start.14 = (bf16[4,16,4736]{2,1,0:T(8,128)(2,1)S(1)}, bf16[4,16,4736]{2,1,0:T(8,128)(2,1)S(1)}, u32[]{:S(2)}, u32[]{:S(2)}) collective-permute-start(bf16[4,16,4736]{2,1,0:T(8,128)(2,1)S(1)} %get-tuple-element.64), channel_id=1, source_target_pairs={{0,1},{1,0},{2,3},{3,2},{4,5},{5,4},{6,7},{7,6},{8,9},{9,8},{10,11... | collective-permute-start | bytes 1818632 | tf_op jit(solution)/shard_map/ppermute | solution.py:285
  47.5 2.9 %collective-permute-start.20 = (bf16[512,512]{1,0:T(8,128)(2,1)S(1)}, bf16[512,512]{1,0:T(8,128)(2,1)S(1)}, u32[]{:S(2)}, u32[]{:S(2)}) collective-permute-start(bf16[512,512]{1,0:T(8,128)(2,1)S(1)} %collective-permute-done.16.refs_5_.refs_6_), channel_id=1, source_target_pairs={{0,1},{1,0},{2,3},{3,2},{4,5},{5,4},{6,7},{7,6},{8,9},{9,8},{10,11... | collective-permute-start | bytes 1572872 | tf_op jit(solution)/shard_map/ppermute | solution.py:285
  48.0 6.2 %collective-permute-start.18 = (bf16[512,512]{1,0:T(8,128)(2,1)S(1)}, bf16[512,512]{1,0:T(8,128)(2,1)S(1)}, u32[]{:S(2)}, u32[]{:S(2)}) collective-permute-start(bf16[512,512]{1,0:T(8,128)(2,1)S(1)} %collective-permute-done.9.refs_1_.refs_2_), channel_id=1, source_target_pairs={{0,1},{1,0},{2,3},{3,2},{4,5},{5,4},{6,7},{7,6},{8,9},{9,8},{10,11... | collective-permute-start | bytes 1572872 | tf_op jit(solution)/shard_map/ppermute | solution.py:285
  48.1 6.8 %collective-permute-start.17 = (bf16[512,512]{1,0:T(8,128)(2,1)S(1)}, bf16[512,512]{1,0:T(8,128)(2,1)S(1)}, u32[]{:S(2)}, u32[]{:S(2)}) collective-permute-start(bf16[512,512]{1,0:T(8,128)(2,1)S(1)} %collective-permute-done.8.refs_0_.refs_1_), channel_id=1, source_target_pairs={{0,1},{1,0},{2,3},{3,2},{4,5},{5,4},{6,7},{7,6},{8,9},{9,8},{10,11... | collective-permute-start | bytes 1572872 | tf_op jit(solution)/shard_map/ppermute | solution.py:285
  48.5 6.4 %collective-permute-start.19 = (bf16[512,512]{1,0:T(8,128)(2,1)S(1)}, bf16[512,512]{1,0:T(8,128)(2,1)S(1)}, u32[]{:S(2)}, u32[]{:S(2)}) collective-permute-start(bf16[512,512]{1,0:T(8,128)(2,1)S(1)} %collective-permute-done.15.refs_4_.refs_5_), channel_id=1, source_target_pairs={{0,1},{1,0},{2,3},{3,2},{4,5},{5,4},{6,7},{7,6},{8,9},{9,8},{10,11... | collective-permute-start | bytes 1572872 | tf_op jit(solution)/shard_map/ppermute | solution.py:285
  49.6 16.1 %collective-permute-start.23 = (bf16[1,16,4736]{2,1,0:T(8,128)(2,1)S(1)}, bf16[1,16,4736]{2,1,0:T(8,128)(2,1)S(1)}, u32[]{:S(2)}, u32[]{:S(2)}) collective-permute-start(bf16[1,16,4736]{2,1,0:T(8,128)(2,1)S(1)} %get-tuple-element.79), channel_id=1, source_target_pairs={{0,4},{1,5},{2,6},{3,7},{4,0},{5,1},{6,2},{7,3},{8,12},{9,13},{10,... | collective-permute-start | bytes 454664 | tf_op jit(solution)/shard_map/ppermute | solution.py:285
  50.4 15.4 %collective-permute-start.24 = (bf16[1,16,4736]{2,1,0:T(8,128)(2,1)S(1)}, bf16[1,16,4736]{2,1,0:T(8,128)(2,1)S(1)}, u32[]{:S(2)}, u32[]{:S(2)}) collective-permute-start(bf16[1,16,4736]{2,1,0:T(8,128)(2,1)S(1)} %get-tuple-element.80), channel_id=1, source_target_pairs={{0,8},{1,9},{2,10},{3,11},{4,12},{5,13},{6,14},{7,15},{8,0},{9,1},... | collective-permute-start | bytes 454664 | tf_op jit(solution)/shard_map/ppermute | solution.py:285
  54.1 11.6 %collective-permute-start.25 = (bf16[1,16,4736]{2,1,0:T(8,128)(2,1)S(1)}, bf16[1,16,4736]{2,1,0:T(8,128)(2,1)S(1)}, u32[]{:S(2)}, u32[]{:S(2)}) collective-permute-start(bf16[1,16,4736]{2,1,0:T(8,128)(2,1)S(1)} %get-tuple-element.81), channel_id=1, source_target_pairs={{0,12},{1,13},{2,14},{3,15},{4,8},{5,9},{6,10},{7,11},{8,4},{9,5},... | collective-permute-start | bytes 454664 | tf_op jit(solution)/shard_map/ppermute | solution.py:285
  54.9 3.9 %copy-start.1 = (bf16[256,4096]{1,0:T(8,128)(2,1)S(1)}, bf16[256,4096]{1,0:T(8,128)(2,1)}, u32[]{:S(2)}) copy-start(bf16[256,4096]{1,0:T(8,128)(2,1)} %shard_map.108.own) | copy-start | bytes 6291460
  56.7 6.4 %collective-permute-start.21 = (bf16[256,256]{1,0:T(8,128)(2,1)S(1)}, bf16[256,256]{1,0:T(8,128)(2,1)S(1)}, u32[]{:S(2)}, u32[]{:S(2)}) collective-permute-start(bf16[256,256]{1,0:T(8,128)(2,1)S(1)} %get-tuple-element.74), channel_id=1, source_target_pairs={{0,16},{16,0},{1,17},{17,1},{2,18},{18,2},{3,19},{19,3},{4,20},{20... | collective-permute-start | bytes 393224 | tf_op jit(solution)/shard_map/ppermute | solution.py:288
  57.9 6.9 %collective-permute-start.22 = (bf16[256,256]{1,0:T(8,128)(2,1)S(1)}, bf16[256,256]{1,0:T(8,128)(2,1)S(1)}, u32[]{:S(2)}, u32[]{:S(2)}) collective-permute-start(bf16[256,256]{1,0:T(8,128)(2,1)S(1)} %get-tuple-element.75), channel_id=1, source_target_pairs={{0,16},{16,0},{1,17},{17,1},{2,18},{18,2},{3,19},{19,3},{4,20},{20... | collective-permute-start | bytes 393224 | tf_op jit(solution)/shard_map/ppermute | solution.py:288
  58.8 7.0 %copy-start.6 = (s32[16]{0:T(128)S(1)}, s32[16]{0:T(128)}, u32[]{:S(2)}) copy-start(s32[16]{0:T(128)} %quotas) | copy-start | bytes 196

commit v5 on v4

--- a/solution.py
+++ b/solution.py
@@ -256,6 +256,13 @@
             for other in received[i::HALVES]:
                 part = part + other[rows].astype(f32)
             out[rows, span] = part.astype(out.dtype)
+
+
+def last_kernel(own, low, blocks, *refs, owned, n_returned):
+    returned, (here, quotas, *sums) = refs[:n_returned], refs[n_returned:-3]
+    out, down_grad, up_grad = refs[-3:]
+    values_kernel(own, low, blocks, *returned, out)
+    final_kernel(here, quotas, *sums, down_grad, up_grad, owned=owned)
 
 
 def after(a, *first):
@@ -405,7 +412,7 @@
         (keep, after(flip(crossing, 1), *[hops[k] for k in of_piece(1) if k in hops])),
         owned=owned,
     )
-    owners = [flip(a, 4 * m) for m, a in enumerate(to_owners, 1)]
+    owners = [flip(a, 4 * m) for m, a in sorted(enumerate(to_owners, 1), key=lambda pair: pair[0] != upper // 2)]
 
     w_groups = []
     for s in shifts:
@@ -442,21 +449,18 @@
         chunk=chunk,
     )
     returned = [turn(a, -(i // HALVES + 1)) for i, a in enumerate(value_parts)]
-    adapted_values = call(
-        values_kernel,
-        [VMEM] * (3 + len(returned)),
-        like((token_rows, values), bf16),
-        VMEM,
-        (value_own, low, blocks, *returned),
-    )
-    down_grad, gradient_up_matrix = call(
-        final_kernel,
-        [SMEM, SMEM] + [VMEM] * upper,
-        [like((owned, RANK, features), f32), like((owned, RANK, values), f32)],
-        [VMEM, VMEM],
-        (here, after(quotas, adapted_values), summed, *owners),
-        moved=1 << 26,
+    adapted_values, down_grad, gradient_up_matrix = call(
+        last_kernel,
+        [VMEM] * (3 + len(returned)) + [SMEM, SMEM] + [VMEM] * upper,
+        [
+            like((token_rows, values), bf16),
+            like((owned, RANK, features), f32),
+            like((owned, RANK, values), f32),
+        ],
+        [VMEM] * 3,
+        (value_own, low, blocks, *returned, here, quotas, summed, *owners),
         owned=owned,
+        n_returned=len(returned),
     )
     return (adapted_values, gradient_inputs, jnp.swapaxes(down_grad, 1, 2), gradient_up_matrix)
 

time: 67.3 us -> 66.7 us (level)
    pallas_call x13 -> x12, Pallas kernels: 23.4 us -> 22.8 us  [call(): pl.pallas_call(functools.partial(kernel, **settings), in_specs=in_specs,...]
  transfers between devices with their start and end apart: 26 -> 26, of which waited for: 11 -> 11; matrix products, arithmetic and copies ran while one was open for 0% -> 0% of each run, Pallas kernels for 31% -> 30%
where the time goes in v5:
time: 66.7 us; the launch traced here: 66.5 us
  starting transfers between devices  26.4 us (40%)
  Pallas kernels  22.8 us (34%)
  waiting for transfers between devices  16.4 us (25%)
  between operations  0.79 us (1%)
    pallas_call x12, Pallas kernels, call(): pl.pallas_call(functools.partial(kernel, **settings), in_specs=in_specs,...  22.8 us
    ppermute x20, starting transfers between devices, flip(): return lax.ppermute(a, 'dp', [(i, i ^ mask) for i in range(n_dp)])  19.4 us
    ppermute x20, waiting for transfers between devices, flip(): return lax.ppermute(a, 'dp', [(i, i ^ mask) for i in range(n_dp)])  8.57 us
    ppermute x6, waiting for transfers between devices, turn(): lax.ppermute(a, 'tensor', [(i, (i + shift) % n_tensor) for i in range(n_t...  7.78 us
    ppermute x6, starting transfers between devices, turn(): lax.ppermute(a, 'tensor', [(i, (i + shift) % n_tensor) for i in range(n_t...  7.06 us
  transfers between devices with their start and end apart: 26, of which 11 were waited for; matrix products, arithmetic and copies ran while one was open for 0% of the time, Pallas kernels for 30%

profile of v5, /device:TPU:0, one launch (start us, length us, event | category | flops | bytes accessed | tf_op | source)
XLA Modules:
  0.0 66.5 jit_solution(7047315156422023906)
XLA Ops:
  0.7 1.3 %shard_map.105 = (bf16[512,512]{1,0:T(8,128)(2,1)S(1)}, bf16[512,512]{1,0:T(8,128)(2,1)S(1)}) custom-call(bf16[8192,512]{1,0:T(8,128)(2,1)} %w.5), custom_call_target="tpu_custom_call" | custom-call | tf_op jit(solution)/shard_map/pallas_call | solution.py:45
  1.9 3.0 %collective-permute-start.8 = (bf16[512,512]{1,0:T(8,128)(2,1)S(1)}, bf16[512,512]{1,0:T(8,128)(2,1)S(1)}, u32[]{:S(2)}, u32[]{:S(2)}) collective-permute-start(bf16[512,512]{1,0:T(8,128)(2,1)S(1)} %get-tuple-element.51), channel_id=1, source_target_pairs={{0,16},{16,0},{1,17},{17,1},{2,18},{18,2},{3,19},{19,3},{4,20},{20... | collective-permute-start | bytes 1572872 | tf_op jit(solution)/shard_map/ppermute | solution.py:295
  5.0 0.1 shard_map.102.refs_0_
  5.1 2.7 %collective-permute-start.2 = (bf16[1,16,4608]{2,1,0:T(8,128)(2,1)S(1)}, bf16[1,16,4608]{2,1,0:T(8,128)(2,1)S(1)}, u32[]{:S(2)}, u32[]{:S(2)}) collective-permute-start(bf16[1,16,4608]{2,1,0:T(8,128)(2,1)S(1)} %shard_map.102.refs_0_), channel_id=1, source_target_pairs={{0,8},{1,9},{2,10},{3,11},{4,12},{5,13},{6,14},{7,15},{8,0},{9,1},... | collective-permute-start | bytes 442376 | tf_op jit(solution)/shard_map/ppermute | solution.py:292
  7.7 1.6 %collective-permute-start.1 = (bf16[1,16,4608]{2,1,0:T(8,128)(2,1)S(1)}, bf16[1,16,4608]{2,1,0:T(8,128)(2,1)S(1)}, u32[]{:S(2)}, u32[]{:S(2)}) collective-permute-start(bf16[1,16,4608]{2,1,0:T(8,128)(2,1)S(1)} %shard_map.102.refs_0_), channel_id=1, source_target_pairs={{0,4},{1,5},{2,6},{3,7},{4,0},{5,1},{6,2},{7,3},{8,12},{9,13},{10,... | collective-permute-start | bytes 442376 | tf_op jit(solution)/shard_map/ppermute | solution.py:292
  9.3 0.5 collective-permute-start.15
  9.8 1.5 %collective-permute-start = (s32[2]{0:T(128)S(1)}, s32[2]{0:T(128)S(1)}, u32[]{:S(2)}, u32[]{:S(2)}) collective-permute-start(s32[2]{0:T(128)S(1)} %copy-done.5), channel_id=1, source_target_pairs={{0,2},{1,3},{2,0},{3,1},{4,6},{5,7},{6,4},{7,5},{8,10},{9,11},{10,... | collective-permute-start | bytes 32 | tf_op jit(solution)/shard_map/ppermute | solution.py:292
  11.4 3.2 %collective-permute-done.2.refs_2_ = bf16[1,16,4608]{2,1,0:T(8,128)(2,1)S(1)} collective-permute-done((bf16[1,16,4608]{2,1,0:T(8,128)(2,1)S(1)}, bf16[1,16,4608]{2,1,0:T(8,128)(2,1)S(1)}, u32[]{:S(2)}, u32[]{:S(2)}) %collective-permute-start.2) | collective-permute-done | bytes 147488 | tf_op jit(solution)/shard_map/ppermute | solution.py:292
  14.6 0.6 collective-permute-start.3
  15.2 2.5 %collective-permute-done.8.refs_0_.refs_1_ = bf16[512,512]{1,0:T(8,128)(2,1)S(1)} collective-permute-done((bf16[512,512]{1,0:T(8,128)(2,1)S(1)}, bf16[512,512]{1,0:T(8,128)(2,1)S(1)}, u32[]{:S(2)}, u32[]{:S(2)}) %collective-permute-start.8) | collective-permute-done | bytes 524320 | tf_op jit(solution)/shard_map/ppermute | solution.py:295
  17.7 2.1 %collective-permute-start.9 = (bf16[512,512]{1,0:T(8,128)(2,1)S(1)}, bf16[512,512]{1,0:T(8,128)(2,1)S(1)}, u32[]{:S(2)}, u32[]{:S(2)}) collective-permute-start(bf16[512,512]{1,0:T(8,128)(2,1)S(1)} %collective-permute-done.8.refs_0_.refs_1_), channel_id=1, source_target_pairs={{0,4},{1,5},{2,6},{3,7},{4,0},{5,1},{6,2},{7,3},{8,12},{9,13},{10,... | collective-permute-start | bytes 1572872 | tf_op jit(solution)/shard_map/ppermute | solution.py:292
  19.9 1.0 %collective-permute-done.3.refs_3_ = bf16[1,16,4608]{2,1,0:T(8,128)(2,1)S(1)} collective-permute-done((bf16[1,16,4608]{2,1,0:T(8,128)(2,1)S(1)}, bf16[1,16,4608]{2,1,0:T(8,128)(2,1)S(1)}, u32[]{:S(2)}, u32[]{:S(2)}) %collective-permute-start.3) | collective-permute-done | bytes 147488 | tf_op jit(solution)/shard_map/ppermute | solution.py:292
  20.8 0.5 collective-permute-start.7
  21.3 0.1 pad_add_fusion.here.refs_2_
  21.4 0.8 %collective-permute-done.6.refs_6_ = bf16[1,16,4608]{2,1,0:T(8,128)(2,1)S(1)} collective-permute-done((bf16[1,16,4608]{2,1,0:T(8,128)(2,1)S(1)}, bf16[1,16,4608]{2,1,0:T(8,128)(2,1)S(1)}, u32[]{:S(2)}, u32[]{:S(2)}) %collective-permute-start.6) | collective-permute-done | bytes 147488 | tf_op jit(solution)/shard_map/ppermute | solution.py:292
  22.2 0.2 collective-permute-done.7.refs_7_
  22.4 0.7 %shard_map.103 = (bf16[2,16,4608]{2,1,0:T(8,128)(2,1)S(1)}, bf16[2,16,4608]{2,1,0:T(8,128)(2,1)S(1)}) custom-call(s32[2]{0:T(128)S(1)} %pad_add_fusion.here.refs_2_, s32[2]{0:T(128)S(1)} %copy-done.5, s32[2]{0:T(128)S(1)} %collective-permute-done.partner, bf16[1,16,4608]{2,1,0:T(8,128)(2,1)S(1)} %shard_map.102.refs_0_, ...), custom_call_target="tpu_custom_call" | custom-call | tf_op jit(solution)/shard_map/pallas_call | solution.py:45
  23.2 0.0 copy-start.2
  23.2 1.7 %collective-permute-start.10 = (bf16[2,16,4608]{2,1,0:T(8,128)(2,1)S(1)}, bf16[2,16,4608]{2,1,0:T(8,128)(2,1)S(1)}, u32[]{:S(2)}, u32[]{:S(2)}) collective-permute-start(bf16[2,16,4608]{2,1,0:T(8,128)(2,1)S(1)} %get-tuple-element.49), channel_id=1, source_target_pairs={{0,2},{1,3},{2,0},{3,1},{4,6},{5,7},{6,4},{7,5},{8,10},{9,11},{10,... | collective-permute-start | bytes 884744 | tf_op jit(solution)/shard_map/ppermute | solution.py:292
  24.8 4.4 %shard_map.104.own = f32[256,512]{1,0:T(8,128)S(1)} custom-call(s32[2]{0:T(128)S(1)} %pad_add_fusion.here.refs_2_, bf16[256,4096]{1,0:T(8,128)(2,1)} %x.7, bf16[8192,512]{1,0:T(8,128)(2,1)} %w.5), custom_call_target="tpu_custom_call" | custom-call | tf_op jit(solution)/shard_map/pallas_call | solution.py:45
  29.3 0.7 %collective-permute-start.16 = (bf16[512,512]{1,0:T(8,128)(2,1)S(1)}, bf16[512,512]{1,0:T(8,128)(2,1)S(1)}, u32[]{:S(2)}, u32[]{:S(2)}) collective-permute-start(bf16[512,512]{1,0:T(8,128)(2,1)S(1)} %collective-permute-done.15.refs_4_.refs_5_), channel_id=1, source_target_pairs={{0,4},{1,5},{2,6},{3,7},{4,0},{5,1},{6,2},{7,3},{8,12},{9,13},{10,... | collective-permute-start | bytes 1572872 | tf_op jit(solution)/shard_map/ppermute | solution.py:292
  30.0 2.4 %collective-permute-done.10.theirs = bf16[2,16,4608]{2,1,0:T(8,128)(2,1)S(1)} collective-permute-done((bf16[2,16,4608]{2,1,0:T(8,128)(2,1)S(1)}, bf16[2,16,4608]{2,1,0:T(8,128)(2,1)S(1)}, u32[]{:S(2)}, u32[]{:S(2)}) %collective-permute-start.10) | collective-permute-done | bytes 294944 | tf_op jit(solution)/shard_map/ppermute | solution.py:292
  32.5 1.5 %shard_map.106 = (bf16[2,16,4608]{2,1,0:T(8,128)(2,1)S(1)}, f32[4,16,128]{2,1,0:T(8,128)S(1)}) custom-call(s32[2]{0:T(128)S(1)} %pad_add_fusion.here.refs_2_, s32[2]{0:T(128)S(1)} %copy-done.5, bf16[256,4096]{1,0:T(8,128)(2,1)S(1)} %copy-done, bf16[256,512]{1,0:T(8,128)(2,1)S(1)} %copy-done.2, bf16[2,16,4608]{2,1,0:T(8,128)(2,1)S(1)} %get-tuple-element.55.mine, ...), custom_call_target="tpu_custom_call" | custom-call | tf_op jit(solution)/shard_map/pallas_call | solution.py:45
  33.9 0.8 %collective-permute-start.11 = (f32[4,16,128]{2,1,0:T(8,128)S(1)}, f32[4,16,128]{2,1,0:T(8,128)S(1)}, u32[]{:S(2)}, u32[]{:S(2)}) collective-permute-start(f32[4,16,128]{2,1,0:T(8,128)S(1)} %get-tuple-element.56.refs_0_), channel_id=1, source_target_pairs={{0,16},{16,0},{1,17},{17,1},{2,18},{18,2},{3,19},{19,3},{4,20},{20... | collective-permute-start | bytes 98312 | tf_op jit(solution)/shard_map/ppermute | solution.py:295
  34.7 3.2 %collective-permute-done.11.refs_1_ = f32[4,16,128]{2,1,0:T(8,128)S(1)} collective-permute-done((f32[4,16,128]{2,1,0:T(8,128)S(1)}, f32[4,16,128]{2,1,0:T(8,128)S(1)}, u32[]{:S(2)}, u32[]{:S(2)}) %collective-permute-start.11) | collective-permute-done | bytes 32800 | tf_op jit(solution)/shard_map/ppermute | solution.py:295
  37.9 0.4 shard_map.107
  38.3 1.7 %collective-permute-start.13 = (bf16[2,16,4736]{2,1,0:T(8,128)(2,1)S(1)}, bf16[2,16,4736]{2,1,0:T(8,128)(2,1)S(1)}, u32[]{:S(2)}, u32[]{:S(2)}) collective-permute-start(bf16[2,16,4736]{2,1,0:T(8,128)(2,1)S(1)} %get-tuple-element.59.mine), channel_id=1, source_target_pairs={{0,2},{1,3},{2,0},{3,1},{4,6},{5,7},{6,4},{7,5},{8,10},{9,11},{10,... | collective-permute-start | bytes 909320 | tf_op jit(solution)/shard_map/ppermute | solution.py:292
  39.9 0.7 collective-permute-start.12
  40.6 5.7 %shard_map.108.own = bf16[256,4096]{1,0:T(8,128)(2,1)} custom-call(s32[2]{0:T(128)S(1)} %pad_add_fusion.here.refs_2_, bf16[256,512]{1,0:T(8,128)(2,1)S(1)} %copy-done.2, bf16[8192,512]{1,0:T(8,128)(2,1)} %w.5), custom_call_target="tpu_custom_call" | custom-call | tf_op jit(solution)/shard_map/pallas_call | solution.py:45
  46.3 0.3 collective-permute-done.12.refs_0_
  46.5 0.9 %shard_map.109 = (f32[4,16,4736]{2,1,0:T(8,128)S(1)}, bf16[4,16,4736]{2,1,0:T(8,128)(2,1)S(1)}) custom-call(s32[2]{0:T(128)S(1)} %pad_add_fusion.here.refs_2_, s32[2]{0:T(128)S(1)} %copy-done.5, s32[2]{0:T(128)S(1)} %collective-permute-done.partner, bf16[2,16,4736]{2,1,0:T(8,128)(2,1)S(1)} %get-tuple-element.59.mine, ...), custom_call_target="tpu_custom_call" | custom-call | tf_op jit(solution)/shard_map/pallas_call | solution.py:45
  47.5 0.1 collective-permute-start.14
  47.5 0.5 collective-permute-start.17
  48.0 0.1 collective-permute-start.18
  48.1 0.4 collective-permute-start.19
  48.5 0.1 collective-permute-start.20
  48.6 0.9 %collective-permute-done.14.received = bf16[4,16,4736]{2,1,0:T(8,128)(2,1)S(1)} collective-permute-done((bf16[4,16,4736]{2,1,0:T(8,128)(2,1)S(1)}, bf16[4,16,4736]{2,1,0:T(8,128)(2,1)S(1)}, u32[]{:S(2)}, u32[]{:S(2)}) %collective-permute-start.14) | collective-permute-done | bytes 606240 | tf_op jit(solution)/shard_map/ppermute | solution.py:292
  49.6 0.1 shard_map.110
  49.7 2.4 %collective-permute-start.23 = (bf16[1,16,4736]{2,1,0:T(8,128)(2,1)S(1)}, bf16[1,16,4736]{2,1,0:T(8,128)(2,1)S(1)}, u32[]{:S(2)}, u32[]{:S(2)}) collective-permute-start(bf16[1,16,4736]{2,1,0:T(8,128)(2,1)S(1)} %get-tuple-element.76), channel_id=1, source_target_pairs={{0,8},{1,9},{2,10},{3,11},{4,12},{5,13},{6,14},{7,15},{8,0},{9,1},... | collective-permute-start | bytes 454664 | tf_op jit(solution)/shard_map/ppermute | solution.py:292
  52.1 2.0 %collective-permute-start.24 = (bf16[1,16,4736]{2,1,0:T(8,128)(2,1)S(1)}, bf16[1,16,4736]{2,1,0:T(8,128)(2,1)S(1)}, u32[]{:S(2)}, u32[]{:S(2)}) collective-permute-start(bf16[1,16,4736]{2,1,0:T(8,128)(2,1)S(1)} %get-tuple-element.77), channel_id=1, source_target_pairs={{0,4},{1,5},{2,6},{3,7},{4,0},{5,1},{6,2},{7,3},{8,12},{9,13},{10,... | collective-permute-start | bytes 454664 | tf_op jit(solution)/shard_map/ppermute | solution.py:292
  54.2 0.7 %collective-permute-start.25 = (bf16[1,16,4736]{2,1,0:T(8,128)(2,1)S(1)}, bf16[1,16,4736]{2,1,0:T(8,128)(2,1)S(1)}, u32[]{:S(2)}, u32[]{:S(2)}) collective-permute-start(bf16[1,16,4736]{2,1,0:T(8,128)(2,1)S(1)} %get-tuple-element.78), channel_id=1, source_target_pairs={{0,12},{1,13},{2,14},{3,15},{4,8},{5,9},{6,10},{7,11},{8,4},{9,5},... | collective-permute-start | bytes 454664 | tf_op jit(solution)/shard_map/ppermute | solution.py:292
  54.9 1.8 %shard_map.111 = (bf16[256,256]{1,0:T(8,128)(2,1)S(1)}, bf16[256,256]{1,0:T(8,128)(2,1)S(1)}) custom-call(s32[2]{0:T(128)S(1)} %pad_add_fusion.here.refs_2_, bf16[256,4096]{1,0:T(8,128)(2,1)S(1)} %copy-done, bf16[512,512]{1,0:T(8,128)(2,1)S(1)} %collective-permute-done.8.refs_0_.refs_1_, bf16[512,512]{1,0:T(8,128)(2,1)S(1)} %collective-permute-done.9.refs_1_.refs_2_, ...), custom_call_target="tpu_custom_call" | custom-call | tf_op jit(solution)/shard_map/pallas_call | solution.py:45
  56.7 1.2 %collective-permute-start.21 = (bf16[256,256]{1,0:T(8,128)(2,1)S(1)}, bf16[256,256]{1,0:T(8,128)(2,1)S(1)}, u32[]{:S(2)}, u32[]{:S(2)}) collective-permute-start(bf16[256,256]{1,0:T(8,128)(2,1)S(1)} %get-tuple-element.74), channel_id=1, source_target_pairs={{0,16},{16,0},{1,17},{17,1},{2,18},{18,2},{3,19},{19,3},{4,20},{20... | collective-permute-start | bytes 393224 | tf_op jit(solution)/shard_map/ppermute | solution.py:295
  57.9 0.9 %collective-permute-start.22 = (bf16[256,256]{1,0:T(8,128)(2,1)S(1)}, bf16[256,256]{1,0:T(8,128)(2,1)S(1)}, u32[]{:S(2)}, u32[]{:S(2)}) collective-permute-start(bf16[256,256]{1,0:T(8,128)(2,1)S(1)} %get-tuple-element.75), channel_id=1, source_target_pairs={{0,16},{16,0},{1,17},{17,1},{2,18},{18,2},{3,19},{19,3},{4,20},{20... | collective-permute-start | bytes 393224 | tf_op jit(solution)/shard_map/ppermute | solution.py:295
  58.8 4.2 %shard_map.113 = bf16[256,4096]{1,0:T(8,128)(2,1)} custom-call(s32[2]{0:T(128)S(1)} %pad_add_fusion.here.refs_2_, bf16[256,4096]{1,0:T(8,128)(2,1)S(1)} %copy-done.1, bf16[2,16,128]{2,1,0:T(8,128)(2,1)S(1)} %get-tuple-element.81.grad_low, bf16[2,16,4608]{2,1,0:T(8,128)(2,1)S(1)} %get-tuple-element.58.blocks, ...), custom_call_target="tpu_custom_call" | custom-call | tf_op jit(solution)/shard_map/pallas_call | solution.py:45
  63.0 0.1 collective-permute-done.21.refs_0_
  63.1 1.7 %collective-permute-done.22.refs_1_ = bf16[256,256]{1,0:T(8,128)(2,1)S(1)} collective-permute-done((bf16[256,256]{1,0:T(8,128)(2,1)S(1)}, bf16[256,256]{1,0:T(8,128)(2,1)S(1)}, u32[]{:S(2)}, u32[]{:S(2)}) %collective-permute-start.22) | collective-permute-done | bytes 131104 | tf_op jit(solution)/shard_map/ppermute | solution.py:295
  64.8 1.6 %shard_map.112 = (bf16[256,512]{1,0:T(8,128)(2,1)}, f32[1,16,4096]{2,1,0:T(8,128)}, f32[1,16,512]{2,1,0:T(8,128)}) custom-call(f32[256,512]{1,0:T(8,128)S(1)} %shard_map.104.own, bf16[2,16,128]{2,1,0:T(8,128)(2,1)S(1)} %get-tuple-element.57.low, bf16[2,16,4608]{2,1,0:T(8,128)(2,1)S(1)} %get-tuple-element.58.blocks, ...), custom_call_target="tpu_custom_call" | custom-call | tf_op jit(solution)/shard_map/pallas_call | solution.py:45
  (31 shorter events, 0.1 us)
Async XLA Ops:
  0.6 4.3 %copy-start.3 = (bf16[1,4096,16]{1,2,0:T(8,128)(2,1)S(1)}, bf16[1,4096,16]{1,2,0:T(8,128)(2,1)}, u32[]{:S(2)}) copy-start(bf16[1,4096,16]{1,2,0:T(8,128)(2,1)} %param.9) | copy-start | bytes 393220
  0.6 4.3 %copy-start.4 = (bf16[1,16,512]{2,1,0:T(8,128)(2,1)S(1)}, bf16[1,16,512]{2,1,0:T(8,128)(2,1)}, u32[]{:S(2)}) copy-start(bf16[1,16,512]{2,1,0:T(8,128)(2,1)} %up.1) | copy-start | bytes 49156
  0.7 9.2 %copy-start.5 = (s32[2]{0:T(128)S(1)}, s32[2]{0:T(128)}, u32[]{:S(2)}) copy-start(s32[2]{0:T(128)} %tenant.4) | copy-start | bytes 28
  1.9 15.8 %collective-permute-start.8 = (bf16[512,512]{1,0:T(8,128)(2,1)S(1)}, bf16[512,512]{1,0:T(8,128)(2,1)S(1)}, u32[]{:S(2)}, u32[]{:S(2)}) collective-permute-start(bf16[512,512]{1,0:T(8,128)(2,1)S(1)} %get-tuple-element.51), channel_id=1, source_target_pairs={{0,16},{16,0},{1,17},{17,1},{2,18},{18,2},{3,19},{19,3},{4,20},{20... | collective-permute-start | bytes 1572872 | tf_op jit(solution)/shard_map/ppermute | solution.py:295
  5.1 9.5 %collective-permute-start.2 = (bf16[1,16,4608]{2,1,0:T(8,128)(2,1)S(1)}, bf16[1,16,4608]{2,1,0:T(8,128)(2,1)S(1)}, u32[]{:S(2)}, u32[]{:S(2)}) collective-permute-start(bf16[1,16,4608]{2,1,0:T(8,128)(2,1)S(1)} %shard_map.102.refs_0_), channel_id=1, source_target_pairs={{0,8},{1,9},{2,10},{3,11},{4,12},{5,13},{6,14},{7,15},{8,0},{9,1},... | collective-permute-start | bytes 442376 | tf_op jit(solution)/shard_map/ppermute | solution.py:292
  7.7 7.5 %collective-permute-start.1 = (bf16[1,16,4608]{2,1,0:T(8,128)(2,1)S(1)}, bf16[1,16,4608]{2,1,0:T(8,128)(2,1)S(1)}, u32[]{:S(2)}, u32[]{:S(2)}) collective-permute-start(bf16[1,16,4608]{2,1,0:T(8,128)(2,1)S(1)} %shard_map.102.refs_0_), channel_id=1, source_target_pairs={{0,4},{1,5},{2,6},{3,7},{4,0},{5,1},{6,2},{7,3},{8,12},{9,13},{10,... | collective-permute-start | bytes 442376 | tf_op jit(solution)/shard_map/ppermute | solution.py:292
  9.3 20.0 %collective-permute-start.15 = (bf16[512,512]{1,0:T(8,128)(2,1)S(1)}, bf16[512,512]{1,0:T(8,128)(2,1)S(1)}, u32[]{:S(2)}, u32[]{:S(2)}) collective-permute-start(bf16[512,512]{1,0:T(8,128)(2,1)S(1)} %get-tuple-element.65), channel_id=1, source_target_pairs={{0,16},{16,0},{1,17},{17,1},{2,18},{18,2},{3,19},{19,3},{4,20},{20... | collective-permute-start | bytes 1572872 | tf_op jit(solution)/shard_map/ppermute | solution.py:295
  9.8 5.3 %collective-permute-start = (s32[2]{0:T(128)S(1)}, s32[2]{0:T(128)S(1)}, u32[]{:S(2)}, u32[]{:S(2)}) collective-permute-start(s32[2]{0:T(128)S(1)} %copy-done.5), channel_id=1, source_target_pairs={{0,2},{1,3},{2,0},{3,1},{4,6},{5,7},{6,4},{7,5},{8,10},{9,11},{10,... | collective-permute-start | bytes 32 | tf_op jit(solution)/shard_map/ppermute | solution.py:292
  14.6 6.2 %collective-permute-start.3 = (bf16[1,16,4608]{2,1,0:T(8,128)(2,1)S(1)}, bf16[1,16,4608]{2,1,0:T(8,128)(2,1)S(1)}, u32[]{:S(2)}, u32[]{:S(2)}) collective-permute-start(bf16[1,16,4608]{2,1,0:T(8,128)(2,1)S(1)} %collective-permute-done.2.refs_2_), channel_id=1, source_target_pairs={{0,4},{1,5},{2,6},{3,7},{4,0},{5,1},{6,2},{7,3},{8,12},{9,13},{10,... | collective-permute-start | bytes 442376 | tf_op jit(solution)/shard_map/ppermute | solution.py:292
  15.2 5.6 %collective-permute-start.4 = (bf16[1,16,4608]{2,1,0:T(8,128)(2,1)S(1)}, bf16[1,16,4608]{2,1,0:T(8,128)(2,1)S(1)}, u32[]{:S(2)}, u32[]{:S(2)}) collective-permute-start(bf16[1,16,4608]{2,1,0:T(8,128)(2,1)S(1)} %shard_map.102.refs_0_), channel_id=1, source_target_pairs={{0,1},{1,0},{2,3},{3,2},{4,5},{5,4},{6,7},{7,6},{8,9},{9,8},{10,11... | collective-permute-start | bytes 442376 | tf_op jit(solution)/shard_map/ppermute | solution.py:292
  17.7 17.0 %collective-permute-start.9 = (bf16[512,512]{1,0:T(8,128)(2,1)S(1)}, bf16[512,512]{1,0:T(8,128)(2,1)S(1)}, u32[]{:S(2)}, u32[]{:S(2)}) collective-permute-start(bf16[512,512]{1,0:T(8,128)(2,1)S(1)} %collective-permute-done.8.refs_0_.refs_1_), channel_id=1, source_target_pairs={{0,4},{1,5},{2,6},{3,7},{4,0},{5,1},{6,2},{7,3},{8,12},{9,13},{10,... | collective-permute-start | bytes 1572872 | tf_op jit(solution)/shard_map/ppermute | solution.py:292
  19.9 1.6 %collective-permute-start.5 = (bf16[1,16,4608]{2,1,0:T(8,128)(2,1)S(1)}, bf16[1,16,4608]{2,1,0:T(8,128)(2,1)S(1)}, u32[]{:S(2)}, u32[]{:S(2)}) collective-permute-start(bf16[1,16,4608]{2,1,0:T(8,128)(2,1)S(1)} %collective-permute-done.1.refs_1_), channel_id=1, source_target_pairs={{0,1},{1,0},{2,3},{3,2},{4,5},{5,4},{6,7},{7,6},{8,9},{9,8},{10,11... | collective-permute-start | bytes 442376 | tf_op jit(solution)/shard_map/ppermute | solution.py:292
  20.8 1.4 %collective-permute-start.6 = (bf16[1,16,4608]{2,1,0:T(8,128)(2,1)S(1)}, bf16[1,16,4608]{2,1,0:T(8,128)(2,1)S(1)}, u32[]{:S(2)}, u32[]{:S(2)}) collective-permute-start(bf16[1,16,4608]{2,1,0:T(8,128)(2,1)S(1)} %collective-permute-done.2.refs_2_), channel_id=1, source_target_pairs={{0,1},{1,0},{2,3},{3,2},{4,5},{5,4},{6,7},{7,6},{8,9},{9,8},{10,11... | collective-permute-start | bytes 442376 | tf_op jit(solution)/shard_map/ppermute | solution.py:292
  20.8 1.6 %collective-permute-start.7 = (bf16[1,16,4608]{2,1,0:T(8,128)(2,1)S(1)}, bf16[1,16,4608]{2,1,0:T(8,128)(2,1)S(1)}, u32[]{:S(2)}, u32[]{:S(2)}) collective-permute-start(bf16[1,16,4608]{2,1,0:T(8,128)(2,1)S(1)} %collective-permute-done.3.refs_3_), channel_id=1, source_target_pairs={{0,1},{1,0},{2,3},{3,2},{4,5},{5,4},{6,7},{7,6},{8,9},{9,8},{10,11... | collective-permute-start | bytes 442376 | tf_op jit(solution)/shard_map/ppermute | solution.py:292
  23.1 9.3 %copy-start = (bf16[256,4096]{1,0:T(8,128)(2,1)S(1)}, bf16[256,4096]{1,0:T(8,128)(2,1)}, u32[]{:S(2)}) copy-start(bf16[256,4096]{1,0:T(8,128)(2,1)} %x.7) | copy-start | bytes 6291460
  23.2 9.3 %copy-start.2 = (bf16[256,512]{1,0:T(8,128)(2,1)S(1)}, bf16[256,512]{1,0:T(8,128)(2,1)}, u32[]{:S(2)}) copy-start(bf16[256,512]{1,0:T(8,128)(2,1)} %cot.4) | copy-start | bytes 786436
  23.2 9.3 %collective-permute-start.10 = (bf16[2,16,4608]{2,1,0:T(8,128)(2,1)S(1)}, bf16[2,16,4608]{2,1,0:T(8,128)(2,1)S(1)}, u32[]{:S(2)}, u32[]{:S(2)}) collective-permute-start(bf16[2,16,4608]{2,1,0:T(8,128)(2,1)S(1)} %get-tuple-element.49), channel_id=1, source_target_pairs={{0,2},{1,3},{2,0},{3,1},{4,6},{5,7},{6,4},{7,5},{8,10},{9,11},{10,... | collective-permute-start | bytes 884744 | tf_op jit(solution)/shard_map/ppermute | solution.py:292
  29.3 19.3 %collective-permute-start.16 = (bf16[512,512]{1,0:T(8,128)(2,1)S(1)}, bf16[512,512]{1,0:T(8,128)(2,1)S(1)}, u32[]{:S(2)}, u32[]{:S(2)}) collective-permute-start(bf16[512,512]{1,0:T(8,128)(2,1)S(1)} %collective-permute-done.15.refs_4_.refs_5_), channel_id=1, source_target_pairs={{0,4},{1,5},{2,6},{3,7},{4,0},{5,1},{6,2},{7,3},{8,12},{9,13},{10,... | collective-permute-start | bytes 1572872 | tf_op jit(solution)/shard_map/ppermute | solution.py:292
  33.9 4.0 %collective-permute-start.11 = (f32[4,16,128]{2,1,0:T(8,128)S(1)}, f32[4,16,128]{2,1,0:T(8,128)S(1)}, u32[]{:S(2)}, u32[]{:S(2)}) collective-permute-start(f32[4,16,128]{2,1,0:T(8,128)S(1)} %get-tuple-element.56.refs_0_), channel_id=1, source_target_pairs={{0,16},{16,0},{1,17},{17,1},{2,18},{18,2},{3,19},{19,3},{4,20},{20... | collective-permute-start | bytes 98312 | tf_op jit(solution)/shard_map/ppermute | solution.py:295
  38.3 8.2 %collective-permute-start.13 = (bf16[2,16,4736]{2,1,0:T(8,128)(2,1)S(1)}, bf16[2,16,4736]{2,1,0:T(8,128)(2,1)S(1)}, u32[]{:S(2)}, u32[]{:S(2)}) collective-permute-start(bf16[2,16,4736]{2,1,0:T(8,128)(2,1)S(1)} %get-tuple-element.59.mine), channel_id=1, source_target_pairs={{0,2},{1,3},{2,0},{3,1},{4,6},{5,7},{6,4},{7,5},{8,10},{9,11},{10,... | collective-permute-start | bytes 909320 | tf_op jit(solution)/shard_map/ppermute | solution.py:292
  39.9 6.6 %collective-permute-start.12 = (bf16[256,512]{1,0:T(8,128)(2,1)S(1)}, bf16[256,512]{1,0:T(8,128)(2,1)S(1)}, u32[]{:S(2)}, u32[]{:S(2)}) collective-permute-start(bf16[256,512]{1,0:T(8,128)(2,1)S(1)} %copy-done.2), channel_id=1, source_target_pairs={{0,16},{16,0},{1,17},{17,1},{2,18},{18,2},{3,19},{19,3},{4,20},{20... | collective-permute-start | bytes 786440 | tf_op jit(solution)/shard_map/ppermute | solution.py:295
  47.5 2.1 %collective-permute-start.14 = (bf16[4,16,4736]{2,1,0:T(8,128)(2,1)S(1)}, bf16[4,16,4736]{2,1,0:T(8,128)(2,1)S(1)}, u32[]{:S(2)}, u32[]{:S(2)}) collective-permute-start(bf16[4,16,4736]{2,1,0:T(8,128)(2,1)S(1)} %get-tuple-element.64), channel_id=1, source_target_pairs={{0,1},{1,0},{2,3},{3,2},{4,5},{5,4},{6,7},{7,6},{8,9},{9,8},{10,11... | collective-permute-start | bytes 1818632 | tf_op jit(solution)/shard_map/ppermute | solution.py:292
  47.5 4.6 %collective-permute-start.17 = (bf16[512,512]{1,0:T(8,128)(2,1)S(1)}, bf16[512,512]{1,0:T(8,128)(2,1)S(1)}, u32[]{:S(2)}, u32[]{:S(2)}) collective-permute-start(bf16[512,512]{1,0:T(8,128)(2,1)S(1)} %collective-permute-done.8.refs_0_.refs_1_), channel_id=1, source_target_pairs={{0,1},{1,0},{2,3},{3,2},{4,5},{5,4},{6,7},{7,6},{8,9},{9,8},{10,11... | collective-permute-start | bytes 1572872 | tf_op jit(solution)/shard_map/ppermute | solution.py:292
  48.0 6.1 %collective-permute-start.18 = (bf16[512,512]{1,0:T(8,128)(2,1)S(1)}, bf16[512,512]{1,0:T(8,128)(2,1)S(1)}, u32[]{:S(2)}, u32[]{:S(2)}) collective-permute-start(bf16[512,512]{1,0:T(8,128)(2,1)S(1)} %collective-permute-done.9.refs_1_.refs_2_), channel_id=1, source_target_pairs={{0,1},{1,0},{2,3},{3,2},{4,5},{5,4},{6,7},{7,6},{8,9},{9,8},{10,11... | collective-permute-start | bytes 1572872 | tf_op jit(solution)/shard_map/ppermute | solution.py:292
  48.1 6.8 %collective-permute-start.19 = (bf16[512,512]{1,0:T(8,128)(2,1)S(1)}, bf16[512,512]{1,0:T(8,128)(2,1)S(1)}, u32[]{:S(2)}, u32[]{:S(2)}) collective-permute-start(bf16[512,512]{1,0:T(8,128)(2,1)S(1)} %collective-permute-done.15.refs_4_.refs_5_), channel_id=1, source_target_pairs={{0,1},{1,0},{2,3},{3,2},{4,5},{5,4},{6,7},{7,6},{8,9},{9,8},{10,11... | collective-permute-start | bytes 1572872 | tf_op jit(solution)/shard_map/ppermute | solution.py:292
  48.5 6.3 %collective-permute-start.20 = (bf16[512,512]{1,0:T(8,128)(2,1)S(1)}, bf16[512,512]{1,0:T(8,128)(2,1)S(1)}, u32[]{:S(2)}, u32[]{:S(2)}) collective-permute-start(bf16[512,512]{1,0:T(8,128)(2,1)S(1)} %collective-permute-done.16.refs_5_.refs_6_), channel_id=1, source_target_pairs={{0,1},{1,0},{2,3},{3,2},{4,5},{5,4},{6,7},{7,6},{8,9},{9,8},{10,11... | collective-permute-start | bytes 1572872 | tf_op jit(solution)/shard_map/ppermute | solution.py:292
  49.7 15.1 %collective-permute-start.23 = (bf16[1,16,4736]{2,1,0:T(8,128)(2,1)S(1)}, bf16[1,16,4736]{2,1,0:T(8,128)(2,1)S(1)}, u32[]{:S(2)}, u32[]{:S(2)}) collective-permute-start(bf16[1,16,4736]{2,1,0:T(8,128)(2,1)S(1)} %get-tuple-element.76), channel_id=1, source_target_pairs={{0,8},{1,9},{2,10},{3,11},{4,12},{5,13},{6,14},{7,15},{8,0},{9,1},... | collective-permute-start | bytes 454664 | tf_op jit(solution)/shard_map/ppermute | solution.py:292
  52.1 12.7 %collective-permute-start.24 = (bf16[1,16,4736]{2,1,0:T(8,128)(2,1)S(1)}, bf16[1,16,4736]{2,1,0:T(8,128)(2,1)S(1)}, u32[]{:S(2)}, u32[]{:S(2)}) collective-permute-start(bf16[1,16,4736]{2,1,0:T(8,128)(2,1)S(1)} %get-tuple-element.77), channel_id=1, source_target_pairs={{0,4},{1,5},{2,6},{3,7},{4,0},{5,1},{6,2},{7,3},{8,12},{9,13},{10,... | collective-permute-start | bytes 454664 | tf_op jit(solution)/shard_map/ppermute | solution.py:292
  54.2 10.7 %collective-permute-start.25 = (bf16[1,16,4736]{2,1,0:T(8,128)(2,1)S(1)}, bf16[1,16,4736]{2,1,0:T(8,128)(2,1)S(1)}, u32[]{:S(2)}, u32[]{:S(2)}) collective-permute-start(bf16[1,16,4736]{2,1,0:T(8,128)(2,1)S(1)} %get-tuple-element.78), channel_id=1, source_target_pairs={{0,12},{1,13},{2,14},{3,15},{4,8},{5,9},{6,10},{7,11},{8,4},{9,5},... | collective-permute-start | bytes 454664 | tf_op jit(solution)/shard_map/ppermute | solution.py:292
  54.9 3.9 %copy-start.1 = (bf16[256,4096]{1,0:T(8,128)(2,1)S(1)}, bf16[256,4096]{1,0:T(8,128)(2,1)}, u32[]{:S(2)}) copy-start(bf16[256,4096]{1,0:T(8,128)(2,1)} %shard_map.108.own) | copy-start | bytes 6291460
  56.7 6.4 %collective-permute-start.21 = (bf16[256,256]{1,0:T(8,128)(2,1)S(1)}, bf16[256,256]{1,0:T(8,128)(2,1)S(1)}, u32[]{:S(2)}, u32[]{:S(2)}) collective-permute-start(bf16[256,256]{1,0:T(8,128)(2,1)S(1)} %get-tuple-element.74), channel_id=1, source_target_pairs={{0,16},{16,0},{1,17},{17,1},{2,18},{18,2},{3,19},{19,3},{4,20},{20... | collective-permute-start | bytes 393224 | tf_op jit(solution)/shard_map/ppermute | solution.py:295
  57.9 6.9 %collective-permute-start.22 = (bf16[256,256]{1,0:T(8,128)(2,1)S(1)}, bf16[256,256]{1,0:T(8,128)(2,1)S(1)}, u32[]{:S(2)}, u32[]{:S(2)}) collective-permute-start(bf16[256,256]{1,0:T(8,128)(2,1)S(1)} %get-tuple-element.75), channel_id=1, source_target_pairs={{0,16},{16,0},{1,17},{17,1},{2,18},{18,2},{3,19},{19,3},{4,20},{20... | collective-permute-start | bytes 393224 | tf_op jit(solution)/shard_map/ppermute | solution.py:295
  58.8 6.1 %copy-start.6 = (s32[16]{0:T(128)S(1)}, s32[16]{0:T(128)}, u32[]{:S(2)}) copy-start(s32[16]{0:T(128)} %refs_3_.1) | copy-start | bytes 196
